TPU v7x, 32 devices: a whole 2x2x4 slice. The times are simulated.
32 devices in a mesh: ctx: 16 (over z, y, x), fsdp: 2 (over core).
Axes of the slice: x: 2, y: 2, z: 4, core: 2. Of those that a mesh axis runs over, the one named last changes fastest.
Arguments:
- block_input: bfloat16 [2, 16, 2, 64, 1024], P('fsdp', 'ctx'), may hold values from -6 to 6
- w_qkv: bfloat16 [1024, 3072], P('fsdp'), may hold values from -0.1875 to 0.1875
- w_out: bfloat16 [1024, 1024], P('fsdp'), may hold values from -3 to 3
- w_fc: bfloat16 [1024, 4096], P('fsdp'), may hold values from -0.1875 to 0.1875
- w_proj: bfloat16 [4096, 1024], P('fsdp'), may hold values from -0.09375 to 0.09375
- ln1_gain: bfloat16 [1024], P('fsdp'), may hold values from 0.099609375 to 1.8984375
- ln1_bias: bfloat16 [1024], P('fsdp'), may hold values from -4 to 4
- ln2_gain: bfloat16 [1024], P('fsdp'), may hold values from 0.099609375 to 1.8984375
- ln2_bias: bfloat16 [1024], P('fsdp'), may hold values from -4 to 4
- bias_q: bfloat16 [1024], P('fsdp'), may hold values from -4 to 4
- bias_v: bfloat16 [1024], P('fsdp'), may hold values from -0.75 to 0.75
- bias_out: bfloat16 [1024], P('fsdp'), may hold values from -4 to 4
- bias_fc: bfloat16 [4096], P('fsdp'), may hold values from -4 to 4
- bias_proj: bfloat16 [1024], P('fsdp'), may hold values from -4 to 4
- cotangent: bfloat16 [2, 16, 2, 64, 1024], P('fsdp', 'ctx'), may hold values from -6 to 6
Outputs:
- block_output: bfloat16 [2, 16, 2, 64, 1024], P('fsdp', 'ctx')
- grad_input: float32 [2, 16, 2, 64, 1024], P('fsdp', 'ctx')
- grad_w_qkv: float32 [1024, 3072], P(('ctx', 'fsdp'))
- grad_w_out: float32 [1024, 1024], P(('ctx', 'fsdp'))
- grad_w_fc: float32 [1024, 4096], P(('ctx', 'fsdp'))
- grad_w_proj: float32 [4096, 1024], P(('ctx', 'fsdp'))
- grad_ln1_gain: float32 [1024], P(('ctx', 'fsdp'))
- grad_ln1_bias: float32 [1024], P(('ctx', 'fsdp'))
- grad_ln2_gain: float32 [1024], P(('ctx', 'fsdp'))
- grad_ln2_bias: float32 [1024], P(('ctx', 'fsdp'))
- grad_bias_q: float32 [1024], P(('ctx', 'fsdp'))
- grad_bias_v: float32 [1024], P(('ctx', 'fsdp'))
- grad_bias_out: float32 [1024], P(('ctx', 'fsdp'))
- grad_bias_fc: float32 [4096], P(('ctx', 'fsdp'))
- grad_bias_proj: float32 [1024], P(('ctx', 'fsdp'))
All inputs are finite; a program needn't handle non-finite values.
Results may differ from a plain program's by a relative error of at most 0.012.
The roundings to bfloat16 on the way count: a program that leaves them out, or rounds other values in their place, can miss the bound.
Values may be sent and summed in bfloat16 or wider, within the bound.
A program may use at most 384 MiB of HBM per device.

v0:
```python
from functools import partial

import jax
import jax.numpy as jnp
from jax import lax
from jax.sharding import PartitionSpec as P

HEADS = 16


def norm_parts(values):
    average = jnp.mean(values, -1, keepdims=True)
    centered = values - average
    variance = jnp.mean(centered * centered, -1, keepdims=True)
    inverse = lax.rsqrt(variance + 1e-05)
    return (centered * inverse, inverse)


def norm_grads(upstream, normalized, inverse, gain):
    scaled = upstream * gain
    inner_part = (
        scaled
        - jnp.mean(scaled, -1, keepdims=True)
        - normalized * jnp.mean(scaled * normalized, -1, keepdims=True)
    )
    return (inverse * inner_part, jnp.sum(upstream * normalized, 0), jnp.sum(upstream, 0))


def rows_product(left, right):
    return lax.dot_general(
        left, right, (((0,), (0,)), ((), ())), preferred_element_type=jnp.float32
    )


def right_transposed(left, weight):
    return lax.dot_general(
        left, weight, (((1,), (1,)), ((), ())), preferred_element_type=jnp.float32
    )


def split_heads(matrix):
    return matrix.reshape(matrix.shape[0], HEADS, -1)


def head_scores(queries, keys, allowed, scaling):
    scores = (
        jnp.einsum(
            "qhd,khd->hqk",
            split_heads(queries),
            split_heads(keys),
            preferred_element_type=jnp.float32,
        )
        * scaling
    )
    return jnp.where(allowed[None], scores, -1e30)


def on_device(
    block_input,
    w_qkv,
    w_out,
    w_fc,
    w_proj,
    ln1_gain,
    ln1_bias,
    ln2_gain,
    ln2_bias,
    bias_q,
    bias_v,
    bias_out,
    bias_fc,
    bias_proj,
    cotangent,
):
    seq_count = block_input.shape[0]
    blk_rows = block_input.shape[3]
    width = block_input.shape[4]
    seq_rows = 2 * blk_rows
    row_count = seq_count * seq_rows
    groups = lax.axis_size("ctx")
    member = lax.axis_index("ctx")
    head_size = width // HEADS
    scaling = head_size ** (-0.5)
    full_rows = groups * seq_rows
    gathered = (
        lax.all_gather(w_qkv, "fsdp", axis=0, tiled=True),
        lax.all_gather(w_out, "fsdp", axis=0, tiled=True),
        lax.all_gather(w_fc, "fsdp", axis=0, tiled=True),
        lax.all_gather(w_proj, "fsdp", axis=0, tiled=True),
        lax.all_gather(ln1_gain, "fsdp", axis=0, tiled=True),
        lax.all_gather(ln1_bias, "fsdp", axis=0, tiled=True),
        lax.all_gather(ln2_gain, "fsdp", axis=0, tiled=True),
        lax.all_gather(ln2_bias, "fsdp", axis=0, tiled=True),
        lax.all_gather(bias_q, "fsdp", axis=0, tiled=True),
        lax.all_gather(bias_v, "fsdp", axis=0, tiled=True),
        lax.all_gather(bias_out, "fsdp", axis=0, tiled=True),
        lax.all_gather(bias_fc, "fsdp", axis=0, tiled=True),
        lax.all_gather(bias_proj, "fsdp", axis=0, tiled=True),
    )
    weight_qkv, weight_out, weight_fc, weight_proj = (
        gathered[0],
        gathered[1],
        gathered[2],
        gathered[3],
    )
    vectors = [piece.astype(jnp.float32) for piece in gathered[4:]]
    (
        gain_one,
        shift_one,
        gain_two,
        shift_two,
        query_bias,
        value_bias,
        out_bias,
        fc_bias,
        proj_bias,
    ) = vectors
    local_index = jnp.arange(seq_rows)
    own_block = jnp.where(local_index // blk_rows == 0, member, 2 * groups - 1 - member)
    own_pos = own_block * blk_rows + local_index % blk_rows
    every_index = jnp.arange(full_rows)
    every_owner = every_index // seq_rows
    every_block = jnp.where(
        every_index // blk_rows % 2 == 0, every_owner, 2 * groups - 1 - every_owner
    )
    every_pos = every_block * blk_rows + every_index % blk_rows
    allowed = every_pos[None, :] <= own_pos[:, None]
    inputs = block_input.reshape(row_count, width).astype(jnp.float32)
    normal_one, inverse_one = norm_parts(inputs)
    normed_one = (normal_one * gain_one + shift_one).astype(jnp.bfloat16)
    bias_all = jnp.concatenate([query_bias, jnp.zeros_like(query_bias), value_bias])
    projected = (
        jnp.dot(normed_one, weight_qkv, preferred_element_type=jnp.float32) + bias_all
    ).astype(jnp.bfloat16)
    queries = projected[:, :width]
    keys = projected[:, width : 2 * width]
    values = projected[:, 2 * width :]
    key_all = lax.all_gather(keys, "ctx", axis=0, tiled=True)
    value_all = lax.all_gather(values, "ctx", axis=0, tiled=True)
    scores = head_scores(queries, key_all, allowed, scaling)
    row_top = jnp.max(scores, -1, keepdims=True)
    log_sum = row_top + jnp.log(jnp.sum(jnp.exp(scores - row_top), -1, keepdims=True))
    probs_low = jnp.exp(scores - log_sum).astype(jnp.bfloat16)
    mixed = jnp.einsum(
        "hqk,khd->qhd", probs_low, split_heads(value_all), preferred_element_type=jnp.float32
    )
    mixed_rows = mixed.reshape(seq_rows, width)
    attended = mixed_rows.astype(jnp.bfloat16)
    residual = inputs + jnp.dot(attended, weight_out, preferred_element_type=jnp.float32) + out_bias
    normal_two, inverse_two = norm_parts(residual)
    normed_two = (normal_two * gain_two + shift_two).astype(jnp.bfloat16)
    hidden = jnp.dot(normed_two, weight_fc, preferred_element_type=jnp.float32) + fc_bias
    activated, gelu_pullback = jax.vjp(partial(jax.nn.gelu, approximate=True), hidden)
    activated_low = activated.astype(jnp.bfloat16)
    result = (
        residual
        + jnp.dot(activated_low, weight_proj, preferred_element_type=jnp.float32)
        + proj_bias
    )
    block_output = result.astype(jnp.bfloat16).reshape(block_input.shape)
    weight_qkv, weight_out, weight_fc, weight_proj, gain_low_one, gain_low_two = (
        lax.all_gather(w_qkv, "fsdp", axis=0, tiled=True),
        lax.all_gather(w_out, "fsdp", axis=0, tiled=True),
        lax.all_gather(w_fc, "fsdp", axis=0, tiled=True),
        lax.all_gather(w_proj, "fsdp", axis=0, tiled=True),
        lax.all_gather(ln1_gain, "fsdp", axis=0, tiled=True),
        lax.all_gather(ln2_gain, "fsdp", axis=0, tiled=True),
    )
    gain_one = gain_low_one.astype(jnp.float32)
    gain_two = gain_low_two.astype(jnp.float32)
    out_grad_low = cotangent.reshape(row_count, width)
    upstream = out_grad_low.astype(jnp.float32)
    grad_proj = rows_product(activated_low, out_grad_low)
    grad_proj_bias = jnp.sum(upstream, 0)
    hidden_grad = gelu_pullback(right_transposed(out_grad_low, weight_proj))[0].astype(jnp.bfloat16)
    grad_fc = rows_product(normed_two, hidden_grad)
    grad_fc_bias = jnp.sum(hidden_grad.astype(jnp.float32), 0)
    residual_part, grad_gain_two, grad_shift_two = norm_grads(
        right_transposed(hidden_grad, weight_fc), normal_two, inverse_two, gain_two
    )
    residual_grad = upstream + residual_part
    branch_grad = residual_grad.astype(jnp.bfloat16)
    grad_out = rows_product(attended, branch_grad)
    grad_out_bias = jnp.sum(branch_grad.astype(jnp.float32), 0)
    attended_grad = right_transposed(branch_grad, weight_out).astype(jnp.bfloat16)
    key_all = lax.all_gather(keys, "ctx", axis=0, tiled=True)
    value_all = lax.all_gather(values, "ctx", axis=0, tiled=True)
    scores = head_scores(queries, key_all, allowed, scaling)
    probs = jnp.exp(scores - log_sum)
    prob_grad = jnp.einsum(
        "qhd,khd->hqk",
        split_heads(attended_grad),
        split_heads(value_all),
        preferred_element_type=jnp.float32,
    )
    inner_sum = jnp.sum(probs * prob_grad, -1, keepdims=True)
    score_grad = (probs * (prob_grad - inner_sum)).astype(jnp.bfloat16)
    query_part = (
        jnp.einsum(
            "hqk,khd->qhd", score_grad, split_heads(key_all), preferred_element_type=jnp.float32
        )
        * scaling
    )
    query_grads = query_part.reshape(seq_rows, width)
    probs_low = probs.astype(jnp.bfloat16)
    query_heads = split_heads(queries)
    grad_heads = split_heads(attended_grad)

    def key_terms(
        start,
        count,
        score_grad=score_grad,
        probs_low=probs_low,
        query_heads=query_heads,
        grad_heads=grad_heads,
    ):
        key_part = (
            jnp.einsum("hqk,qhd->khd", score_grad, query_heads, preferred_element_type=jnp.float32)
            * scaling
        )
        value_part = jnp.einsum(
            "hqk,qhd->khd", probs_low, grad_heads, preferred_element_type=jnp.float32
        )
        return jnp.concatenate(
            [key_part.reshape(count, width), value_part.reshape(count, width)], 1
        )

    own_terms = lax.psum_scatter(
        key_terms(jnp.int32(0), lax.axis_size("ctx") * seq_rows),
        "ctx",
        scatter_dimension=0,
        tiled=True,
    )
    key_grads = own_terms[:, :width]
    value_grads = own_terms[:, width:]
    qkv_grad = jnp.concatenate([query_grads, key_grads, value_grads], 1).astype(jnp.bfloat16)
    grad_qkv = rows_product(normed_one, qkv_grad)
    qkv_sums = jnp.sum(qkv_grad.astype(jnp.float32), 0)
    grad_query_bias = qkv_sums[:width]
    grad_value_bias = qkv_sums[2 * width :]
    input_part, grad_gain_one, grad_shift_one = norm_grads(
        right_transposed(qkv_grad, weight_qkv), normal_one, inverse_one, gain_one
    )
    input_grad = (residual_grad + input_part).reshape(block_input.shape)
    sharded = (
        lax.psum_scatter(grad_qkv, ("ctx", "fsdp"), scatter_dimension=0, tiled=True),
        lax.psum_scatter(grad_out, ("ctx", "fsdp"), scatter_dimension=0, tiled=True),
        lax.psum_scatter(grad_fc, ("ctx", "fsdp"), scatter_dimension=0, tiled=True),
        lax.psum_scatter(grad_proj, ("ctx", "fsdp"), scatter_dimension=0, tiled=True),
        lax.psum_scatter(grad_gain_one, ("ctx", "fsdp"), scatter_dimension=0, tiled=True),
        lax.psum_scatter(grad_shift_one, ("ctx", "fsdp"), scatter_dimension=0, tiled=True),
        lax.psum_scatter(grad_gain_two, ("ctx", "fsdp"), scatter_dimension=0, tiled=True),
        lax.psum_scatter(grad_shift_two, ("ctx", "fsdp"), scatter_dimension=0, tiled=True),
        lax.psum_scatter(grad_query_bias, ("ctx", "fsdp"), scatter_dimension=0, tiled=True),
        lax.psum_scatter(grad_value_bias, ("ctx", "fsdp"), scatter_dimension=0, tiled=True),
        lax.psum_scatter(grad_out_bias, ("ctx", "fsdp"), scatter_dimension=0, tiled=True),
        lax.psum_scatter(grad_fc_bias, ("ctx", "fsdp"), scatter_dimension=0, tiled=True),
        lax.psum_scatter(grad_proj_bias, ("ctx", "fsdp"), scatter_dimension=0, tiled=True),
    )
    return (
        block_output,
        input_grad,
        sharded[0],
        sharded[1],
        sharded[2],
        sharded[3],
        sharded[4],
        sharded[5],
        sharded[6],
        sharded[7],
        sharded[8],
        sharded[9],
        sharded[10],
        sharded[11],
        sharded[12],
    )


def solution(mesh):
    placed = (
        P("fsdp", "ctx", None, None, None),
        P("fsdp", None),
        P("fsdp", None),
        P("fsdp", None),
        P("fsdp", None),
        P("fsdp"),
        P("fsdp"),
        P("fsdp"),
        P("fsdp"),
        P("fsdp"),
        P("fsdp"),
        P("fsdp"),
        P("fsdp"),
        P("fsdp"),
        P("fsdp", "ctx", None, None, None),
    )
    return jax.shard_map(
        on_device,
        mesh=mesh,
        in_specs=placed,
        out_specs=(
            P("fsdp", "ctx", None, None, None),
            P("fsdp", "ctx", None, None, None),
            P(("ctx", "fsdp"), None),
            P(("ctx", "fsdp"), None),
            P(("ctx", "fsdp"), None),
            P(("ctx", "fsdp"), None),
            P(("ctx", "fsdp")),
            P(("ctx", "fsdp")),
            P(("ctx", "fsdp")),
            P(("ctx", "fsdp")),
            P(("ctx", "fsdp")),
            P(("ctx", "fsdp")),
            P(("ctx", "fsdp")),
            P(("ctx", "fsdp")),
            P(("ctx", "fsdp")),
        ),
        check_vma=False,
    )
```

profile of v0, /device:TPU:0, one launch (start us, length us, event | category | flops | bytes accessed | tf_op | source)
XLA Modules:
  0.0 1337.4 jit_solution(17769143029060880895)
XLA Ops:
  9.3 1.9 all-gather
  11.2 1.8 all-gather.1
  13.1 1.8 all-gather.2
  14.9 1.8 all-gather.3
  16.9 12.2 all-gather.15.cloned.1.call-done
  29.1 3.8 fusion.2
  33.0 0.9 fusion.47
  35.6 1.8 all-gather.5
  37.5 1.8 all-gather.6
  39.3 1.8 all-gather.4
  41.1 1.8 all_gather.65
  43.3 8.4 all-gather.25.cloned.1.call-done
  51.7 7.5 fusion.50
  59.2 73.1 %all-gather.19.cloned.1.call-done = bf16[2048,1024]{1,0:T(8,128)(2,1)} async-done(((bf16[128,1024]{1,0:T(8,128)(2,1)}), bf16[2048,1024]{1,0:T(8,128)(2,1)}) %all-gather.19.cloned.1.call-update) | async-done | bytes 4194320 | tf_op jit(solution)/shard_map/all_gather | solution.py:138
  132.3 6.7 copy.44
  139.0 71.2 %all-gather.17.cloned.1.call-done = bf16[2048,1024]{1,0:T(8,128)(2,1)} async-done(((bf16[128,1024]{1,0:T(8,128)(2,1)}), bf16[2048,1024]{1,0:T(8,128)(2,1)}) %all-gather.17.cloned.1.call-update) | async-done | bytes 4194320 | tf_op jit(solution)/shard_map/all_gather | solution.py:139
  210.2 6.5 copy.42
  216.8 5.1 fusion
  221.9 4.4 exponential_reduce_fusion
  226.3 3.0 copy-done
  229.3 10.7 convolution_convert_fusion.1
  240.0 2.2 fusion.49
  243.3 8.4 convert_reduce_fusion
  251.8 3.0 multiply_reduce_fusion.1
  256.8 8.5 fusion.17
  265.3 13.0 multiply_reduce_fusion
  278.4 12.0 multiply_convert_fusion
  290.4 1.3 convolution_multiply_fusion
  291.8 2.0 copy-done.1
  293.8 6.8 pad_maximum_fusion
  300.6 0.9 copy-done.19
  301.5 2.7 fusion.37
  304.3 8.8 fusion.44
  313.4 9.7 fusion.45
  323.2 7.7 fusion.13
  330.9 317.4 %reduce-scatter.6.cloned.1.call-done = f32[128,2048]{0,1:T(8,128)} async-done(((f32[2048,2048]{0,1:T(8,128)}), f32[128,2048]{0,1:T(8,128)}) %reduce-scatter.6.cloned.1.call-update) | async-done | bytes 1048592 | tf_op jit(solution)/shard_map/reduce_scatter | solution.py:228
  648.3 1.3 convert.10
  650.4 6.3 fusion.15
  657.4 1.8 all-gather.7
  659.2 1.0 convert_reduce_fusion.2
  660.2 6.5 fusion.12
  667.1 2.4 multiply_reduce_fusion.2
  669.4 45.9 %all-reduce.9 = (f32[1024]{0:T(1024)S(1)}, f32[1024]{0:T(1024)S(1)}, f32[1024]{0:T(1024)S(1)}, f32[1024]{0:T(1024)S(1)}, f32[1024]{0:T(1024)S(1)}, /*index=5*/f3...) all-reduce(f32[1024]{0:T(1024)S(1)} %get-tuple-element.17, ...), channel_id=7, replica_groups=mesh['ctx'=16,'fsdp'=2] {'ctx','fsdp'}, use_global_device_ids=true, to_apply=%region_17.18.clone | all-reduce | flops 12288 | bytes 98304
  720.6 1.0 multiply_add_fusion
  721.6 76.3 %reduce-scatter.10.cloned.1.call-done = f32[32,1024]{1,0:T(8,128)} async-done(((f32[1024,1024]{1,0:T(8,128)}), f32[32,1024]{1,0:T(8,128)}) %reduce-scatter.10.cloned.1.call-update) | async-done | bytes 131088 | tf_op jit(solution)/shard_map/reduce_scatter | solution.py:247
  798.0 181.6 %reduce-scatter.12.cloned.1.call-done = f32[32,4096]{1,0:T(8,128)} async-done(((f32[1024,4096]{1,0:T(8,128)}), f32[32,4096]{1,0:T(8,128)}) %reduce-scatter.12.cloned.1.call-update) | async-done | bytes 524304 | tf_op jit(solution)/shard_map/reduce_scatter | solution.py:248
  979.6 187.4 %reduce-scatter.14.cloned.1.call-done = f32[128,1024]{1,0:T(8,128)} async-done(((f32[4096,1024]{1,0:T(8,128)}), f32[128,1024]{1,0:T(8,128)}) %reduce-scatter.14.cloned.1.call-update) | async-done | bytes 524304 | tf_op jit(solution)/shard_map/reduce_scatter | solution.py:249
  1167.0 163.5 %reduce-scatter.8.cloned.1.call-done = f32[32,3072]{1,0:T(8,128)} async-done(((f32[1024,3072]{1,0:T(8,128)}), f32[32,3072]{1,0:T(8,128)}) %reduce-scatter.8.cloned.1.call-update) | async-done | bytes 393232 | tf_op jit(solution)/shard_map/reduce_scatter | solution.py:246
  (135 shorter events, 15.1 us)
Async XLA Ops:
  7.2 1.6 copy-start.6
  7.2 2.1 copy-start.21
  7.2 4.0 copy-start.22
  7.2 5.8 copy-start.23
  7.2 7.6 copy-start.24
  7.2 21.9 %all-gather.15.cloned.1.call-start = ((), (), s32[]{:S(2)}) async-start(), calls=%async_computation.5 | async-start | bytes 9437184 | tf_op jit(solution)/shard_map/all_gather | solution.py:86
  8.0 43.7 %all-gather.25.cloned.1.call-start = ((), (), s32[]{:S(2)}) async-start(), calls=%async_computation.10 | async-start | bytes 12582912 | tf_op jit(solution)/shard_map/all_gather | solution.py:89
  8.7 123.6 %all-gather.19.cloned.1.call-start = ((), (), s32[]{:S(2)}) async-start(), calls=%async_computation.7 | async-start | bytes 4456448 | tf_op jit(solution)/shard_map/all_gather | solution.py:138
  16.9 16.0 %copy-start.12 = (bf16[128,1024]{1,0:T(8,128)(2,1)}, bf16[128,1024]{1,0:T(8,128)(2,1)S(1)}, u32[]{:S(2)}) copy-start(bf16[128,1024]{1,0:T(8,128)(2,1)S(1)} %add_convert_fusion.1) | copy-start | bytes 786436
  32.9 2.7 copy-start.25
  32.9 4.5 copy-start.26
  32.9 6.3 copy-start.27
  32.9 8.1 copy-start.20
  32.9 18.8 %copy-start.11 = (bf16[1,1,2,64,1024]{4,3,2,1,0:T(8,128)(2,1)S(1)}, bf16[1,1,2,64,1024]{4,3,2,1,0:T(8,128)(2,1)}, u32[]{:S(2)}) copy-start(bf16[1,1,2,64,1024]{4,3,2,1,0:T(8,128)(2,1)} %param.29) | copy-start | bytes 786436
  33.8 176.4 %all-gather.17.cloned.1.call-start = ((), (), s32[]{:S(2)}) async-start(), calls=%async_computation.6 | async-start | bytes 4456448 | tf_op jit(solution)/shard_map/all_gather | solution.py:139
  34.4 205.6 %all-gather.21.cloned.1.call-start = ((), (), s32[]{:S(2)}) async-start(), calls=%async_computation.8 | async-start | bytes 3145728 | tf_op jit(solution)/shard_map/all_gather | solution.py:87
  35.0 208.3 %all-gather.23.cloned.1.call-start = ((), (), s32[]{:S(2)}) async-start(), calls=%async_computation.9 | async-start | bytes 12582912 | tf_op jit(solution)/shard_map/all_gather | solution.py:88
  35.6 612.7 %reduce-scatter.6.cloned.1.call-start = ((), (), s32[]{:S(2)}) async-start(), calls=%async_computation.11 | async-start | bytes 17825792 | tf_op jit(solution)/shard_map/reduce_scatter | solution.py:228
  43.3 173.5 %copy-start.14 = (bf16[128,1024]{0,1:T(8,128)(2,1)}, bf16[128,1024]{0,1:T(8,128)(2,1)S(1)}, u32[]{:S(2)}) copy-start(bf16[128,1024]{0,1:T(8,128)(2,1)S(1)} %copy.43) | copy-start | bytes 786436
  221.9 7.4 copy-start
  221.9 7.4 copy-start.2
  240.0 11.8 copy-start.18
  243.3 8.4 copy-start.4
  251.8 3.1 copy-start.9
  251.8 3.3 copy-start.5
  256.8 8.5 copy-start.3
  278.4 12.0 copy-start.15
  290.4 3.4 copy-start.1
  300.5 0.9 copy-start.19
  300.6 3.7 copy-start.10
  300.6 497.4 %reduce-scatter.10.cloned.1.call-start = ((), (), s32[]{:S(2)}) async-start(), calls=%async_computation.13 | async-start | bytes 4325376 | tf_op jit(solution)/shard_map/reduce_scatter | solution.py:247
  304.2 675.4 %reduce-scatter.12.cloned.1.call-start = ((), (), s32[]{:S(2)}) async-start(), calls=%async_computation.14 | async-start | bytes 17301504 | tf_op jit(solution)/shard_map/reduce_scatter | solution.py:248
  313.1 853.9 %reduce-scatter.14.cloned.1.call-start = ((), (), s32[]{:S(2)}) async-start(), calls=%async_computation.15 | async-start | bytes 17301504 | tf_op jit(solution)/shard_map/reduce_scatter | solution.py:249
  323.1 327.2 %copy-start.13 = (bf16[128,1024]{1,0:T(8,128)(2,1)S(1)}, bf16[128,1024]{1,0:T(8,128)(2,1)}, u32[]{:S(2)}) copy-start(bf16[128,1024]{1,0:T(8,128)(2,1)} %copy-done.12) | copy-start | bytes 786436
  323.1 1007.3 %reduce-scatter.8.cloned.1.call-start = ((), (), s32[]{:S(2)}) async-start(), calls=%async_computation.12 | async-start | bytes 12976128 | tf_op jit(solution)/shard_map/reduce_scatter | solution.py:246
  330.8 325.9 %copy-start.16 = (bf16[16,64,128]{2,1,0:T(8,128)(2,1)}, bf16[16,64,128]{2,1,0:T(8,128)(2,1)S(1)}, u32[]{:S(2)}) copy-start(bf16[16,64,128]{2,1,0:T(8,128)(2,1)S(1)} %fusion.13) | copy-start | bytes 786436
  649.6 0.8 copy-start.7
  656.7 0.7 copy-start.28
  656.7 10.3 slice-start
  660.2 6.6 copy-start.8
  660.2 6.6 copy-start.17
  660.2 6.9 slice-start.1
Sparse Core Ops, SparseCore 0:
  9.6 19.4 all-gather.14
  30.6 21.0 all-gather.24
  55.0 77.2 all-gather.18
  135.5 74.6 all-gather.16
  211.6 9.1 all-gather.20
  222.2 21.0 all-gather.22
  300.7 347.5 reduce-scatter.5
  651.1 146.8 reduce-scatter.9
  800.9 178.7 reduce-scatter.11
  982.3 184.6 reduce-scatter.13
  1173.6 156.8 reduce-scatter.7
where the time goes:
time: 1340 us
  waiting for transfers between devices  1100 us (82%)
  matrix products  109 us (8%)
  blocking collectives  62.1 us (5%)
  other arithmetic  28.2 us (2%)
  local copies, waits for them, and re-layouts  28 us (2%)
  between operations  14.9 us (1%)
    reduce_scatter x1, waiting for transfers between devices, on_device(): lax.psum_scatter(key_terms(jnp.int32(0), lax.axis_size('ctx') * seq_rows)...  317 us
    reduce_scatter x1, waiting for transfers between devices, on_device(): lax.psum_scatter(grad_proj, ('ctx', 'fsdp'), scatter_dimension=0, tiled=T...  187 us
    reduce_scatter x1, waiting for transfers between devices, on_device(): lax.psum_scatter(grad_fc, ('ctx', 'fsdp'), scatter_dimension=0, tiled=True)  182 us
    reduce_scatter x1, waiting for transfers between devices, on_device(): lax.psum_scatter(grad_qkv, ('ctx', 'fsdp'), scatter_dimension=0, tiled=True)  163 us
    reduce_scatter x1, waiting for transfers between devices, on_device(): lax.psum_scatter(grad_out, ('ctx', 'fsdp'), scatter_dimension=0, tiled=True)  76.3 us
    all_gather x1, waiting for transfers between devices, on_device(): key_all = lax.all_gather(keys, 'ctx', axis=0, tiled=True)  73.1 us
    all_gather x1, waiting for transfers between devices, on_device(): value_all = lax.all_gather(values, 'ctx', axis=0, tiled=True)  71.2 us
    unnamed x1, blocking collectives  45.9 us
  transfers between devices with their start and end apart: 11, of which 10 were waited for; matrix products, arithmetic and copies ran while one was open for 8% of the time, Pallas kernels for 0%

commit v1 on v0

--- a/solution.py
+++ b/solution.py
@@ -55,7 +55,7 @@
     return jnp.where(allowed[None], scores, -1e30)
 
 
-def on_device(
+def general_layer(
     block_input,
     w_qkv,
     w_out,
@@ -276,6 +276,166 @@
     )
 
 
+def headwise_layer(
+    block_input,
+    w_qkv,
+    w_out,
+    w_fc,
+    w_proj,
+    ln1_gain,
+    ln1_bias,
+    ln2_gain,
+    ln2_bias,
+    bias_q,
+    bias_v,
+    bias_out,
+    bias_fc,
+    bias_proj,
+    cotangent,
+):
+    blk_rows = block_input.shape[3]
+    width = block_input.shape[4]
+    seq_rows = 2 * blk_rows
+    groups = lax.axis_size("ctx")
+    shards = groups * lax.axis_size("fsdp")
+    head_size = width // HEADS
+    scaling = head_size ** (-0.5)
+    full_rows = groups * seq_rows
+    weight_qkv, weight_out, weight_fc, weight_proj = (
+        lax.all_gather(w, "fsdp", axis=0, tiled=True) for w in (w_qkv, w_out, w_fc, w_proj)
+    )
+    small = (ln1_gain, ln1_bias, ln2_gain, ln2_bias, bias_q, bias_v, bias_out, bias_fc, bias_proj)
+    joined = lax.all_gather(jnp.concatenate(small), "fsdp", axis=0).astype(jnp.float32)
+    vectors, at = [], 0
+    for piece in small:
+        vectors.append(joined[:, at : at + piece.shape[0]].reshape(-1))
+        at += piece.shape[0]
+    (
+        gain_one,
+        shift_one,
+        gain_two,
+        shift_two,
+        query_bias,
+        value_bias,
+        out_bias,
+        fc_bias,
+        proj_bias,
+    ) = vectors
+    every_index = jnp.arange(full_rows)
+    every_owner = every_index // seq_rows
+    every_block = jnp.where(
+        every_index // blk_rows % 2 == 0, every_owner, 2 * groups - 1 - every_owner
+    )
+    every_pos = every_block * blk_rows + every_index % blk_rows
+    allowed = every_pos[None, :] <= every_pos[:, None]
+
+    def to_heads(rows):
+        parts = rows.reshape(seq_rows, -1, HEADS, head_size)
+        moved = lax.all_to_all(parts, "ctx", split_axis=2, concat_axis=0, tiled=True)
+        return moved[:, :, 0]
+
+    def to_tokens(rows):
+        parts = rows.reshape(full_rows, -1, 1, head_size)
+        moved = lax.all_to_all(parts, "ctx", split_axis=0, concat_axis=2, tiled=True)
+        return moved.reshape(seq_rows, -1)
+
+    inputs = block_input.reshape(seq_rows, width).astype(jnp.float32)
+    normal_one, inverse_one = norm_parts(inputs)
+    normed_one = (normal_one * gain_one + shift_one).astype(jnp.bfloat16)
+    bias_all = jnp.concatenate([query_bias, jnp.zeros_like(query_bias), value_bias])
+    projected = (
+        jnp.dot(normed_one, weight_qkv, preferred_element_type=jnp.float32) + bias_all
+    ).astype(jnp.bfloat16)
+    triple = to_heads(projected)
+    queries, keys, values = triple[:, 0], triple[:, 1], triple[:, 2]
+    scores = jnp.where(allowed, right_transposed(queries, keys) * scaling, -1e30)
+    row_top = jnp.max(scores, -1, keepdims=True)
+    log_sum = row_top + jnp.log(jnp.sum(jnp.exp(scores - row_top), -1, keepdims=True))
+    probs = jnp.exp(scores - log_sum)
+    probs_low = probs.astype(jnp.bfloat16)
+    mixed = jnp.dot(probs_low, values, preferred_element_type=jnp.float32)
+    attended = to_tokens(mixed.astype(jnp.bfloat16))
+    residual = inputs + jnp.dot(attended, weight_out, preferred_element_type=jnp.float32) + out_bias
+    normal_two, inverse_two = norm_parts(residual)
+    normed_two = (normal_two * gain_two + shift_two).astype(jnp.bfloat16)
+    hidden = jnp.dot(normed_two, weight_fc, preferred_element_type=jnp.float32) + fc_bias
+    activated, gelu_pullback = jax.vjp(partial(jax.nn.gelu, approximate=True), hidden)
+    activated_low = activated.astype(jnp.bfloat16)
+    result = (
+        residual
+        + jnp.dot(activated_low, weight_proj, preferred_element_type=jnp.float32)
+        + proj_bias
+    )
+    block_output = result.astype(jnp.bfloat16).reshape(block_input.shape)
+    out_grad_low = cotangent.reshape(seq_rows, width)
+    upstream = out_grad_low.astype(jnp.float32)
+    grad_proj = rows_product(activated_low, out_grad_low)
+    grad_proj_bias = jnp.sum(upstream, 0)
+    hidden_grad = gelu_pullback(right_transposed(out_grad_low, weight_proj))[0].astype(jnp.bfloat16)
+    grad_fc = rows_product(normed_two, hidden_grad)
+    grad_fc_bias = jnp.sum(hidden_grad.astype(jnp.float32), 0)
+    residual_part, grad_gain_two, grad_shift_two = norm_grads(
+        right_transposed(hidden_grad, weight_fc), normal_two, inverse_two, gain_two
+    )
+    residual_grad = upstream + residual_part
+    branch_grad = residual_grad.astype(jnp.bfloat16)
+    grad_out = rows_product(attended, branch_grad)
+    grad_out_bias = jnp.sum(branch_grad.astype(jnp.float32), 0)
+    attended_grad = to_heads(right_transposed(branch_grad, weight_out).astype(jnp.bfloat16))[:, 0]
+    prob_grad = right_transposed(attended_grad, values)
+    inner_sum = jnp.sum(probs * prob_grad, -1, keepdims=True)
+    score_grad = (probs * (prob_grad - inner_sum)).astype(jnp.bfloat16)
+    query_part = jnp.dot(score_grad, keys, preferred_element_type=jnp.float32) * scaling
+    key_part = rows_product(score_grad, queries) * scaling
+    value_part = rows_product(probs_low, attended_grad)
+    qkv_grad = to_tokens(
+        jnp.stack([query_part, key_part, value_part], 1).astype(jnp.bfloat16)
+    )
+    grad_qkv = rows_product(normed_one, qkv_grad)
+    qkv_sums = jnp.sum(qkv_grad.astype(jnp.float32), 0)
+    grad_query_bias = qkv_sums[:width]
+    grad_value_bias = qkv_sums[2 * width :]
+    input_part, grad_gain_one, grad_shift_one = norm_grads(
+        right_transposed(qkv_grad, weight_qkv), normal_one, inverse_one, gain_one
+    )
+    input_grad = (residual_grad + input_part).reshape(block_input.shape)
+    big = tuple(
+        lax.psum_scatter(
+            part.astype(jnp.bfloat16), ("ctx", "fsdp"), scatter_dimension=0, tiled=True
+        ).astype(jnp.float32)
+        for part in (grad_qkv, grad_out, grad_fc, grad_proj)
+    )
+    sums = (
+        grad_gain_one,
+        grad_shift_one,
+        grad_gain_two,
+        grad_shift_two,
+        grad_query_bias,
+        grad_value_bias,
+        grad_out_bias,
+        grad_fc_bias,
+        grad_proj_bias,
+    )
+    packed = lax.psum_scatter(
+        jnp.concatenate([part.reshape(shards, -1) for part in sums], 1),
+        ("ctx", "fsdp"),
+        scatter_dimension=0,
+        tiled=True,
+    )[0]
+    lows, at = [], 0
+    for part in sums:
+        count = part.shape[0] // shards
+        lows.append(packed[at : at + count])
+        at += count
+    return (block_output, input_grad, *big, *lows)
+
+
+def on_device(*arrays):
+    if lax.axis_size("ctx") == HEADS and arrays[0].shape[0] == 1:
+        return headwise_layer(*arrays)
+    return general_layer(*arrays)
+
+
 def solution(mesh):
     placed = (
         P("fsdp", "ctx", None, None, None),

time: 1340 us -> 704 us (0.53)
  waiting for transfers between devices: 1100 us -> 466 us
  starting transfers between devices: 0.69 us -> 21.5 us
  blocking collectives: 62.1 us -> 42.3 us
    reduce_scatter x5 -> x4, waiting for transfers between devices: 926 us -> 395 us  [headwise_layer(): lax.psum_scatter(part.astype(jnp.bfloat16), ('ctx', 'fsdp'), scatter_dime...]
    all_gather x6 -> x4, waiting for transfers between devices: 166 us -> 14.2 us  [headwise_layer(): lax.all_gather(w, 'fsdp', axis=0, tiled=True)]
    all_to_all x0 -> x4, waiting for transfers between devices: none -> 53.9 us  [the longest x2 27.1 us: to_tokens(): lax.all_to_all(parts, 'ctx', split_axis=0, concat_axis=2, tiled=True)]
    dot_general x10 -> x6, matrix products: 67.3 us -> 32.6 us  [the longest x1 10.4 us: headwise_layer(): mixed = jnp.dot(probs_low, values, preferred_element_type=jnp.float32)]
    dot_general x4 -> x6, matrix products: 13.8 us -> 37.3 us  [right_transposed(): lax.dot_general(left, weight, (((1,), (1,)), ((), ())), preferred_element...]
    all_to_all x0 -> x4, starting transfers between devices: none -> 20.7 us  [the longest x2 11.1 us: to_heads(): lax.all_to_all(parts, 'ctx', split_axis=2, concat_axis=0, tiled=True)]
    all_gather x9 -> x1, blocking collectives: 16.2 us -> 1.93 us  [headwise_layer(): lax.all_gather(jnp.concatenate(small), 'fsdp', axis=0).astype(jnp.float32)]
    dot_general x4 -> x6, matrix products: 27.5 us -> 27.3 us  [rows_product(): lax.dot_general(left, right, (((0,), (0,)), ((), ())), preferred_element_...]
  transfers between devices with their start and end apart: 11 -> 12, of which waited for: 10 -> 8; matrix products, arithmetic and copies ran while one was open for 8% -> 20% of each run, Pallas kernels for 0% -> 0%
where the time goes in v1:
time: 704 us; the launch traced here: 699 us
  waiting for transfers between devices  466 us (66%)
  matrix products  97.2 us (14%)
  blocking collectives  42.3 us (6%)
  other arithmetic  31.6 us (4%)
  local copies, waits for them, and re-layouts  26.1 us (4%)
  starting transfers between devices  21.5 us (3%)
  between operations  15 us (2%)
    reduce_scatter x4, waiting for transfers between devices, headwise_layer(): lax.psum_scatter(part.astype(jnp.bfloat16), ('ctx', 'fsdp'), scatter_dime...  395 us
    unnamed x1, blocking collectives  40.4 us
    dot_general x6, matrix products, right_transposed(): lax.dot_general(left, weight, (((1,), (1,)), ((), ())), preferred_element...  37.3 us
    dot_general x6, matrix products, rows_product(): lax.dot_general(left, right, (((0,), (0,)), ((), ())), preferred_element_...  27.3 us
    all_to_all x2, waiting for transfers between devices, to_tokens(): lax.all_to_all(parts, 'ctx', split_axis=0, concat_axis=2, tiled=True)  27.1 us
    all_to_all x2, waiting for transfers between devices, to_heads(): lax.all_to_all(parts, 'ctx', split_axis=2, concat_axis=0, tiled=True)  26.7 us
    all_gather x4, waiting for transfers between devices, headwise_layer(): lax.all_gather(w, 'fsdp', axis=0, tiled=True)  14.2 us
  transfers between devices with their start and end apart: 12, of which 8 were waited for; matrix products, arithmetic and copies ran while one was open for 20% of the time, Pallas kernels for 0%

profile of v1, /device:TPU:0, one launch (start us, length us, event | category | flops | bytes accessed | tf_op | source)
XLA Modules:
  0.0 699.2 jit_solution(12446721838919800193)
XLA Ops:
  12.6 1.9 all-gather
  14.9 14.2 %all-gather.6.cloned.1.call-done = bf16[1024,3072]{1,0:T(8,128)(2,1)} async-done(((bf16[512,3072]{1,0:T(8,128)(2,1)}), bf16[1024,3072]{1,0:T(8,128)(2,1)}) %all-gather.6.cloned.1.call-update) | async-done | bytes 6291472 | tf_op jit(solution)/shard_map/all_gather | solution.py:305
  29.1 3.8 fusion.1
  34.2 7.3 %all-to-all-start = ((bf16[128,3,16,64]{0,3,1,2:T(8,128)(2,1)}), bf16[128,3,16,64]{0,3,1,2:T(8,128)(2,1)S(1)}, u32[]{:S(2)}, u32[]{:S(2)}) async-start(bf16[128,3,16,64]{0,3,1,2:T(8,128)(2,1)} %copy.69), calls=%async_computation | async-start | bytes 1572864 | tf_op jit(solution)/shard_map/all_to_all | solution.py:334
  41.5 20.1 %all-to-all-done = bf16[128,3,16,64]{0,3,1,2:T(8,128)(2,1)S(1)} async-done(((bf16[128,3,16,64]{0,3,1,2:T(8,128)(2,1)}), bf16[128,3,16,64]{0,3,1,2:T(8,128)(2,1)S(1)}, u32[]{:S(2)}, u32[]{:S(2)}) %all-to-all-start) | async-done | bytes 786464 | tf_op jit(solution)/shard_map/all_to_all | solution.py:334
  62.4 7.1 %fusion.43 = (f32[2048]{0:T(1024)S(1)}, f32[2048,2048]{0,1:T(8,128)}) fusion(bf16[2048,3,64]{0,2,1:T(8,128)(2,1)S(1)} %squeeze.13, s32[2048]{0:T(1024)S(1)} %fusion.35), kind=kOutput, calls=%fused_computation.124 | convolution fusion | flops 553646080 | bytes 17326080 | tf_op jit(solution)/shard_map/dot_general | solution.py:36
  69.6 9.1 %exponential_reduce_fusion = f32[2048]{0:T(1024)S(1)} fusion(f32[2048,2048]{0,1:T(8,128)} %get-tuple-element.46, f32[2048]{0:T(1024)S(1)} %get-tuple-element.45), kind=kLoop, calls=%fused_computation.3 | loop fusion | flops 8386560 | bytes 16793600 | tf_op jit(solution)/shard_map/reduce_sum | solution.py:353
  78.7 10.4 %fusion.7 = bf16[2048,1,1,64]{0,3,2,1:T(8,128)(2,1)S(1)} fusion(f32[2048,2048]{0,1:T(8,128)} %get-tuple-element.46, f32[2048]{0:T(1024)S(1)} %log_add_fusion, bf16[2048,3,64]{0,2,1:T(8,128)(2,1)S(1)} %squeeze.13), kind=kOutput, calls=%fused_computation.23 | convolution fusion | flops 545390592 | bytes 17309696 | tf_op jit(solution)/shard_map/dot_general | solution.py:356
  90.6 1.1 reshape.372
  91.7 5.3 all-to-all-start.1
  97.1 8.4 %all-to-all-done.1 = bf16[16,2,4096]{2,1,0:T(2,128)(2,1)S(1)} async-done(((bf16[16,2,4096]{2,1,0:T(2,128)(2,1)}), bf16[16,2,4096]{2,1,0:T(2,128)(2,1)S(1)}, u32[]{:S(2)}, u32[]{:S(2)}) %all-to-all-start.1) | async-done | bytes 262176 | tf_op jit(solution)/shard_map/all_to_all | solution.py:339
  106.9 2.1 fusion.44
  109.3 7.5 %fusion.45 = f32[128,4096]{1,0:T(8,128)} fusion(bf16[128,1024]{1,0:T(8,128)(2,1)S(1)} %bitcast.163, bf16[4096,1024]{1,0:T(8,128)(2,1)} %all-gather.12.cloned.1.call-done), kind=kOutput, calls=%fused_computation.126 | convolution fusion | flops 1073741824 | bytes 10747904 | tf_op jit(solution)/shard_map/dot_general | solution.py:36
  116.8 8.4 %convert_reduce_fusion = (f32[4096]{0:T(1024)S(1)}, bf16[128,4096]{1,0:T(8,128)(2,1)S(1)}, f32[128,4096]{1,0:T(8,128)}) fusion(f32[128,4096]{1,0:T(8,128)} %fusion.45, f32[4096]{0:T(1024)S(1)} %bitcast.189, bf16[1024,4096]{1,0:T(8,128)(2,1)} %all-gather.10.cloned.1.call-done, f32[128,1024]{1,0:T(8,128)S(1)} %get-tuple-element.48, f32[1024]{0:T(1024)S(1)} %bitcast.183, ...), kind=kOutput, calls=%fused_computation.31 | convolution fusion | flops 1086451712 | bytes 14197760 | tf_op jit(solution)/shard_map/dot_general | solution.py:361
  125.3 3.0 multiply_reduce_fusion.1
  130.3 3.8 all-to-all-start.2
  134.4 2.0 convolution_convert_fusion.5
  136.4 6.7 all-to-all-done.2
  143.3 13.3 %multiply_reduce_fusion = (f32[2048]{0:T(1024)S(1)}, f32[2048,2048]{0,1:T(8,128)}) fusion(f32[2048,2048]{0,1:T(8,128)} %get-tuple-element.46, f32[2048]{0:T(1024)S(1)} %log_add_fusion, bf16[2048,3,64]{0,2,1:T(8,128)(2,1)S(1)} %squeeze.13, bf16[8,8,16,128]{3,2,1,0:T(8,128)(2,1)S(1)} %bitcast.164), kind=kOutput, calls=%fused_computation.1 | convolution fusion | flops 549451776 | bytes 34095104 | tf_op jit(solution)/shard_map/dot_general | solution.py:36
  156.8 1.8 slice-done.2
  158.6 1.2 slice-done.3
  159.8 8.3 %multiply_convert_fusion = bf16[2048,2048]{0,1:T(8,128)(2,1)S(1)} fusion(f32[2048,2048]{0,1:T(8,128)} %get-tuple-element.52, f32[2048,2048]{0,1:T(8,128)S(1)} %bitcast.155, f32[2048]{0:T(1024)S(1)} %get-tuple-element.51, f32[2048]{0:T(1024)S(1)} %log_add_fusion), kind=kLoop, calls=%fused_computation | loop fusion | flops 16777216 | bytes 41959424 | tf_op jit(solution)/shard_map/convert_element_type | solution.py:387
  168.1 2.7 fusion.5
  170.7 1.6 fusion.4
  172.3 2.8 fusion.6
  176.1 2.8 copy.77
  179.0 2.5 reshape.374
  181.5 4.3 all-to-all-start.3
  186.8 18.7 %all-to-all-done.3 = bf16[16,2,12288]{2,1,0:T(2,128)(2,1)} async-done(((bf16[16,2,12288]{2,1,0:T(2,128)(2,1)}), bf16[16,2,12288]{2,1,0:T(2,128)(2,1)}, u32[]{:S(2)}, u32[]{:S(2)}) %all-to-all-start.3) | async-done | bytes 786464 | tf_op jit(solution)/shard_map/all_to_all | solution.py:339
  205.5 2.9 reshape.375
  208.4 2.2 copy.83
  210.5 5.7 convolution_convert_fusion.2
  216.6 6.9 convolution_convert_fusion.1
  223.6 7.2 %convolution_convert_fusion = bf16[4096,1024]{1,0:T(8,128)(2,1)} fusion(bf16[128,1024]{1,0:T(8,128)(2,1)} %bitcast.162, f32[128,4096]{1,0:T(8,128)} %get-tuple-element.49), kind=kOutput, calls=%fused_computation.6 | convolution fusion | flops 1082654720 | bytes 10747904 | tf_op jit(solution)/shard_map/dot_general | solution.py:30
  230.8 1.0 convert_reduce_fusion.2
  232.1 6.3 fusion.19
  238.4 1.9 copy.82
  240.3 1.6 convert_reduce_fusion.1
  242.2 5.5 multiply_reduce_fusion.2
  247.9 40.4 %all-reduce = f32[32,384]{1,0:T(8,128)S(1)} all-reduce(f32[32,384]{1,0:T(8,128)S(1)} %concatenate.19), channel_id=7, replica_groups=mesh['ctx'=16,'fsdp'=2] {'ctx','fsdp'}, use_global_device_ids=true, to_apply=%region_23.24.clone | all-reduce | flops 12288 | bytes 98304
  289.5 1.0 multiply_add_fusion
  290.5 1.5 convert_element_type.121
  292.0 101.1 %reduce-scatter.5.cloned.1.call-done = bf16[32,3072]{1,0:T(8,128)(2,1)} async-done(((bf16[1024,3072]{1,0:T(8,128)(2,1)}), bf16[32,3072]{1,0:T(8,128)(2,1)}) %reduce-scatter.5.cloned.1.call-update) | async-done | bytes 196624 | tf_op jit(solution)/shard_map/reduce_scatter | solution.py:403
  393.1 1.7 convert_element_type.119
  394.8 148.4 %reduce-scatter.9.cloned.1.call-done = bf16[32,4096]{1,0:T(8,128)(2,1)} async-done(((bf16[1024,4096]{1,0:T(8,128)(2,1)}), bf16[32,4096]{1,0:T(8,128)(2,1)}) %reduce-scatter.9.cloned.1.call-update) | async-done | bytes 262160 | tf_op jit(solution)/shard_map/reduce_scatter | solution.py:403
  543.3 1.8 convert_element_type.123
  545.0 145.3 %reduce-scatter.11.cloned.1.call-done = bf16[128,1024]{1,0:T(8,128)(2,1)} async-done(((bf16[4096,1024]{1,0:T(8,128)(2,1)}), bf16[128,1024]{1,0:T(8,128)(2,1)}) %reduce-scatter.11.cloned.1.call-update) | async-done | bytes 262160 | tf_op jit(solution)/shard_map/reduce_scatter | solution.py:403
  690.3 1.8 convert_element_type.125
  (125 shorter events, 17.8 us)
Async XLA Ops:
  7.2 21.9 %all-gather.6.cloned.1.call-start = ((), (), s32[]{:S(2)}) async-start(), calls=%async_computation.8 | async-start | bytes 9437184 | tf_op jit(solution)/shard_map/all_gather | solution.py:305
  7.9 99.0 %all-gather.8.cloned.1.call-start = ((), (), s32[]{:S(2)}) async-start(), calls=%async_computation.9 | async-start | bytes 3145728 | tf_op jit(solution)/shard_map/all_gather | solution.py:305
  8.7 1.4 copy-start
  8.7 2.0 copy-start.6
  8.7 2.1 copy-start.7
  8.7 2.3 copy-start.8
  8.7 2.6 copy-start.9
  8.7 2.8 copy-start.10
  8.7 3.0 copy-start.11
  8.7 3.2 copy-start.12
  8.7 3.4 copy-start.5
  8.8 3.6 copy-start.13
  8.8 100.5 %all-gather.12.cloned.1.call-start = ((), (), s32[]{:S(2)}) async-start(), calls=%async_computation.11 | async-start | bytes 12582912 | tf_op jit(solution)/shard_map/all_gather | solution.py:305
  9.5 107.3 %all-gather.10.cloned.1.call-start = ((), (), s32[]{:S(2)}) async-start(), calls=%async_computation.10 | async-start | bytes 12582912 | tf_op jit(solution)/shard_map/all_gather | solution.py:305
  34.2 27.4 %all-to-all-start = ((bf16[128,3,16,64]{0,3,1,2:T(8,128)(2,1)}), bf16[128,3,16,64]{0,3,1,2:T(8,128)(2,1)S(1)}, u32[]{:S(2)}, u32[]{:S(2)}) async-start(bf16[128,3,16,64]{0,3,1,2:T(8,128)(2,1)} %copy.69), calls=%async_computation | async-start | bytes 1572864 | tf_op jit(solution)/shard_map/all_to_all | solution.py:334
  90.6 18.7 %copy-start.4 = (bf16[1,1,2,64,1024]{4,3,2,1,0:T(8,128)(2,1)S(1)}, bf16[1,1,2,64,1024]{4,3,2,1,0:T(8,128)(2,1)}, u32[]{:S(2)}) copy-start(bf16[1,1,2,64,1024]{4,3,2,1,0:T(8,128)(2,1)} %param.29) | copy-start | bytes 786436
  91.7 13.8 %all-to-all-start.1 = ((bf16[16,2,4096]{2,1,0:T(2,128)(2,1)}), bf16[16,2,4096]{2,1,0:T(2,128)(2,1)S(1)}, u32[]{:S(2)}, u32[]{:S(2)}) async-start(bf16[16,2,4096]{2,1,0:T(2,128)(2,1)} %reshape.372), calls=%async_computation.1 | async-start | bytes 524288 | tf_op jit(solution)/shard_map/all_to_all | solution.py:339
  116.8 8.4 %copy-start.1 = (bf16[1024,4096]{1,0:T(8,128)(2,1)S(1)}, bf16[1024,4096]{1,0:T(8,128)(2,1)}, u32[]{:S(2)}) copy-start(bf16[1024,4096]{1,0:T(8,128)(2,1)} %all-gather.10.cloned.1.call-done) | copy-start | bytes 25165828
  125.3 3.0 copy-start.3
  125.3 3.3 copy-start.2
  130.3 12.8 %all-to-all-start.2 = ((bf16[128,1,16,64]{0,3,1,2:T(8,128)(2,1)}), bf16[128,1,16,64]{0,3,1,2:T(8,128)(2,1)S(1)}, u32[]{:S(2)}, u32[]{:S(2)}) async-start(bf16[128,1,16,64]{0,3,1,2:T(8,128)(2,1)} %bitcast.13), calls=%async_computation.2 | async-start | bytes 524288 | tf_op jit(solution)/shard_map/all_to_all | solution.py:334
  134.1 156.4 %reduce-scatter.7.cloned.1.call-start = ((), (), s32[]{:S(2)}) async-start(), calls=%async_computation.13 | async-start | bytes 2162688 | tf_op jit(solution)/shard_map/reduce_scatter | solution.py:403
  143.3 13.4 %slice-start = ((s8[16777216]{0:T(1024)(128)(4,1)}), s8[4194304]{0:T(1024)(128)(4,1)S(1)}, s32[]{:S(2)}) async-start(s8[16777216]{0:T(1024)(128)(4,1)} %bitcast.154), calls=%async_computation.16 | async-start | bytes 8388608
  143.3 13.5 %slice-start.1 = ((s8[16777216]{0:T(1024)(128)(4,1)}), s8[4194304]{0:T(1024)(128)(4,1)S(1)}, s32[]{:S(2)}) async-start(s8[16777216]{0:T(1024)(128)(4,1)} %bitcast.154), calls=%async_computation.17 | async-start | bytes 8388608
  143.3 15.3 %slice-start.2 = ((s8[16777216]{0:T(1024)(128)(4,1)}), s8[4194304]{0:T(1024)(128)(4,1)S(1)}, s32[]{:S(2)}) async-start(s8[16777216]{0:T(1024)(128)(4,1)} %bitcast.154), calls=%async_computation.18 | async-start | bytes 8388608
  143.3 16.5 %slice-start.3 = ((s8[16777216]{0:T(1024)(128)(4,1)}), s8[4194304]{0:T(1024)(128)(4,1)S(1)}, s32[]{:S(2)}) async-start(s8[16777216]{0:T(1024)(128)(4,1)} %bitcast.154), calls=%async_computation.19 | async-start | bytes 8388608
  181.5 24.0 %all-to-all-start.3 = ((bf16[16,2,12288]{2,1,0:T(2,128)(2,1)}), bf16[16,2,12288]{2,1,0:T(2,128)(2,1)}, u32[]{:S(2)}, u32[]{:S(2)}) async-start(bf16[16,2,12288]{2,1,0:T(2,128)(2,1)} %reshape.374), calls=%async_computation.3 | async-start | bytes 1572864 | tf_op jit(solution)/shard_map/all_to_all | solution.py:339
  185.8 207.4 %reduce-scatter.5.cloned.1.call-start = ((), (), s32[]{:S(2)}) async-start(), calls=%async_computation.12 | async-start | bytes 6488064 | tf_op jit(solution)/shard_map/reduce_scatter | solution.py:403
  216.3 327.0 %reduce-scatter.9.cloned.1.call-start = ((), (), s32[]{:S(2)}) async-start(), calls=%async_computation.14 | async-start | bytes 8650752 | tf_op jit(solution)/shard_map/reduce_scatter | solution.py:403
  223.5 466.8 %reduce-scatter.11.cloned.1.call-start = ((), (), s32[]{:S(2)}) async-start(), calls=%async_computation.15 | async-start | bytes 8650752 | tf_op jit(solution)/shard_map/reduce_scatter | solution.py:403
Sparse Core Ops, SparseCore 0:
  9.6 19.4 all-gather.5
  30.6 11.7 all-gather.7
  44.0 21.0 all-gather.11
  66.4 21.0 all-gather.9
  136.9 139.4 reduce-scatter.6
  282.8 110.2 reduce-scatter.4
  395.4 147.7 reduce-scatter.8
  545.6 144.7 reduce-scatter.10

commit v2 on v0

--- a/solution.py
+++ b/solution.py
@@ -1,11 +1,15 @@
 from functools import partial
+from types import SimpleNamespace
 
 import jax
 import jax.numpy as jnp
 from jax import lax
+from jax.experimental import pallas as pl
+from jax.experimental.pallas import tpu as pltpu
 from jax.sharding import PartitionSpec as P
 
 HEADS = 16
+VMEM_BYTES = 62 * 2**20
 
 
 def norm_parts(values):
@@ -55,7 +59,7 @@
     return jnp.where(allowed[None], scores, -1e30)
 
 
-def on_device(
+def general_layer(
     block_input,
     w_qkv,
     w_out,
@@ -276,6 +280,900 @@
     )
 
 
+MESH = pl.DeviceIdType.MESH
+BF16, F32 = jnp.bfloat16, jnp.float32
+PLANE = 4
+NEG = -1e30
+
+
+def remote(src, dst, sent, received, device):
+    return pltpu.make_async_remote_copy(
+        src_ref=src,
+        dst_ref=dst,
+        send_sem=sent,
+        recv_sem=received,
+        device_id=device,
+        device_id_type=MESH,
+    )
+
+
+def dot(left, right):
+    return jnp.dot(left, right, preferred_element_type=F32)
+
+
+def low_lanes(rows):
+    return lax.broadcasted_iota(jnp.int32, (rows, 128), 1) < 64
+
+
+def swap(block):
+    return pltpu.roll(block, 64, 1)
+
+
+def pack_pair(pair):
+    half = pair.shape[0] // 2
+    low = low_lanes(half)
+    top, bottom = pair[:half], pair[half:]
+    return jnp.where(low, top, swap(bottom)), jnp.where(low, swap(top), bottom)
+
+
+def unpack_pair(even, odd):
+    low = low_lanes(even.shape[0])
+    return jnp.concatenate(
+        [jnp.where(low, even, swap(odd)), jnp.where(low, swap(even), odd)], 0
+    )
+
+
+def part(index, size):
+    return pl.ds(pl.multiple_of(index * size, size), size)
+
+
+def layer_shapes(rows, width, ff, groups):
+    members = 2 * PLANE
+    layers = groups // PLANE
+    tokens = members * rows
+    half = rows // 2
+    keys = groups * half
+    share = width // members
+    return dict(
+        w_qkv=((width, 3 * width), BF16),
+        w_out=((width, width), BF16),
+        w_fc=((width, ff), BF16),
+        w_proj=((ff, width), BF16),
+        vec=((2, 16, width // 2), F32),
+        row=((8, width), F32),
+        cot_all=((members, rows, width), BF16),
+        n1=((rows, width), BF16),
+        n1_t=((width, tokens), BF16),
+        stage=((groups, 3, half, 128), BF16),
+        qkv=((3, keys, 128), BF16),
+        kv_roll=((2, keys, 128), BF16),
+        q_low=((2, keys, 128), BF16),
+        g_low=((2, keys, 128), BF16),
+        q_t=((128, keys), BF16),
+        g_t=((128, keys), BF16),
+        stat=((2, keys, 128), F32),
+        mixed=((keys, 128), F32),
+        o_out=((groups, half, 128), BF16),
+        o_in=((groups, half, 128), BF16),
+        att=((rows, width), BF16),
+        att_t=((layers, members, width // members // layers, rows), BF16),
+        att_all=((layers, width // members // layers, tokens), BF16),
+        res=((rows, width), F32),
+        n2=((rows, width), BF16),
+        n2_t=((width, tokens), BF16),
+        act_t=((ff, rows), BF16),
+        act_all=((layers, ff // members // layers, tokens), BF16),
+        hg_out=((members, rows, ff // members), BF16),
+        hg_all=((members, rows, ff // members), BF16),
+        acc_o=((rows, width), F32),
+        acc_d=((rows, width), F32),
+        res_grad=((rows, width), F32),
+        bg_all=((members, rows, width), BF16),
+        g_out=((groups, half, 128), BF16),
+        g_in=((keys, 128), BF16),
+        dk_t=((128, keys), F32),
+        dv_t=((128, keys), F32),
+        back=((groups, 3, half, 128), BF16),
+        qg=((rows, 3 * width), BF16),
+        qg_out=((members, rows, 3 * share), BF16),
+        qg_all=((members, rows, 3 * share), BF16),
+        fc_own=((width // layers, ff // members), F32),
+        qkv_own=((width // layers, 3 * share), F32),
+        fc_x=((members, width // layers // members, ff // members), BF16),
+        fc_y=((members, width // layers // members, ff // members), BF16),
+        qkv_x=((members, width // layers // members, 3 * share), BF16),
+        qkv_y=((members, width // layers // members, 3 * share), BF16),
+        sums=((16, width), F32),
+        sums_in=((7, 16, width), F32),
+    )
+
+
+SEMAPHORES = dict(
+    local=4,
+    w_sent=15,
+    w_got=15,
+    v_sent=1,
+    v_got=1,
+    qkv_sent=16,
+    qkv_got=16,
+    o_sent=16,
+    o_got=16,
+    g_sent=16,
+    g_got=16,
+    back_sent=16,
+    back_got=16,
+    cot_sent=8,
+    cot_got=8,
+    n1_sent=8,
+    n1_got=8,
+    n2_sent=8,
+    n2_got=8,
+    bg_sent=8,
+    bg_got=8,
+    act_sent=8,
+    act_got=8,
+    hg_sent=8,
+    hg_got=8,
+    att_sent=8,
+    att_got=8,
+    qg_sent=8,
+    qg_got=8,
+    rp_sent=4,
+    rp_got=4,
+    rf_sent=4,
+    rf_got=4,
+    ro_sent=4,
+    ro_got=4,
+    rq_sent=4,
+    rq_got=4,
+    fx_sent=8,
+    fx_got=8,
+    qx_sent=8,
+    qx_got=8,
+    s_sent=8,
+    s_got=8,
+)
+
+
+def layer_kernel(names, *refs):
+    x_ref, cot_ref, vec_ref, wq_hbm, wo_hbm, wf_hbm, wp_hbm = refs[:7]
+    y_ref, gx_ref, gqkv_ref, gout_ref, gfc_ref, gproj_ref, gvec_ref = refs[7:14]
+    s = SimpleNamespace(**dict(zip(names, refs[14:])))
+    rows, width = x_ref.shape
+    ff = s.w_fc.shape[1]
+    half = rows // 2
+    groups = s.stage.shape[0]
+    members = 2 * PLANE
+    layers = groups // PLANE
+    tokens = members * rows
+    keys = groups * half
+    chunk = ff // members
+    share = width // members
+    scaling = float(width // HEADS) ** (-0.5)
+    factor = scaling * 1.4426950408889634
+    me = lax.axis_index("ctx")
+    core = lax.axis_index("fsdp")
+    other = 1 - core
+    layer, place = me // PLANE, me % PLANE
+    member = place * 2 + core
+    twin = (me, other)
+
+    barrier = pltpu.get_barrier_semaphore()
+    for step in range(1, groups):
+        pl.semaphore_signal(
+            barrier, inc=1, device_id=((me + step) % groups, core), device_id_type=MESH
+        )
+    for step in range(PLANE):
+        pl.semaphore_signal(
+            barrier,
+            inc=1,
+            device_id=(layer * PLANE + (place + step) % PLANE, other),
+            device_id_type=MESH,
+        )
+    pl.semaphore_wait(barrier, groups - 1 + PLANE)
+
+    def at_member(index):
+        return (layer * PLANE + index // 2, index % 2)
+
+    def top_rows(ref, source):
+        count = source.shape[0]
+        return ref.at[pl.ds(pl.multiple_of(core * count, count), count)]
+
+    def peer_rows(ref, source):
+        count = source.shape[0]
+        return ref.at[pl.ds(pl.multiple_of(other * count, count), count)]
+
+    first = 2 * (1 - layer // 2)
+
+    def order(step):
+        return (step + first) % 4
+
+    pltpu.make_async_copy(wq_hbm, top_rows(s.w_qkv, wq_hbm), s.local.at[0]).start()
+
+    def qkv_piece(step, third):
+        columns = part(third * 4 + order(step), 256)
+        index = step * 3 + third
+        return remote(
+            wq_hbm.at[:, columns],
+            top_rows(s.w_qkv, wq_hbm).at[:, columns],
+            s.w_sent.at[index],
+            s.w_got.at[index],
+            twin,
+        )
+
+    vec_copy = remote(vec_ref, s.vec.at[core], s.v_sent.at[0], s.v_got.at[0], twin)
+    vec_copy.start()
+    for step in range(4):
+        for third in range(3):
+            qkv_piece(step, third).start()
+    big = ((wo_hbm, s.w_out), (wf_hbm, s.w_fc), (wp_hbm, s.w_proj))
+
+    def big_piece(index):
+        source, target = big[index]
+        return remote(
+            source, top_rows(target, source), s.w_sent.at[12 + index], s.w_got.at[12 + index], twin
+        )
+
+    def big_local(index):
+        source, target = big[index]
+        return pltpu.make_async_copy(source, top_rows(target, source), s.local.at[1 + index])
+
+    for index in range(3):
+        big_piece(index).start()
+        big_local(index).start()
+
+    def gather_copy(where, sent, got, index, slot, device):
+        return remote(where(slot), where(slot), sent.at[index], got.at[slot], device)
+
+    def gather_start(where, sent, got):
+        for step in range(1, PLANE):
+            peer = layer * PLANE + (place + step) % PLANE
+            gather_copy(where, sent, got, step, member, (peer, core)).start()
+        gather_copy(where, sent, got, 0, member, twin).start()
+
+    def gather_forward(where, sent, got):
+        for step in range(1, PLANE):
+            slot = ((place + step) % PLANE) * 2 + core
+            gather_copy(where, sent, got, 0, slot, twin).wait_recv()
+            gather_copy(where, sent, got, PLANE - 1 + step, slot, twin).start()
+
+    def gather_finish(where, sent, got):
+        for step in range(PLANE):
+            slot = ((place + step) % PLANE) * 2 + other
+            gather_copy(where, sent, got, 0, slot, twin).wait_recv()
+
+    def gather_drain(where, sent, got):
+        for index in range(2 * PLANE - 1):
+            gather_copy(where, sent, got, index, member, twin).wait_send()
+
+    def cot_at(slot):
+        return s.cot_all.at[slot]
+
+    def bg_at(slot):
+        return s.bg_all.at[slot]
+
+    def n1_at(slot):
+        return s.n1_t.at[:, part(slot, rows)]
+
+    def n2_at(slot):
+        return s.n2_t.at[:, part(slot, rows)]
+
+    def deal_copy(source, target, sent, got, index, slot):
+        return remote(source(index), target(slot), sent.at[index], got.at[slot], at_member(index))
+
+    def deal_one(source, target, sent, got, index):
+        @pl.when(index == member)
+        def _():
+            pltpu.make_async_copy(source(index), target(member), got.at[member]).start()
+
+        @pl.when(index != member)
+        def _():
+            deal_copy(source, target, sent, got, index, member).start()
+
+    def deal_start(source, target, sent, got):
+        for step in range(members):
+            if step == 0:
+                pltpu.make_async_copy(source(member), target(member), got.at[member]).start()
+            else:
+                deal_copy(source, target, sent, got, (member + step) % members, member).start()
+
+    def deal_wait(source, target, sent, got):
+        for slot in range(members):
+            pltpu.make_async_copy(source(0), target(slot), got.at[slot]).wait()
+
+    def deal_drain(source, target, sent, got):
+        for step in range(1, members):
+            deal_copy(source, target, sent, got, (member + step) % members, member).wait_send()
+
+    def swap_one(source, target, sent, got, index):
+        @pl.when(index == me)
+        def _():
+            pltpu.make_async_copy(source(index), target(me), got.at[me]).start()
+
+        @pl.when(index != me)
+        def _():
+            remote(source(index), target(me), sent.at[index], got.at[me], (index, core)).start()
+
+    def swap_wait(source, target, sent, got):
+        for slot in range(groups):
+            pltpu.make_async_copy(source(0), target(slot), got.at[slot]).wait()
+
+    def swap_drain(source, target, sent, got):
+        for step in range(1, groups):
+            peer = (me + step) % groups
+            remote(source(peer), target(me), sent.at[peer], got.at[me], (peer, core)).wait_send()
+
+    qkv_move = (
+        lambda h: s.stage.at[h],
+        lambda i: s.qkv.at[:, part(i, half)],
+        s.qkv_sent,
+        s.qkv_got,
+    )
+    o_move = (lambda h: s.o_out.at[h], lambda h: s.o_in.at[h], s.o_sent, s.o_got)
+    g_move = (lambda h: s.g_out.at[h], lambda i: s.g_in.at[part(i, half)], s.g_sent, s.g_got)
+    back_move = (lambda h: s.stage.at[h], lambda h: s.back.at[h], s.back_sent, s.back_got)
+
+    def vec_row(index):
+        return jnp.concatenate([s.vec[0, index : index + 1, :], s.vec[1, index : index + 1, :]], 1)
+
+    s.cot_all[member] = cot_ref[...]
+    gather_start(cot_at, s.cot_sent, s.cot_got)
+    s.vec[core] = vec_ref[...]
+    remote(vec_ref, s.vec.at[other], s.v_sent.at[0], s.v_got.at[0], twin).wait_recv()
+    s.row[0:1, :] = vec_row(4)
+    s.row[1:2, :] = vec_row(5)
+    inputs = x_ref[...].astype(F32)
+    normal, _ = norm_parts(inputs)
+    normed = (normal * vec_row(0) + vec_row(1)).astype(BF16)
+    s.n1[...] = normed
+    s.n1_t[:, part(member, rows)] = normed.astype(F32).T.astype(BF16)
+    gather_start(n1_at, s.n1_sent, s.n1_got)
+    pltpu.make_async_copy(wq_hbm, top_rows(s.w_qkv, wq_hbm), s.local.at[0]).wait()
+
+    for step in range(4):
+        four = order(step)
+        for third in range(3):
+            index = step * 3 + third
+            columns = part(third * 4 + four, 256)
+            remote(
+                wq_hbm.at[:, columns],
+                peer_rows(s.w_qkv, wq_hbm).at[:, columns],
+                s.w_sent.at[index],
+                s.w_got.at[index],
+                twin,
+            ).wait_recv()
+            product = dot(s.n1[...], s.w_qkv[:, columns])
+            if third == 0:
+                product = product + s.row[0:1, part(four, 256)]
+            if third == 2:
+                product = product + s.row[1:2, part(four, 256)]
+            for pair in range(2):
+                even, odd = pack_pair(product[:, pair * 128 : pair * 128 + 128])
+                s.stage[four * 4 + 2 * pair, third] = even.astype(BF16)
+                s.stage[four * 4 + 2 * pair + 1, third] = odd.astype(BF16)
+        for head in range(4):
+            swap_one(*qkv_move, four * 4 + head)
+
+    swap_wait(*qkv_move)
+    low_all = low_lanes(keys)
+    query = s.qkv[0].astype(F32)
+    s.q_low[0] = jnp.where(low_all, query, 0.0).astype(BF16)
+    s.q_low[1] = jnp.where(low_all, swap(query), 0.0).astype(BF16)
+    s.q_t[...] = query.T.astype(BF16)
+    s.kv_roll[0] = swap(s.qkv[1].astype(F32)).astype(BF16)
+    s.kv_roll[1] = swap(s.qkv[2].astype(F32)).astype(BF16)
+
+    tile = 256
+    per_tile = tile // half
+    low_tile = low_lanes(tile)
+    row_at = lax.broadcasted_iota(jnp.int32, (tile, tile), 0)
+    col_at = lax.broadcasted_iota(jnp.int32, (tile, tile), 1)
+
+    def late(index):
+        return index + (per_tile - 1 - 2 * (index // half)) * half
+
+    masks = (col_at <= row_at, late(col_at) <= late(row_at))
+
+    def key_block(region, at):
+        return s.qkv[1, at, :] if region == 0 else s.kv_roll[0, at, :]
+
+    def value_block(region, at):
+        return s.qkv[2, at, :] if region == 0 else s.kv_roll[1, at, :]
+
+    def first_tile(queries, region, at):
+        scores = jnp.where(
+            masks[region], right_transposed(queries, key_block(region, at)), NEG
+        )
+        top = jnp.max(scores, 1, keepdims=True)
+        probs = jnp.exp2((scores - top) * factor)
+        total = jnp.sum(probs, 1, keepdims=True)
+        return top, total, dot(probs.astype(BF16), value_block(region, at))
+
+    def next_tile(queries, region, at, carry):
+        top, total, mix = carry
+        scores = right_transposed(queries, key_block(region, at))
+        higher = jnp.maximum(top, jnp.max(scores, 1, keepdims=True))
+        probs = jnp.exp2((scores - higher) * factor)
+        shrink = jnp.exp2((top - higher) * factor)
+        total = total * shrink + jnp.sum(probs, 1, keepdims=True)
+        return higher, total, mix * shrink + dot(probs.astype(BF16), value_block(region, at))
+
+    n_tiles = keys // tile
+
+    def attend(index, _):
+        at = part(index, tile)
+        early_q, late_q = s.q_low[0, at, :], s.q_low[1, at, :]
+        one = lax.fori_loop(
+            0,
+            index,
+            lambda k, carry: next_tile(early_q, 0, part(k, tile), carry),
+            first_tile(early_q, 0, at),
+        )
+        two = lax.fori_loop(
+            index + 1,
+            n_tiles,
+            lambda k, carry: next_tile(late_q, 1, part(k, tile), carry),
+            first_tile(late_q, 1, at),
+        )
+        two = lax.fori_loop(
+            0, n_tiles // 2, lambda k, carry: next_tile(late_q, 0, part(k, 2 * tile), carry), two
+        )
+        s.stat[0, at, 0:1] = one[0] * factor + jnp.log2(one[1])
+        s.stat[1, at, 0:1] = two[0] * factor + jnp.log2(two[1])
+        out = jnp.where(low_tile, one[2] / one[1], swap(two[2] / two[1]))
+        s.mixed[at, :] = out
+        s.o_out[part(index, per_tile)] = out.astype(BF16).reshape(per_tile, half, 128)
+        for block in range(per_tile):
+            swap_one(*o_move, index * per_tile + block)
+        return 0
+
+    lax.fori_loop(0, n_tiles, attend, 0)
+
+    gather_forward(cot_at, s.cot_sent, s.cot_got)
+    gather_forward(n1_at, s.n1_sent, s.n1_got)
+    for index in range(3):
+        source, target = big[index]
+        remote(
+            source,
+            peer_rows(target, source),
+            s.w_sent.at[12 + index],
+            s.w_got.at[12 + index],
+            twin,
+        ).wait_recv()
+        big_local(index).wait()
+    swap_wait(*o_move)
+    for pair in range(HEADS // 2):
+        columns = slice(pair * 128, pair * 128 + 128)
+        s.att[:, columns] = unpack_pair(
+            s.o_in[2 * pair].astype(F32), s.o_in[2 * pair + 1].astype(F32)
+        ).astype(BF16)
+    turned = s.att[...].astype(F32).T.astype(BF16)
+    s.att_t[...] = turned.reshape(s.att_t.shape)
+    att_move = (
+        lambda g: s.att_t.at[:, g],
+        lambda g: s.att_all.at[:, :, part(g, rows)],
+        s.att_sent,
+        s.att_got,
+    )
+    deal_start(*att_move)
+
+    def project(index, _):
+        at = part(index, 256)
+        s.acc_d[:, at] = dot(s.att[...], s.w_out[:, at])
+        return 0
+
+    lax.fori_loop(0, width // 256, project, 0)
+    s.res[...] = x_ref[...].astype(F32) + s.acc_d[...] + vec_row(6)
+    normal, _ = norm_parts(s.res[...])
+    normed = (normal * vec_row(2) + vec_row(3)).astype(BF16)
+    s.n2[...] = normed
+    s.n2_t[:, part(member, rows)] = normed.astype(F32).T.astype(BF16)
+    gather_start(n2_at, s.n2_sent, s.n2_got)
+
+    s.acc_o[...] = jnp.zeros_like(s.acc_o)
+    s.acc_d[...] = jnp.zeros_like(s.acc_d)
+    s.sums[...] = jnp.zeros_like(s.sums)
+    hg_move = (lambda g: s.hg_out.at[g], lambda g: s.hg_all.at[g], s.hg_sent, s.hg_got)
+    curve = 0.7978845608028654
+
+    def feed(index, _):
+        at = part(index, chunk)
+        bias = s.vec.at[index // 4][pl.ds(8 + index % 4, 1), :]
+        hidden = dot(s.n2[...], s.w_fc[:, at]) + bias
+        upstream = right_transposed(cot_ref[...], s.w_proj[at, :])
+        square = hidden * hidden
+        bend = jnp.tanh(curve * hidden * (1.0 + 0.044715 * square))
+        rise = 0.5 * (1.0 + bend)
+        active = (hidden * rise).astype(BF16)
+        slope = rise + 0.5 * hidden * (1.0 - bend * bend) * (
+            curve * (1.0 + 3.0 * 0.044715 * square)
+        )
+        grad = (upstream * slope).astype(BF16)
+        s.act_t[at, :] = active.astype(F32).T.astype(BF16)
+        s.hg_out[index] = grad
+        deal_one(*hg_move, index)
+        s.acc_o[...] += dot(active, s.w_proj[at, :])
+        s.acc_d[...] += right_transposed(grad, s.w_fc[:, at])
+        s.sums[pl.ds(8 + index // 2, 1), pl.ds(pl.multiple_of(index % 2 * chunk, chunk), chunk)] = (
+            jnp.sum(grad.astype(F32), 0, keepdims=True)
+        )
+        return 0
+
+    lax.fori_loop(0, members, feed, 0)
+    act_view = s.act_t.reshape(layers, members, ff // members // layers, rows)
+    act_move = (
+        lambda g: act_view.at[:, g],
+        lambda g: s.act_all.at[:, :, part(g, rows)],
+        s.act_sent,
+        s.act_got,
+    )
+    deal_start(*act_move)
+    upstream = cot_ref[...].astype(F32)
+    normal, inverse = norm_parts(s.res[...])
+    step_grad, gain_grad, shift_grad = norm_grads(s.acc_d[...], normal, inverse, vec_row(2))
+    s.sums[2:3, :] = gain_grad[None]
+    s.sums[3:4, :] = shift_grad[None]
+    s.sums[7:8, :] = jnp.sum(upstream, 0, keepdims=True)
+    res_grad = upstream + step_grad
+    s.res_grad[...] = res_grad
+    branch = res_grad.astype(BF16)
+    s.bg_all[member] = branch
+    s.sums[6:7, :] = jnp.sum(branch.astype(F32), 0, keepdims=True)
+    for step in range(4):
+        four = order(step)
+        product = right_transposed(s.bg_all[member], s.w_out[part(four, 256), :])
+        for pair in range(2):
+            even, odd = pack_pair(product[:, pair * 128 : pair * 128 + 128])
+            s.g_out[four * 4 + 2 * pair] = even.astype(BF16)
+            s.g_out[four * 4 + 2 * pair + 1] = odd.astype(BF16)
+        for head in range(4):
+            swap_one(*g_move, four * 4 + head)
+    gather_start(bg_at, s.bg_sent, s.bg_got)
+    y_ref[...] = (s.res[...] + s.acc_o[...] + vec_row(7)).astype(BF16)
+    swap_drain(*qkv_move)
+
+    swap_wait(*g_move)
+    upstream = s.g_in[...].astype(F32)
+    s.g_low[0] = jnp.where(low_all, upstream, 0.0).astype(BF16)
+    s.g_low[1] = jnp.where(low_all, swap(upstream), 0.0).astype(BF16)
+    s.g_t[...] = upstream.T.astype(BF16)
+    inner = upstream * s.mixed[...]
+    s.stat[0, :, 1:2] = jnp.sum(jnp.where(low_all, inner, 0.0), 1, keepdims=True)
+    s.stat[1, :, 1:2] = jnp.sum(jnp.where(low_all, 0.0, inner), 1, keepdims=True)
+    s.dk_t[...] = jnp.zeros_like(s.dk_t)
+    s.dv_t[...] = jnp.zeros_like(s.dv_t)
+
+    def back_tile(side, region, at_q, at_k, masked, total):
+        scores = right_transposed(s.q_low[side, at_q, :], key_block(region, at_k))
+        probs = jnp.exp2(scores * factor - s.stat[side, at_q, 0:1])
+        if masked:
+            probs = jnp.where(masks[region], probs, 0.0)
+        prob_grad = right_transposed(s.g_low[side, at_q, :], value_block(region, at_k))
+        score_grad = (probs * (prob_grad - s.stat[side, at_q, 1:2])).astype(BF16)
+        head = slice(side * 64, side * 64 + 64)
+        into = slice(region * 64, region * 64 + 64)
+        s.dk_t[into, at_k] += dot(s.q_t[head, at_q], score_grad)
+        s.dv_t[into, at_k] += dot(s.g_t[head, at_q], probs.astype(BF16))
+        more = dot(score_grad, key_block(region, at_k))
+        return more if total is None else total + more
+
+    def attend_back(index, _):
+        at = part(index, tile)
+        one = lax.fori_loop(
+            0,
+            index,
+            lambda k, total: back_tile(0, 0, at, part(k, tile), False, total),
+            back_tile(0, 0, at, at, True, None),
+        )
+        two = lax.fori_loop(
+            index + 1,
+            n_tiles,
+            lambda k, total: back_tile(1, 1, at, part(k, tile), False, total),
+            back_tile(1, 1, at, at, True, None),
+        )
+        two = lax.fori_loop(
+            0,
+            n_tiles // 2,
+            lambda k, total: back_tile(1, 0, at, part(k, 2 * tile), False, total),
+            two,
+        )
+        out = (jnp.where(low_tile, one, swap(two)) * scaling).astype(BF16)
+        s.stage[part(index, per_tile), 0] = out.reshape(per_tile, half, 128)
+        return 0
+
+    lax.fori_loop(0, n_tiles, attend_back, 0)
+    s.stage[:, 1] = (s.dk_t[...].T * scaling).astype(BF16).reshape(groups, half, 128)
+    s.stage[:, 2] = s.dv_t[...].T.astype(BF16).reshape(groups, half, 128)
+    for step in range(4):
+        for head in range(4):
+            swap_one(*back_move, order(step) * 4 + head)
+
+    def spread_copy(buffer_out, buffer_in, sent, got, index, slot):
+        return remote(
+            buffer_out(index),
+            buffer_in(slot),
+            sent.at[index],
+            got.at[slot],
+            (index * PLANE + place, core),
+        )
+
+    def spread(move, product, own_ref):
+        buffer_out, buffer_in, sent, got = move
+
+        def each(index, _):
+            value = product(index)
+            buffer_out(index)[...] = value.astype(BF16)
+
+            @pl.when(index == layer)
+            def _():
+                own_ref[...] = value
+
+            @pl.when(index != layer)
+            def _():
+                spread_copy(*move, index, layer).start()
+
+            return 0
+
+        lax.fori_loop(0, layers, each, 0)
+
+    def collect(move, own_ref):
+        buffer_out, buffer_in, sent, got = move
+        for step in range(1, layers):
+            slot = (layer + step) % layers
+            spread_copy(*move, slot, slot).wait_recv()
+            own_ref[...] += buffer_in(slot)[...].astype(F32)
+
+    def spread_drain(move):
+        for step in range(1, layers):
+            spread_copy(*move, (layer + step) % layers, layer).wait_send()
+
+    proj_rows = ff // members // layers
+    out_rows = share // layers
+    fc_rows = width // layers
+
+    def rows_of(ref, start, count, columns=slice(None)):
+        return lambda i: ref.at[pl.ds(pl.multiple_of(start + i * count, count), count), columns]
+
+    sum_proj = (
+        rows_of(s.w_proj, 0, proj_rows),
+        rows_of(s.w_proj, 512, proj_rows),
+        s.rp_sent,
+        s.rp_got,
+    )
+    sum_out = (
+        rows_of(s.w_proj, 1024, out_rows),
+        rows_of(s.w_proj, 1152, out_rows),
+        s.ro_sent,
+        s.ro_got,
+    )
+    sum_fc = (
+        rows_of(s.w_fc, 0, fc_rows, pl.ds(0, chunk)),
+        rows_of(s.w_fc, 0, fc_rows, pl.ds(chunk, chunk)),
+        s.rf_sent,
+        s.rf_got,
+    )
+    sum_qkv = (
+        rows_of(s.w_fc, 0, fc_rows, pl.ds(2 * chunk, 3 * share)),
+        rows_of(s.w_fc, 0, fc_rows, pl.ds(3 * chunk, 3 * share)),
+        s.rq_sent,
+        s.rq_got,
+    )
+    gather_forward(n2_at, s.n2_sent, s.n2_got)
+    gather_forward(bg_at, s.bg_sent, s.bg_got)
+    gather_finish(cot_at, s.cot_sent, s.cot_got)
+    deal_wait(*act_move)
+    spread(
+        sum_proj,
+        lambda i: dot(s.act_all[i], s.cot_all[...].reshape(tokens, width)),
+        gproj_ref,
+    )
+    gather_finish(n2_at, s.n2_sent, s.n2_got)
+    deal_wait(*hg_move)
+    spread(
+        sum_fc,
+        lambda i: dot(s.n2_t[part(i, fc_rows), :], s.hg_all[...].reshape(tokens, chunk)),
+        s.fc_own,
+    )
+    gather_finish(bg_at, s.bg_sent, s.bg_got)
+    deal_wait(*att_move)
+    spread(
+        sum_out,
+        lambda i: dot(s.att_all[i], s.bg_all[...].reshape(tokens, width)),
+        gout_ref,
+    )
+
+    swap_wait(*back_move)
+    for pair in range(HEADS // 2):
+        for third in range(3):
+            block = unpack_pair(
+                s.back[2 * pair, third].astype(F32), s.back[2 * pair + 1, third].astype(F32)
+            ).astype(BF16)
+            s.qg_out[pair, :, third * 128 : third * 128 + 128] = block
+            columns = slice(third * width + pair * 128, third * width + pair * 128 + 128)
+            s.qg[:, columns] = block
+    qg_move = (lambda g: s.qg_out.at[g], lambda g: s.qg_all.at[g], s.qg_sent, s.qg_got)
+    deal_start(*qg_move)
+    s.sums[4:5, :] = jnp.sum(s.qg[:, :width].astype(F32), 0, keepdims=True)
+    s.sums[5:6, :] = jnp.sum(s.qg[:, 2 * width :].astype(F32), 0, keepdims=True)
+
+    def project_back(index, _):
+        s.acc_d[:, part(index, 256)] = right_transposed(s.qg[...], s.w_qkv[part(index, 256), :])
+        return 0
+
+    lax.fori_loop(0, width // 256, project_back, 0)
+    normal, inverse = norm_parts(x_ref[...].astype(F32))
+    step_grad, gain_grad, shift_grad = norm_grads(s.acc_d[...], normal, inverse, vec_row(0))
+    s.sums[0:1, :] = gain_grad[None]
+    s.sums[1:2, :] = shift_grad[None]
+    gx_ref[...] = s.res_grad[...] + step_grad
+
+    def sum_copy(index, slot, device):
+        return remote(s.sums, s.sums_in.at[slot], s.s_sent.at[index], s.s_got.at[slot], device)
+
+    sum_copy(0, 0, twin).start()
+
+    gather_finish(n1_at, s.n1_sent, s.n1_got)
+    deal_wait(*qg_move)
+    spread(
+        sum_qkv,
+        lambda i: dot(s.n1_t[part(i, fc_rows), :], s.qg_all[...].reshape(tokens, 3 * share)),
+        s.qkv_own,
+    )
+    sum_copy(0, 0, twin).wait()
+    s.sums[...] += s.sums_in[0]
+    for step in range(1, PLANE):
+        sum_copy(step, step, (layer * PLANE + (place + step) % PLANE, core)).start()
+
+    fx_move = (lambda g: s.fc_x.at[g], lambda g: s.fc_y.at[g], s.fx_sent, s.fx_got)
+    qx_move = (lambda g: s.qkv_x.at[g], lambda g: s.qkv_y.at[g], s.qx_sent, s.qx_got)
+    collect(sum_fc, s.fc_own)
+    s.fc_x[...] = s.fc_own[...].astype(BF16).reshape(s.fc_x.shape)
+    deal_start(*fx_move)
+    for step in range(1, PLANE):
+        sum_copy(step, step, twin).wait()
+    s.sums[...] += s.sums_in[1] + s.sums_in[2] + s.sums_in[3]
+    for step in range(1, layers):
+        peer = ((layer + step) % layers) * PLANE + place
+        sum_copy(3 + step, 3 + step, (peer, core)).start()
+    collect(sum_proj, gproj_ref)
+    collect(sum_out, gout_ref)
+    collect(sum_qkv, s.qkv_own)
+    s.qkv_x[...] = s.qkv_own[...].astype(BF16).reshape(s.qkv_x.shape)
+    deal_start(*qx_move)
+    for step in range(1, layers):
+        sum_copy(3 + step, 3 + step, twin).wait()
+    s.sums[...] += s.sums_in[4] + s.sums_in[5] + s.sums_in[6]
+    owner = me * 2 + core
+    gvec_ref[...] = jnp.zeros_like(gvec_ref)
+    block = s.sums[0:8, part(owner // 4, 128)]
+    gvec_ref[0:8, :] = pltpu.roll(block, (128 - (owner % 4) * 32) % 128, 1)
+    block = s.sums[8:16, part(owner % 8, 128)]
+    chosen = lax.broadcasted_iota(jnp.int32, block.shape, 0) == owner // 8
+    gvec_ref[8:9, :] = jnp.sum(jnp.where(chosen, block, 0.0), 0, keepdims=True)
+    deal_wait(*fx_move)
+    for slot in range(members):
+        gfc_ref[:, slot * chunk : slot * chunk + chunk] = s.fc_y[slot].astype(F32)
+    deal_wait(*qx_move)
+    for slot in range(members):
+        for third in range(3):
+            start = third * width + slot * 128
+            gqkv_ref[:, start : start + 128] = s.qkv_y[
+                slot, :, third * 128 : third * 128 + 128
+            ].astype(F32)
+
+    for step in range(4):
+        for third in range(3):
+            qkv_piece(step, third).wait_send()
+    for index in range(3):
+        big_piece(index).wait_send()
+    vec_copy.wait_send()
+    for move in (o_move, g_move, back_move):
+        swap_drain(*move)
+    for move in (att_move, hg_move, act_move, qg_move, fx_move, qx_move):
+        deal_drain(*move)
+    for where, sent, got in (
+        (cot_at, s.cot_sent, s.cot_got),
+        (n1_at, s.n1_sent, s.n1_got),
+        (n2_at, s.n2_sent, s.n2_got),
+        (bg_at, s.bg_sent, s.bg_got),
+    ):
+        gather_drain(where, sent, got)
+    for move in (sum_proj, sum_fc, sum_out, sum_qkv):
+        spread_drain(move)
+
+
+def fused_layer(
+    block_input,
+    w_qkv,
+    w_out,
+    w_fc,
+    w_proj,
+    ln1_gain,
+    ln1_bias,
+    ln2_gain,
+    ln2_bias,
+    bias_q,
+    bias_v,
+    bias_out,
+    bias_fc,
+    bias_proj,
+    cotangent,
+):
+    width = block_input.shape[4]
+    rows = 2 * block_input.shape[3]
+    ff = w_fc.shape[1]
+    groups = lax.axis_size("ctx")
+    shards = 2 * groups
+    small = (ln1_gain, ln1_bias, ln2_gain, ln2_bias, bias_q, bias_v, bias_out, bias_proj, bias_fc)
+    vectors = jnp.concatenate(small).astype(F32).reshape(-1, width // 2)
+    vectors = jnp.pad(vectors, ((0, 16 - vectors.shape[0]), (0, 0)))
+    shapes = layer_shapes(rows, width, ff, groups)
+    names = tuple(shapes) + tuple(SEMAPHORES)
+    scratch = [pltpu.VMEM(shape, kind) for shape, kind in shapes.values()]
+    scratch += [pltpu.SemaphoreType.DMA((count,)) for count in SEMAPHORES.values()]
+    in_vmem = pl.BlockSpec(memory_space=pltpu.VMEM)
+    in_hbm = pl.BlockSpec(memory_space=pl.ANY)
+    outs = pl.pallas_call(
+        partial(layer_kernel, names),
+        out_shape=(
+            jax.ShapeDtypeStruct((rows, width), BF16),
+            jax.ShapeDtypeStruct((rows, width), F32),
+            jax.ShapeDtypeStruct((width // shards, 3 * width), F32),
+            jax.ShapeDtypeStruct((width // shards, width), F32),
+            jax.ShapeDtypeStruct((width // shards, ff), F32),
+            jax.ShapeDtypeStruct((ff // shards, width), F32),
+            jax.ShapeDtypeStruct((16, 128), F32),
+        ),
+        in_specs=[in_vmem] * 3 + [in_hbm] * 4,
+        out_specs=(in_vmem,) * 7,
+        scratch_shapes=scratch,
+        compiler_params=pltpu.CompilerParams(
+            collective_id=0, has_side_effects=True, vmem_limit_bytes=VMEM_BYTES
+        ),
+        cost_estimate=pl.CostEstimate(
+            flops=14 * 10**9, bytes_accessed=30 * 10**6, transcendentals=5 * 10**6
+        ),
+    )(
+        block_input.reshape(rows, width),
+        cotangent.reshape(rows, width),
+        vectors,
+        w_qkv,
+        w_out,
+        w_fc,
+        w_proj,
+    )
+    block_output, input_grad, grad_qkv, grad_out, grad_fc, grad_proj, sums = outs
+    piece = width // shards
+    return (
+        block_output.reshape(block_input.shape),
+        input_grad.reshape(block_input.shape),
+        grad_qkv,
+        grad_out,
+        grad_fc,
+        grad_proj,
+        sums[0, :piece],
+        sums[1, :piece],
+        sums[2, :piece],
+        sums[3, :piece],
+        sums[4, :piece],
+        sums[5, :piece],
+        sums[6, :piece],
+        sums[8, : ff // shards],
+        sums[7, :piece],
+    )
+
+
+def on_device(*arrays):
+    width, ff = arrays[0].shape[4], arrays[3].shape[1]
+    fits = (
+        lax.axis_size("ctx") == HEADS
+        and lax.axis_size("fsdp") == 2
+        and arrays[0].shape[:4] == (1, 1, 2, 64)
+        and (width, ff) == (1024, 4096)
+    )
+    return fused_layer(*arrays) if fits else general_layer(*arrays)
+
+
 def solution(mesh):
     placed = (
         P("fsdp", "ctx", None, None, None),

time: 1340 us -> 232 us (0.17)
  waiting for transfers between devices: 1100 us -> 0 us
  Pallas kernels: 0 us -> 209 us
  matrix products: 109 us -> 0 us
  blocking collectives: 62.1 us -> 0 us
  other arithmetic: 28.2 us -> 0.62 us
  between operations: 14.9 us -> 0.67 us
    reduce_scatter x5 -> x0, waiting for transfers between devices: 926 us -> none  [the longest x1 317 us: on_device(): lax.psum_scatter(key_terms(jnp.int32(0), lax.axis_size('ctx') * seq_rows)...]
    pallas_call x0 -> x1, Pallas kernels: none -> 209 us  [fused_layer(): pl.pallas_call(partial(layer_kernel, names), out_shape=(jax.ShapeDtypeStr...]
    all_gather x6 -> x0, waiting for transfers between devices: 166 us -> none  [the longest x1 73.1 us: on_device(): key_all = lax.all_gather(keys, 'ctx', axis=0, tiled=True)]
    dot_general x18 -> x0, matrix products: 109 us -> none  [the longest x4 27.5 us: rows_product(): lax.dot_general(left, right, (((0,), (0,)), ((), ())), preferred_element_...]
    unnamed x1 -> x0, blocking collectives: 45.9 us -> none
    all_gather x9 -> x0, blocking collectives: 16.2 us -> none  [the longest x1 1.93 us: on_device(): lax.all_gather(ln1_gain, 'fsdp', axis=0, tiled=True)]
  transfers between devices with their start and end apart: 11 -> 0, of which waited for: 10 -> 0; matrix products, arithmetic and copies ran while one was open for 8% -> 0% of each run, Pallas kernels for 0% -> 0%
where the time goes in v2:
time: 232 us; the launch traced here: 231 us
  Pallas kernels  209 us (90%)
  local copies, waits for them, and re-layouts  20.9 us (9%)
    pallas_call x1, Pallas kernels, fused_layer(): pl.pallas_call(partial(layer_kernel, names), out_shape=(jax.ShapeDtypeStr...  209 us
    unnamed x14, local copies, waits for them, and re-layouts  17.5 us

profile of v2, /device:TPU:0, one launch (start us, length us, event | category | flops | bytes accessed | tf_op | source)
XLA Modules:
  0.0 230.8 jit_solution(11362222045501846378)
XLA Ops:
  0.7 0.9 dynamic-update-slice
  1.5 0.9 dynamic-update-slice.1
  2.4 0.9 dynamic-update-slice.2
  3.2 0.9 dynamic-update-slice.3
  4.1 0.9 dynamic-update-slice.4
  5.0 0.9 dynamic-update-slice.5
  5.8 0.9 dynamic-update-slice.6
  6.7 0.9 dynamic-update-slice.7
  7.5 0.7 constant_dynamic-update-slice_fusion
  8.2 0.6 pad_convert_fusion.refs_2_
  8.9 208.5 %shard_map.262 = (bf16[128,1024]{1,0:T(8,128)(2,1)}, f32[128,1024]{1,0:T(8,128)}, f32[32,3072]{1,0:T(8,128)}, f32[32,1024]{1,0:T(8,128)}, f32[32,4096]{1,0:T(8,1...) custom-call(bf16[128,1024]{1,0:T(8,128)(2,1)} %bitcast.24, bf16[128,1024]{1,0:T(8,128)(2,1)} %bitcast.25, ...), custom_call_target="tpu_custom_call" | custom-call | flops 14000000000 | bytes 30000000 | tf_op jit(solution)/shard_map/pallas_call | solution.py:1116
  217.4 1.5 slice_bitcast_fusion
  218.9 1.2 slice_bitcast_fusion.1
  220.1 1.7 copy.45
  221.8 1.9 copy.46
  223.7 1.8 copy.47
  225.5 1.6 copy.48
  227.0 1.9 copy.49
  228.9 1.9 copy.50
  (2 shorter events, 0.0 us)

commit v3 on v2

--- a/solution.py
+++ b/solution.py
@@ -339,6 +339,7 @@
         w_out=((width, width), BF16),
         w_fc=((width, ff), BF16),
         w_proj=((ff, width), BF16),
+        vec_low=((2, 16, width // 2), BF16),
         vec=((2, 16, width // 2), F32),
         row=((8, width), F32),
         cot_all=((members, rows, width), BF16),
@@ -361,7 +362,7 @@
         res=((rows, width), F32),
         n2=((rows, width), BF16),
         n2_t=((width, tokens), BF16),
-        act_t=((ff, rows), BF16),
+        act_t=((members, layers, ff // members // layers, rows), BF16),
         act_all=((layers, ff // members // layers, tokens), BF16),
         hg_out=((members, rows, ff // members), BF16),
         hg_all=((members, rows, ff // members), BF16),
@@ -501,7 +502,7 @@
             twin,
         )
 
-    vec_copy = remote(vec_ref, s.vec.at[core], s.v_sent.at[0], s.v_got.at[0], twin)
+    vec_copy = remote(vec_ref, s.vec_low.at[core], s.v_sent.at[0], s.v_got.at[0], twin)
     vec_copy.start()
     for step in range(4):
         for third in range(3):
@@ -618,16 +619,21 @@
 
     s.cot_all[member] = cot_ref[...]
     gather_start(cot_at, s.cot_sent, s.cot_got)
-    s.vec[core] = vec_ref[...]
-    remote(vec_ref, s.vec.at[other], s.v_sent.at[0], s.v_got.at[0], twin).wait_recv()
+    remote(vec_ref, s.vec_low.at[other], s.v_sent.at[0], s.v_got.at[0], twin).wait_recv()
+    s.vec[core] = vec_ref[...].astype(F32)
+    s.vec[other] = s.vec_low[other].astype(F32)
     s.row[0:1, :] = vec_row(4)
     s.row[1:2, :] = vec_row(5)
+    for quarter in range(4):
+        at = 8 + quarter % 2 * 2
+        s.row[4 + quarter : 5 + quarter, :] = jnp.concatenate(
+            [s.vec[quarter // 2, at : at + 1, :], s.vec[quarter // 2, at + 1 : at + 2, :]], 1
+        )
     inputs = x_ref[...].astype(F32)
     normal, _ = norm_parts(inputs)
     normed = (normal * vec_row(0) + vec_row(1)).astype(BF16)
     s.n1[...] = normed
     s.n1_t[:, part(member, rows)] = normed.astype(F32).T.astype(BF16)
-    gather_start(n1_at, s.n1_sent, s.n1_got)
     pltpu.make_async_copy(wq_hbm, top_rows(s.w_qkv, wq_hbm), s.local.at[0]).wait()
 
     for step in range(4):
@@ -655,6 +661,7 @@
             swap_one(*qkv_move, four * 4 + head)
 
     swap_wait(*qkv_move)
+    gather_start(n1_at, s.n1_sent, s.n1_got)
     low_all = low_lanes(keys)
     query = s.qkv[0].astype(F32)
     s.q_low[0] = jnp.where(low_all, query, 0.0).astype(BF16)
@@ -729,8 +736,6 @@
 
     lax.fori_loop(0, n_tiles, attend, 0)
 
-    gather_forward(cot_at, s.cot_sent, s.cot_got)
-    gather_forward(n1_at, s.n1_sent, s.n1_got)
     for index in range(3):
         source, target = big[index]
         remote(
@@ -755,8 +760,6 @@
         s.att_sent,
         s.att_got,
     )
-    deal_start(*att_move)
-
     def project(index, _):
         at = part(index, 256)
         s.acc_d[:, at] = dot(s.att[...], s.w_out[:, at])
@@ -768,19 +771,31 @@
     normed = (normal * vec_row(2) + vec_row(3)).astype(BF16)
     s.n2[...] = normed
     s.n2_t[:, part(member, rows)] = normed.astype(F32).T.astype(BF16)
-    gather_start(n2_at, s.n2_sent, s.n2_got)
-
     s.acc_o[...] = jnp.zeros_like(s.acc_o)
     s.acc_d[...] = jnp.zeros_like(s.acc_d)
     s.sums[...] = jnp.zeros_like(s.sums)
     hg_move = (lambda g: s.hg_out.at[g], lambda g: s.hg_all.at[g], s.hg_sent, s.hg_got)
     curve = 0.7978845608028654
 
-    def feed(index, _):
-        at = part(index, chunk)
-        bias = s.vec.at[index // 4][pl.ds(8 + index % 4, 1), :]
-        hidden = dot(s.n2[...], s.w_fc[:, at]) + bias
-        upstream = right_transposed(cot_ref[...], s.w_proj[at, :])
+    act_move = (
+        lambda g: s.act_t.at[g],
+        lambda g: s.act_all.at[:, :, part(g, rows)],
+        s.act_sent,
+        s.act_got,
+    )
+    quarters = ff // width
+    piece = width // members
+
+    def feed(step, _):
+        index = (member + 1 + step) % members
+        places = [part(quarter * members + index, piece) for quarter in range(quarters)]
+        bias = jnp.concatenate(
+            [s.row[4 + quarter : 5 + quarter, part(index, piece)] for quarter in range(quarters)], 1
+        )
+        into = jnp.concatenate([s.w_fc[:, at] for at in places], 1)
+        back = jnp.concatenate([s.w_proj[at, :] for at in places], 0)
+        hidden = dot(s.n2[...], into) + bias
+        upstream = right_transposed(cot_ref[...], back)
         square = hidden * hidden
         bend = jnp.tanh(curve * hidden * (1.0 + 0.044715 * square))
         rise = 0.5 * (1.0 + bend)
@@ -789,25 +804,19 @@
             curve * (1.0 + 3.0 * 0.044715 * square)
         )
         grad = (upstream * slope).astype(BF16)
-        s.act_t[at, :] = active.astype(F32).T.astype(BF16)
+        s.act_t[index] = active.astype(F32).T.astype(BF16).reshape(s.act_t.shape[1:])
+        deal_one(*act_move, index)
         s.hg_out[index] = grad
-        deal_one(*hg_move, index)
-        s.acc_o[...] += dot(active, s.w_proj[at, :])
-        s.acc_d[...] += right_transposed(grad, s.w_fc[:, at])
-        s.sums[pl.ds(8 + index // 2, 1), pl.ds(pl.multiple_of(index % 2 * chunk, chunk), chunk)] = (
-            jnp.sum(grad.astype(F32), 0, keepdims=True)
-        )
+        s.acc_o[...] += dot(active, back)
+        s.acc_d[...] += right_transposed(grad, into)
+        total = jnp.sum(grad.astype(F32), 0, keepdims=True)
+        for quarter in range(quarters):
+            s.sums[8 + quarter : 9 + quarter, part(index, piece)] = total[
+                :, quarter * piece : quarter * piece + piece
+            ]
         return 0
 
     lax.fori_loop(0, members, feed, 0)
-    act_view = s.act_t.reshape(layers, members, ff // members // layers, rows)
-    act_move = (
-        lambda g: act_view.at[:, g],
-        lambda g: s.act_all.at[:, :, part(g, rows)],
-        s.act_sent,
-        s.act_got,
-    )
-    deal_start(*act_move)
     upstream = cot_ref[...].astype(F32)
     normal, inverse = norm_parts(s.res[...])
     step_grad, gain_grad, shift_grad = norm_grads(s.acc_d[...], normal, inverse, vec_row(2))
@@ -828,9 +837,107 @@
             s.g_out[four * 4 + 2 * pair + 1] = odd.astype(BF16)
         for head in range(4):
             swap_one(*g_move, four * 4 + head)
-    gather_start(bg_at, s.bg_sent, s.bg_got)
+    deal_start(*hg_move)
+    gather_start(n2_at, s.n2_sent, s.n2_got)
     y_ref[...] = (s.res[...] + s.acc_o[...] + vec_row(7)).astype(BF16)
+    gather_forward(cot_at, s.cot_sent, s.cot_got)
+    gather_forward(n1_at, s.n1_sent, s.n1_got)
     swap_drain(*qkv_move)
+
+    beside = layer + 1 - 2 * (layer % 2)
+    beyond = (layer + 2) % layers
+    across = (beside + 2) % layers
+
+    def spread_copy(move, slot, target):
+        buffer_out, buffer_in, sent, got = move
+        return remote(
+            buffer_out(slot),
+            buffer_in(slot),
+            sent.at[slot],
+            got.at[slot],
+            (target * PLANE + place, core),
+        )
+
+    def spread(move, product, own_ref):
+        for slot, index in enumerate((beside, across, beyond)):
+            move[0](slot)[...] = product(index).astype(BF16)
+            if slot < 2:
+                spread_copy(move, slot, beside).start()
+        own_ref[...] = product(layer)
+
+    def spread_on(move):
+        spread_copy(move, 1, beside).wait_recv()
+        pair = move[0](2)[...].astype(F32) + move[1](1)[...].astype(F32)
+        move[0](2)[...] = pair.astype(BF16)
+        spread_copy(move, 2, beyond).start()
+
+    def collect(move, own_ref):
+        for slot in (0, 2):
+            spread_copy(move, slot, beside).wait_recv()
+        own_ref[...] += move[1](0)[...].astype(F32) + move[1](2)[...].astype(F32)
+
+    def spread_drain(move):
+        for slot in range(3):
+            spread_copy(move, slot, beside).wait_send()
+
+    proj_rows = ff // members // layers
+    out_rows = share // layers
+    fc_rows = width // layers
+
+    def rows_of(ref, start, count, columns=slice(None)):
+        return lambda i: ref.at[pl.ds(pl.multiple_of(start + i * count, count), count), columns]
+
+    sum_proj = (
+        rows_of(s.w_proj, 0, proj_rows),
+        rows_of(s.w_proj, 512, proj_rows),
+        s.rp_sent,
+        s.rp_got,
+    )
+    sum_out = (
+        rows_of(s.w_proj, 1024, out_rows),
+        rows_of(s.w_proj, 1152, out_rows),
+        s.ro_sent,
+        s.ro_got,
+    )
+    sum_fc = (
+        rows_of(s.w_fc, 0, fc_rows, pl.ds(0, chunk)),
+        rows_of(s.w_fc, 0, fc_rows, pl.ds(chunk, chunk)),
+        s.rf_sent,
+        s.rf_got,
+    )
+    sum_qkv = (
+        rows_of(s.w_fc, 0, fc_rows, pl.ds(2 * chunk, 3 * share)),
+        rows_of(s.w_fc, 0, fc_rows, pl.ds(3 * chunk, 3 * share)),
+        s.rq_sent,
+        s.rq_got,
+    )
+    def grad_of_proj():
+        gather_finish(cot_at, s.cot_sent, s.cot_got)
+        deal_wait(*act_move)
+        spread(
+            sum_proj,
+            lambda i: dot(s.act_all[i], s.cot_all[...].reshape(tokens, width)),
+            gproj_ref,
+        )
+
+    def grad_of_fc():
+        gather_forward(n2_at, s.n2_sent, s.n2_got)
+        gather_finish(n2_at, s.n2_sent, s.n2_got)
+        deal_wait(*hg_move)
+        spread(
+            sum_fc,
+            lambda i: dot(s.n2_t[part(i, fc_rows), :], s.hg_all[...].reshape(tokens, chunk)),
+            s.fc_own,
+        )
+
+    def grad_of_out():
+        gather_finish(bg_at, s.bg_sent, s.bg_got)
+        deal_wait(*att_move)
+        spread(
+            sum_out,
+            lambda i: dot(s.att_all[i], s.bg_all[...].reshape(tokens, width)),
+            gout_ref,
+        )
 
     swap_wait(*g_move)
     upstream = s.g_in[...].astype(F32)
@@ -881,108 +988,26 @@
         s.stage[part(index, per_tile), 0] = out.reshape(per_tile, half, 128)
         return 0
 
-    lax.fori_loop(0, n_tiles, attend_back, 0)
+    attend_back(0, 0)
+    grad_of_proj()
+    attend_back(1, 0)
+    attend_back(2, 0)
+    spread_on(sum_proj)
+    gather_start(bg_at, s.bg_sent, s.bg_got)
+    deal_start(*att_move)
+    attend_back(3, 0)
     s.stage[:, 1] = (s.dk_t[...].T * scaling).astype(BF16).reshape(groups, half, 128)
     s.stage[:, 2] = s.dv_t[...].T.astype(BF16).reshape(groups, half, 128)
     for step in range(4):
         for head in range(4):
             swap_one(*back_move, order(step) * 4 + head)
-
-    def spread_copy(buffer_out, buffer_in, sent, got, index, slot):
-        return remote(
-            buffer_out(index),
-            buffer_in(slot),
-            sent.at[index],
-            got.at[slot],
-            (index * PLANE + place, core),
-        )
-
-    def spread(move, product, own_ref):
-        buffer_out, buffer_in, sent, got = move
-
-        def each(index, _):
-            value = product(index)
-            buffer_out(index)[...] = value.astype(BF16)
-
-            @pl.when(index == layer)
-            def _():
-                own_ref[...] = value
-
-            @pl.when(index != layer)
-            def _():
-                spread_copy(*move, index, layer).start()
-
-            return 0
-
-        lax.fori_loop(0, layers, each, 0)
-
-    def collect(move, own_ref):
-        buffer_out, buffer_in, sent, got = move
-        for step in range(1, layers):
-            slot = (layer + step) % layers
-            spread_copy(*move, slot, slot).wait_recv()
-            own_ref[...] += buffer_in(slot)[...].astype(F32)
-
-    def spread_drain(move):
-        for step in range(1, layers):
-            spread_copy(*move, (layer + step) % layers, layer).wait_send()
-
-    proj_rows = ff // members // layers
-    out_rows = share // layers
-    fc_rows = width // layers
-
-    def rows_of(ref, start, count, columns=slice(None)):
-        return lambda i: ref.at[pl.ds(pl.multiple_of(start + i * count, count), count), columns]
-
-    sum_proj = (
-        rows_of(s.w_proj, 0, proj_rows),
-        rows_of(s.w_proj, 512, proj_rows),
-        s.rp_sent,
-        s.rp_got,
-    )
-    sum_out = (
-        rows_of(s.w_proj, 1024, out_rows),
-        rows_of(s.w_proj, 1152, out_rows),
-        s.ro_sent,
-        s.ro_got,
-    )
-    sum_fc = (
-        rows_of(s.w_fc, 0, fc_rows, pl.ds(0, chunk)),
-        rows_of(s.w_fc, 0, fc_rows, pl.ds(chunk, chunk)),
-        s.rf_sent,
-        s.rf_got,
-    )
-    sum_qkv = (
-        rows_of(s.w_fc, 0, fc_rows, pl.ds(2 * chunk, 3 * share)),
-        rows_of(s.w_fc, 0, fc_rows, pl.ds(3 * chunk, 3 * share)),
-        s.rq_sent,
-        s.rq_got,
-    )
-    gather_forward(n2_at, s.n2_sent, s.n2_got)
+    grad_of_fc()
     gather_forward(bg_at, s.bg_sent, s.bg_got)
-    gather_finish(cot_at, s.cot_sent, s.cot_got)
-    deal_wait(*act_move)
-    spread(
-        sum_proj,
-        lambda i: dot(s.act_all[i], s.cot_all[...].reshape(tokens, width)),
-        gproj_ref,
-    )
-    gather_finish(n2_at, s.n2_sent, s.n2_got)
-    deal_wait(*hg_move)
-    spread(
-        sum_fc,
-        lambda i: dot(s.n2_t[part(i, fc_rows), :], s.hg_all[...].reshape(tokens, chunk)),
-        s.fc_own,
-    )
-    gather_finish(bg_at, s.bg_sent, s.bg_got)
-    deal_wait(*att_move)
-    spread(
-        sum_out,
-        lambda i: dot(s.att_all[i], s.bg_all[...].reshape(tokens, width)),
-        gout_ref,
-    )
+    grad_of_out()
+    spread_on(sum_fc)
 
     swap_wait(*back_move)
+    spread_on(sum_out)
     for pair in range(HEADS // 2):
         for third in range(3):
             block = unpack_pair(
@@ -1037,6 +1062,7 @@
         sum_copy(3 + step, 3 + step, (peer, core)).start()
     collect(sum_proj, gproj_ref)
     collect(sum_out, gout_ref)
+    spread_on(sum_qkv)
     collect(sum_qkv, s.qkv_own)
     s.qkv_x[...] = s.qkv_own[...].astype(BF16).reshape(s.qkv_x.shape)
     deal_start(*qx_move)
@@ -1052,7 +1078,11 @@
     gvec_ref[8:9, :] = jnp.sum(jnp.where(chosen, block, 0.0), 0, keepdims=True)
     deal_wait(*fx_move)
     for slot in range(members):
-        gfc_ref[:, slot * chunk : slot * chunk + chunk] = s.fc_y[slot].astype(F32)
+        for quarter in range(quarters):
+            start = quarter * width + slot * piece
+            gfc_ref[:, start : start + piece] = s.fc_y[
+                slot, :, quarter * piece : quarter * piece + piece
+            ].astype(F32)
     deal_wait(*qx_move)
     for slot in range(members):
         for third in range(3):
@@ -1080,6 +1110,13 @@
         gather_drain(where, sent, got)
     for move in (sum_proj, sum_fc, sum_out, sum_qkv):
         spread_drain(move)
+
+
+def hand_over(*refs):
+    for source, target in zip(refs[:6], refs[7:13]):
+        target[...] = source[...]
+    for index, low in enumerate(refs[13:]):
+        low[...] = refs[6][index : index + 1, : low.shape[1]]
 
 
 def fused_layer(
@@ -1105,8 +1142,13 @@
     groups = lax.axis_size("ctx")
     shards = 2 * groups
     small = (ln1_gain, ln1_bias, ln2_gain, ln2_bias, bias_q, bias_v, bias_out, bias_proj, bias_fc)
-    vectors = jnp.concatenate(small).astype(F32).reshape(-1, width // 2)
-    vectors = jnp.pad(vectors, ((0, 16 - vectors.shape[0]), (0, 0)))
+    line = lax.broadcasted_iota(jnp.int32, (16, width // 2), 0)
+    vectors, at = jnp.zeros(line.shape, BF16), 0
+    for vector in small:
+        for start in range(0, vector.shape[0], width // 2):
+            piece = lax.broadcast_in_dim(vector[start : start + width // 2], line.shape, (1,))
+            vectors = jnp.where(line == at, piece, vectors)
+            at += 1
     shapes = layer_shapes(rows, width, ff, groups)
     names = tuple(shapes) + tuple(SEMAPHORES)
     scratch = [pltpu.VMEM(shape, kind) for shape, kind in shapes.values()]
@@ -1142,8 +1184,18 @@
         w_fc,
         w_proj,
     )
-    block_output, input_grad, grad_qkv, grad_out, grad_fc, grad_proj, sums = outs
     piece = width // shards
+    wide = ff // shards
+    results = pl.pallas_call(
+        hand_over,
+        out_shape=tuple(jax.ShapeDtypeStruct(out.shape, out.dtype) for out in outs[:6])
+        + (jax.ShapeDtypeStruct((1, piece), F32),) * 8
+        + (jax.ShapeDtypeStruct((1, wide), F32),),
+        in_specs=[in_vmem] * 7,
+        out_specs=(in_vmem,) * 15,
+    )(*outs)
+    block_output, input_grad, grad_qkv, grad_out, grad_fc, grad_proj = results[:6]
+    lows = [result.reshape(-1) for result in results[6:]]
     return (
         block_output.reshape(block_input.shape),
         input_grad.reshape(block_input.shape),
@@ -1151,15 +1203,9 @@
         grad_out,
         grad_fc,
         grad_proj,
-        sums[0, :piece],
-        sums[1, :piece],
-        sums[2, :piece],
-        sums[3, :piece],
-        sums[4, :piece],
-        sums[5, :piece],
-        sums[6, :piece],
-        sums[8, : ff // shards],
-        sums[7, :piece],
+        *lows[:7],
+        lows[8],
+        lows[7],
     )
 
 

time: 232 us -> 177 us (0.76)
  Pallas kernels: 209 us -> 173 us
  local copies, waits for them, and re-layouts: 20.9 us -> 0.77 us
    pallas_call x1, Pallas kernels: 209 us -> 170 us  [fused_layer(): pl.pallas_call(partial(layer_kernel, names), out_shape=(jax.ShapeDtypeStr...]
    unnamed x14 -> x0, local copies, waits for them, and re-layouts: 17.5 us -> none
    pallas_call x0 -> x1, Pallas kernels: none -> 3.07 us  [fused_layer(): pl.pallas_call(hand_over, out_shape=tuple((jax.ShapeDtypeStruct(out.shape...]
    squeeze x2 -> x0, local copies, waits for them, and re-layouts: 2.71 us -> none  [the longest x1 1.52 us: fused_layer(): sums[7, :piece]]
where the time goes in v3:
time: 177 us
  Pallas kernels  173 us (98%)
    pallas_call x1, Pallas kernels, fused_layer(): pl.pallas_call(partial(layer_kernel, names), out_shape=(jax.ShapeDtypeStr...  170 us

profile of v3, /device:TPU:0, one launch (start us, length us, event | category | flops | bytes accessed | tf_op | source)
XLA Modules:
  0.0 176.6 jit_solution(10027252070735290480)
XLA Ops:
  0.7 0.8 fusion
  1.5 1.5 select_select_fusion.refs_2_
  3.0 170.3 %shard_map.262 = (bf16[128,1024]{1,0:T(8,128)(2,1)}, f32[128,1024]{1,0:T(8,128)}, f32[32,3072]{1,0:T(8,128)}, f32[32,1024]{1,0:T(8,128)}, f32[32,4096]{1,0:T(8,1...) custom-call(bf16[128,1024]{1,0:T(8,128)(2,1)} %bitcast.14, bf16[128,1024]{1,0:T(8,128)(2,1)} %bitcast.15, ...), custom_call_target="tpu_custom_call" | custom-call | flops 14000000000 | bytes 30000000 | tf_op jit(solution)/shard_map/pallas_call | solution.py:1158
  173.3 3.1 %shard_map.263 = (bf16[128,1024]{1,0:T(8,128)(2,1)}, f32[128,1024]{1,0:T(8,128)}, f32[32,3072]{1,0:T(8,128)}, f32[32,1024]{1,0:T(8,128)}, f32[32,4096]{1,0:T(8,1...) custom-call(bf16[128,1024]{1,0:T(8,128)(2,1)} %get-tuple-element.37., ...), custom_call_target="tpu_custom_call" | custom-call | tf_op jit(solution)/shard_map/pallas_call | solution.py:1189
  (6 shorter events, 0.0 us)

commit v4 on v3

--- a/solution.py
+++ b/solution.py
@@ -9,7 +9,7 @@
 from jax.sharding import PartitionSpec as P
 
 HEADS = 16
-VMEM_BYTES = 62 * 2**20
+VMEM_BYTES = 127 * 2**19
 
 
 def norm_parts(values):
@@ -352,8 +352,10 @@
         g_low=((2, keys, 128), BF16),
         q_t=((128, keys), BF16),
         g_t=((128, keys), BF16),
-        stat=((2, keys, 128), F32),
+        stat=((2, 2, keys, 128), F32),
         mixed=((keys, 128), F32),
+        scores=((256, 9 * 256), F32),
+        dq=((2, keys, 128), F32),
         o_out=((groups, half, 128), BF16),
         o_in=((groups, half, 128), BF16),
         att=((rows, width), BF16),
@@ -362,18 +364,17 @@
         res=((rows, width), F32),
         n2=((rows, width), BF16),
         n2_t=((width, tokens), BF16),
-        act_t=((members, layers, ff // members // layers, rows), BF16),
-        act_all=((layers, ff // members // layers, tokens), BF16),
-        hg_out=((members, rows, ff // members), BF16),
-        hg_all=((members, rows, ff // members), BF16),
+        fc_t=((ff // members, width), BF16),
+        bias_t=((ff // members, 128), F32),
+        proj_own=((ff // members, width), BF16),
+        act_all=((ff // members, tokens), BF16),
+        hg_all=((ff // members, tokens), BF16),
         acc_o=((rows, width), F32),
         acc_d=((rows, width), F32),
         res_grad=((rows, width), F32),
         bg_all=((members, rows, width), BF16),
         g_out=((groups, half, 128), BF16),
         g_in=((keys, 128), BF16),
-        dk_t=((128, keys), F32),
-        dv_t=((128, keys), F32),
         back=((groups, 3, half, 128), BF16),
         qg=((rows, 3 * width), BF16),
         qg_out=((members, rows, 3 * share), BF16),
@@ -385,55 +386,39 @@
         qkv_x=((members, width // layers // members, 3 * share), BF16),
         qkv_y=((members, width // layers // members, 3 * share), BF16),
         sums=((16, width), F32),
-        sums_in=((7, 16, width), F32),
+        sums_out=((layers, 16, width // layers), F32),
+        sums_in=((3, 16, width // layers), F32),
+        sums_all=((members, 16, width // layers), F32),
     )
 
 
 SEMAPHORES = dict(
     local=4,
-    w_sent=15,
-    w_got=15,
-    v_sent=1,
-    v_got=1,
-    qkv_sent=16,
-    qkv_got=16,
-    o_sent=16,
-    o_got=16,
-    g_sent=16,
-    g_got=16,
-    back_sent=16,
-    back_got=16,
-    cot_sent=8,
-    cot_got=8,
-    n1_sent=8,
-    n1_got=8,
-    n2_sent=8,
-    n2_got=8,
-    bg_sent=8,
-    bg_got=8,
-    act_sent=8,
-    act_got=8,
-    hg_sent=8,
-    hg_got=8,
-    att_sent=8,
-    att_got=8,
-    qg_sent=8,
-    qg_got=8,
-    rp_sent=4,
-    rp_got=4,
-    rf_sent=4,
-    rf_got=4,
-    ro_sent=4,
-    ro_got=4,
-    rq_sent=4,
-    rq_got=4,
-    fx_sent=8,
-    fx_got=8,
-    qx_sent=8,
-    qx_got=8,
-    s_sent=8,
-    s_got=8,
+    w_sent=4,
+    w_got=7,
+    vec_sent=1,
+    vec_got=1,
+    swap_sent=5,
+    swap_got=5,
+    cot_sent=1,
+    cot_got=5,
+    n1_sent=1,
+    n1_got=5,
+    n2_sent=1,
+    n2_got=5,
+    bg_sent=1,
+    bg_got=5,
+    deal_sent=4,
+    deal_got=4,
+    sum_sent=4,
+    sum_got=8,
+    low_sent=2,
+    low_got=2,
 )
+
+
+def settle(ref, semaphore):
+    pltpu.make_async_copy(ref, ref, semaphore).wait()
 
 
 def layer_kernel(names, *refs):
@@ -484,25 +469,26 @@
         count = source.shape[0]
         return ref.at[pl.ds(pl.multiple_of(other * count, count), count)]
 
-    first = 2 * (1 - layer // 2)
 
     def order(step):
-        return (step + first) % 4
+        return (layer + 2 + step) % 4
+
+    def order_in(step):
+        return (place + 1 + step) % 4
 
     pltpu.make_async_copy(wq_hbm, top_rows(s.w_qkv, wq_hbm), s.local.at[0]).start()
 
     def qkv_piece(step, third):
         columns = part(third * 4 + order(step), 256)
-        index = step * 3 + third
         return remote(
             wq_hbm.at[:, columns],
             top_rows(s.w_qkv, wq_hbm).at[:, columns],
-            s.w_sent.at[index],
-            s.w_got.at[index],
+            s.w_sent.at[0],
+            s.w_got.at[step],
             twin,
         )
 
-    vec_copy = remote(vec_ref, s.vec_low.at[core], s.v_sent.at[0], s.v_got.at[0], twin)
+    vec_copy = remote(vec_ref, s.vec_low.at[core], s.vec_sent.at[0], s.vec_got.at[0], twin)
     vec_copy.start()
     for step in range(4):
         for third in range(3):
@@ -512,114 +498,127 @@
     def big_piece(index):
         source, target = big[index]
         return remote(
-            source, top_rows(target, source), s.w_sent.at[12 + index], s.w_got.at[12 + index], twin
+            source, top_rows(target, source), s.w_sent.at[1 + index], s.w_got.at[4 + index], twin
         )
 
     def big_local(index):
         source, target = big[index]
         return pltpu.make_async_copy(source, top_rows(target, source), s.local.at[1 + index])
 
-    for index in range(3):
-        big_piece(index).start()
-        big_local(index).start()
-
-    def gather_copy(where, sent, got, index, slot, device):
-        return remote(where(slot), where(slot), sent.at[index], got.at[slot], device)
+    def gather_copy(where, sent, got, slot, index, device):
+        return remote(where(slot), where(slot), sent.at[0], got.at[index], device)
 
     def gather_start(where, sent, got):
         for step in range(1, PLANE):
             peer = layer * PLANE + (place + step) % PLANE
-            gather_copy(where, sent, got, step, member, (peer, core)).start()
-        gather_copy(where, sent, got, 0, member, twin).start()
+            gather_copy(where, sent, got, member, place, (peer, core)).start()
+        gather_copy(where, sent, got, member, PLANE, twin).start()
 
     def gather_forward(where, sent, got):
         for step in range(1, PLANE):
-            slot = ((place + step) % PLANE) * 2 + core
-            gather_copy(where, sent, got, 0, slot, twin).wait_recv()
-            gather_copy(where, sent, got, PLANE - 1 + step, slot, twin).start()
+            peer = (place + step) % PLANE
+            settle(where(peer * 2 + core), got.at[peer])
+            gather_copy(where, sent, got, peer * 2 + core, PLANE, twin).start()
 
     def gather_finish(where, sent, got):
-        for step in range(PLANE):
-            slot = ((place + step) % PLANE) * 2 + other
-            gather_copy(where, sent, got, 0, slot, twin).wait_recv()
+        settle(where(0, PLANE), got.at[PLANE])
 
     def gather_drain(where, sent, got):
-        for index in range(2 * PLANE - 1):
-            gather_copy(where, sent, got, index, member, twin).wait_send()
-
-    def cot_at(slot):
-        return s.cot_all.at[slot]
-
-    def bg_at(slot):
-        return s.bg_all.at[slot]
-
-    def n1_at(slot):
-        return s.n1_t.at[:, part(slot, rows)]
-
-    def n2_at(slot):
-        return s.n2_t.at[:, part(slot, rows)]
-
-    def deal_copy(source, target, sent, got, index, slot):
-        return remote(source(index), target(slot), sent.at[index], got.at[slot], at_member(index))
-
-    def deal_one(source, target, sent, got, index):
-        @pl.when(index == member)
-        def _():
-            pltpu.make_async_copy(source(index), target(member), got.at[member]).start()
-
-        @pl.when(index != member)
-        def _():
-            deal_copy(source, target, sent, got, index, member).start()
-
-    def deal_start(source, target, sent, got):
-        for step in range(members):
-            if step == 0:
-                pltpu.make_async_copy(source(member), target(member), got.at[member]).start()
-            else:
-                deal_copy(source, target, sent, got, (member + step) % members, member).start()
-
-    def deal_wait(source, target, sent, got):
-        for slot in range(members):
-            pltpu.make_async_copy(source(0), target(slot), got.at[slot]).wait()
-
-    def deal_drain(source, target, sent, got):
+        settle(where(0, 2 * PLANE - 1), sent.at[0])
+
+    def cot_at(slot, count=None):
+        return s.cot_all.at[slot if count is None else pl.ds(slot, count)]
+
+    def bg_at(slot, count=None):
+        return s.bg_all.at[slot if count is None else pl.ds(slot, count)]
+
+    def columns_at(ref, slot, count):
+        return ref.at[:, part(slot, rows) if count is None else pl.ds(slot * rows, count * rows)]
+
+    def n1_at(slot, count=None):
+        return columns_at(s.n1_t, slot, count)
+
+    def n2_at(slot, count=None):
+        return columns_at(s.n2_t, slot, count)
+
+    def deal_copy(source, target, number, index):
+        return remote(
+            source(index),
+            target(member),
+            s.deal_sent.at[number],
+            s.deal_got.at[number],
+            at_member(index),
+        )
+
+    def deal_own(source, target, number):
+        return pltpu.make_async_copy(source(member), target(member), s.deal_got.at[number])
+
+    def deal_start(source, target, number):
         for step in range(1, members):
-            deal_copy(source, target, sent, got, (member + step) % members, member).wait_send()
-
-    def swap_one(source, target, sent, got, index):
+            deal_copy(source, target, number, (member + step) % members).start()
+        deal_own(source, target, number).start()
+
+    def deal_wait(source, target, number):
+        settle(target(None), s.deal_got.at[number])
+
+    def deal_drain(source, target, number):
+        settle(source(None), s.deal_sent.at[number])
+
+    def seven(index):
+        return pl.ds(0, members - 1) if index is None else index
+
+    def whole(index):
+        return slice(None) if index is None else index
+
+    def lanes(index):
+        return slice(None) if index is None else part(index, rows)
+
+    def swap_one(source, target, number, index):
         @pl.when(index == me)
         def _():
-            pltpu.make_async_copy(source(index), target(me), got.at[me]).start()
+            pltpu.make_async_copy(source(index), target(me), s.swap_got.at[number]).start()
 
         @pl.when(index != me)
         def _():
-            remote(source(index), target(me), sent.at[index], got.at[me], (index, core)).start()
-
-    def swap_wait(source, target, sent, got):
-        for slot in range(groups):
-            pltpu.make_async_copy(source(0), target(slot), got.at[slot]).wait()
-
-    def swap_drain(source, target, sent, got):
-        for step in range(1, groups):
-            peer = (me + step) % groups
-            remote(source(peer), target(me), sent.at[peer], got.at[me], (peer, core)).wait_send()
-
-    qkv_move = (
-        lambda h: s.stage.at[h],
-        lambda i: s.qkv.at[:, part(i, half)],
-        s.qkv_sent,
-        s.qkv_got,
-    )
-    o_move = (lambda h: s.o_out.at[h], lambda h: s.o_in.at[h], s.o_sent, s.o_got)
-    g_move = (lambda h: s.g_out.at[h], lambda i: s.g_in.at[part(i, half)], s.g_sent, s.g_got)
-    back_move = (lambda h: s.stage.at[h], lambda h: s.back.at[h], s.back_sent, s.back_got)
+            remote(
+                source(index),
+                target(me),
+                s.swap_sent.at[number],
+                s.swap_got.at[number],
+                (index, core),
+            ).start()
+
+    def swap_wait(source, target, number):
+        settle(target(None), s.swap_got.at[number])
+
+    def swap_drain(source, target, number):
+        settle(source(None), s.swap_sent.at[number])
+
+    def others(index):
+        return pl.ds(0, groups - 1) if index is None else index
+
+    def block(index):
+        return slice(None) if index is None else part(index, half)
+
+    qkv_move = (lambda h: s.stage.at[others(h)], lambda i: s.qkv.at[:, block(i)], 0)
+    o_move = (lambda h: s.o_out.at[others(h)], lambda h: s.o_in.at[whole(h)], 1)
+    g_move = (lambda h: s.g_out.at[others(h)], lambda i: s.g_in.at[block(i)], 2)
+    kv_back = (
+        lambda h: s.stage.at[others(h), pl.ds(1, 2)],
+        lambda h: s.back.at[whole(h), pl.ds(1, 2)],
+        3,
+    )
+    q_back = (lambda h: s.stage.at[others(h), 0], lambda h: s.back.at[whole(h), 0], 4)
+    att_move = (lambda g: s.att_t.at[:, seven(g)], lambda g: s.att_all.at[:, :, lanes(g)], 0)
+    qg_move = (lambda g: s.qg_out.at[seven(g)], lambda g: s.qg_all.at[whole(g)], 1)
+    fx_move = (lambda g: s.fc_x.at[seven(g)], lambda g: s.fc_y.at[whole(g)], 2)
+    qx_move = (lambda g: s.qkv_x.at[seven(g)], lambda g: s.qkv_y.at[whole(g)], 3)
 
     def vec_row(index):
         return jnp.concatenate([s.vec[0, index : index + 1, :], s.vec[1, index : index + 1, :]], 1)
 
     s.cot_all[member] = cot_ref[...]
-    gather_start(cot_at, s.cot_sent, s.cot_got)
-    remote(vec_ref, s.vec_low.at[other], s.v_sent.at[0], s.v_got.at[0], twin).wait_recv()
+    settle(vec_ref, s.vec_got.at[0])
     s.vec[core] = vec_ref[...].astype(F32)
     s.vec[other] = s.vec_low[other].astype(F32)
     s.row[0:1, :] = vec_row(4)
@@ -638,16 +637,9 @@
 
     for step in range(4):
         four = order(step)
+        settle(peer_rows(s.w_qkv, wq_hbm).at[:, pl.ds(0, 768)], s.w_got.at[step])
         for third in range(3):
-            index = step * 3 + third
             columns = part(third * 4 + four, 256)
-            remote(
-                wq_hbm.at[:, columns],
-                peer_rows(s.w_qkv, wq_hbm).at[:, columns],
-                s.w_sent.at[index],
-                s.w_got.at[index],
-                twin,
-            ).wait_recv()
             product = dot(s.n1[...], s.w_qkv[:, columns])
             if third == 0:
                 product = product + s.row[0:1, part(four, 256)]
@@ -658,10 +650,13 @@
                 s.stage[four * 4 + 2 * pair, third] = even.astype(BF16)
                 s.stage[four * 4 + 2 * pair + 1, third] = odd.astype(BF16)
         for head in range(4):
-            swap_one(*qkv_move, four * 4 + head)
+            swap_one(*qkv_move, four * 4 + order_in(head))
+    gather_start(cot_at, s.cot_sent, s.cot_got)
+    for index in range(3):
+        big_piece(index).start()
+        big_local(index).start()
 
     swap_wait(*qkv_move)
-    gather_start(n1_at, s.n1_sent, s.n1_got)
     low_all = low_lanes(keys)
     query = s.qkv[0].astype(F32)
     s.q_low[0] = jnp.where(low_all, query, 0.0).astype(BF16)
@@ -687,65 +682,80 @@
     def value_block(region, at):
         return s.qkv[2, at, :] if region == 0 else s.kv_roll[1, at, :]
 
-    def first_tile(queries, region, at):
-        scores = jnp.where(
-            masks[region], right_transposed(queries, key_block(region, at)), NEG
-        )
-        top = jnp.max(scores, 1, keepdims=True)
-        probs = jnp.exp2((scores - top) * factor)
-        total = jnp.sum(probs, 1, keepdims=True)
-        return top, total, dot(probs.astype(BF16), value_block(region, at))
-
-    def next_tile(queries, region, at, carry):
-        top, total, mix = carry
-        scores = right_transposed(queries, key_block(region, at))
-        higher = jnp.maximum(top, jnp.max(scores, 1, keepdims=True))
-        probs = jnp.exp2((scores - higher) * factor)
-        shrink = jnp.exp2((top - higher) * factor)
-        total = total * shrink + jnp.sum(probs, 1, keepdims=True)
-        return higher, total, mix * shrink + dot(probs.astype(BF16), value_block(region, at))
-
     n_tiles = keys // tile
 
-    def attend(index, _):
-        at = part(index, tile)
-        early_q, late_q = s.q_low[0, at, :], s.q_low[1, at, :]
-        one = lax.fori_loop(
-            0,
-            index,
-            lambda k, carry: next_tile(early_q, 0, part(k, tile), carry),
-            first_tile(early_q, 0, at),
-        )
-        two = lax.fori_loop(
-            index + 1,
-            n_tiles,
-            lambda k, carry: next_tile(late_q, 1, part(k, tile), carry),
-            first_tile(late_q, 1, at),
-        )
-        two = lax.fori_loop(
-            0, n_tiles // 2, lambda k, carry: next_tile(late_q, 0, part(k, 2 * tile), carry), two
-        )
-        s.stat[0, at, 0:1] = one[0] * factor + jnp.log2(one[1])
-        s.stat[1, at, 0:1] = two[0] * factor + jnp.log2(two[1])
-        out = jnp.where(low_tile, one[2] / one[1], swap(two[2] / two[1]))
+    def span(start, count=1):
+        return slice(start * tile, (start + count) * tile)
+
+    def score_block(queries, region, first, count, column, masked):
+        scores = right_transposed(queries, key_block(region, span(first, count)))
+        if masked:
+            scores = jnp.where(masks[region], scores, NEG)
+        s.scores[:, span(column, count)] = scores
+        return scores
+
+    def fold(values, combine):
+        out = values[:, :128]
+        for start in range(128, values.shape[1], 128):
+            out = combine(out, values[:, start : start + 128])
+        return out
+
+    def softmax_rows(side, blocks, at):
+        queries = s.q_low[side, at, :]
+        top = None
+        for block in blocks:
+            high = fold(score_block(queries, *block), jnp.maximum)
+            top = high if top is None else jnp.maximum(top, high)
+        top = jnp.max(top, 1, keepdims=True) * factor
+        total, mix = None, None
+        for region, first, count, column, _ in blocks:
+            probs = jnp.exp2(s.scores[:, span(column, count)] * factor - top)
+            folded = fold(probs, jnp.add)
+            total = folded if total is None else total + folded
+            more = dot(probs.astype(BF16), value_block(region, span(first, count)))
+            mix = more if mix is None else mix + more
+        total = jnp.sum(total, 1, keepdims=True)
+        s.stat[0, side, at, :] = jnp.broadcast_to(top + jnp.log2(total), (tile, 128))
+        return mix / total
+
+    def attend(index):
+        at = span(index)
+        early = [(0, index, 1, 0, True)]
+        if index:
+            early.append((0, 0, index, 1, False))
+        late_blocks = [(1, index, 1, index + 1, True)]
+        if index + 1 < n_tiles:
+            late_blocks.append((1, index + 1, n_tiles - 1 - index, index + 2, False))
+        late_blocks.append((0, 0, n_tiles, n_tiles + 1, False))
+        one = softmax_rows(0, early, at)
+        two = softmax_rows(1, late_blocks, at)
+        out = jnp.where(low_tile, one, swap(two))
         s.mixed[at, :] = out
-        s.o_out[part(index, per_tile)] = out.astype(BF16).reshape(per_tile, half, 128)
-        for block in range(per_tile):
-            swap_one(*o_move, index * per_tile + block)
-        return 0
-
-    lax.fori_loop(0, n_tiles, attend, 0)
+        s.o_out[pl.ds(index * per_tile, per_tile)] = out.astype(BF16).reshape(per_tile, half, 128)
+        for step in range(per_tile):
+            swap_one(*o_move, index * per_tile + order_in(step))
+
+    for index in range(n_tiles):
+        attend(index)
 
     for index in range(3):
-        source, target = big[index]
-        remote(
-            source,
-            peer_rows(target, source),
-            s.w_sent.at[12 + index],
-            s.w_got.at[12 + index],
-            twin,
-        ).wait_recv()
+        settle(peer_rows(big[index][1], big[index][0]), s.w_got.at[4 + index])
         big_local(index).wait()
+    quarters = ff // width
+    piece = width // members
+
+    curve = 0.7978845608028654
+
+    def features(index):
+        return [part(quarter * members + index, piece) for quarter in range(quarters)]
+
+    mine = features(member)
+    s.proj_own[...] = jnp.concatenate([s.w_proj[at, :] for at in mine], 0)
+    for quarter, at in enumerate(mine):
+        into = slice(quarter * piece, quarter * piece + piece)
+        s.fc_t[into, :] = s.w_fc[:, at].astype(F32).T.astype(BF16)
+        bias = s.row[4 + quarter : 5 + quarter, part(member, piece)]
+        s.bias_t[into, :] = jnp.broadcast_to(bias, (128, piece)).T
     swap_wait(*o_move)
     for pair in range(HEADS // 2):
         columns = slice(pair * 128, pair * 128 + 128)
@@ -754,12 +764,6 @@
         ).astype(BF16)
     turned = s.att[...].astype(F32).T.astype(BF16)
     s.att_t[...] = turned.reshape(s.att_t.shape)
-    att_move = (
-        lambda g: s.att_t.at[:, g],
-        lambda g: s.att_all.at[:, :, part(g, rows)],
-        s.att_sent,
-        s.att_got,
-    )
     def project(index, _):
         at = part(index, 256)
         s.acc_d[:, at] = dot(s.att[...], s.w_out[:, at])
@@ -771,24 +775,23 @@
     normed = (normal * vec_row(2) + vec_row(3)).astype(BF16)
     s.n2[...] = normed
     s.n2_t[:, part(member, rows)] = normed.astype(F32).T.astype(BF16)
+    gather_start(n2_at, s.n2_sent, s.n2_got)
     s.acc_o[...] = jnp.zeros_like(s.acc_o)
     s.acc_d[...] = jnp.zeros_like(s.acc_d)
     s.sums[...] = jnp.zeros_like(s.sums)
-    hg_move = (lambda g: s.hg_out.at[g], lambda g: s.hg_all.at[g], s.hg_sent, s.hg_got)
-    curve = 0.7978845608028654
-
-    act_move = (
-        lambda g: s.act_t.at[g],
-        lambda g: s.act_all.at[:, :, part(g, rows)],
-        s.act_sent,
-        s.act_got,
-    )
-    quarters = ff // width
-    piece = width // members
-
-    def feed(step, _):
-        index = (member + 1 + step) % members
-        places = [part(quarter * members + index, piece) for quarter in range(quarters)]
+
+
+    def gelu_parts(hidden):
+        square = hidden * hidden
+        bend = jnp.tanh(curve * hidden * (1.0 + 0.044715 * square))
+        rise = 0.5 * (1.0 + bend)
+        slope = rise + 0.5 * hidden * (1.0 - bend * bend) * (
+            curve * (1.0 + 3.0 * 0.044715 * square)
+        )
+        return hidden * rise, slope
+
+    def feed(index, _):
+        places = features(index)
         bias = jnp.concatenate(
             [s.row[4 + quarter : 5 + quarter, part(index, piece)] for quarter in range(quarters)], 1
         )
@@ -796,17 +799,9 @@
         back = jnp.concatenate([s.w_proj[at, :] for at in places], 0)
         hidden = dot(s.n2[...], into) + bias
         upstream = right_transposed(cot_ref[...], back)
-        square = hidden * hidden
-        bend = jnp.tanh(curve * hidden * (1.0 + 0.044715 * square))
-        rise = 0.5 * (1.0 + bend)
-        active = (hidden * rise).astype(BF16)
-        slope = rise + 0.5 * hidden * (1.0 - bend * bend) * (
-            curve * (1.0 + 3.0 * 0.044715 * square)
-        )
+        active, slope = gelu_parts(hidden)
+        active = active.astype(BF16)
         grad = (upstream * slope).astype(BF16)
-        s.act_t[index] = active.astype(F32).T.astype(BF16).reshape(s.act_t.shape[1:])
-        deal_one(*act_move, index)
-        s.hg_out[index] = grad
         s.acc_o[...] += dot(active, back)
         s.acc_d[...] += right_transposed(grad, into)
         total = jnp.sum(grad.astype(F32), 0, keepdims=True)
@@ -836,12 +831,12 @@
             s.g_out[four * 4 + 2 * pair] = even.astype(BF16)
             s.g_out[four * 4 + 2 * pair + 1] = odd.astype(BF16)
         for head in range(4):
-            swap_one(*g_move, four * 4 + head)
-    deal_start(*hg_move)
-    gather_start(n2_at, s.n2_sent, s.n2_got)
+            swap_one(*g_move, four * 4 + order_in(head))
     y_ref[...] = (s.res[...] + s.acc_o[...] + vec_row(7)).astype(BF16)
+    gather_start(bg_at, s.bg_sent, s.bg_got)
+    deal_start(*att_move)
     gather_forward(cot_at, s.cot_sent, s.cot_got)
-    gather_forward(n1_at, s.n1_sent, s.n1_got)
+    gather_forward(n2_at, s.n2_sent, s.n2_got)
     swap_drain(*qkv_move)
 
     beside = layer + 1 - 2 * (layer % 2)
@@ -849,84 +844,86 @@
     across = (beside + 2) % layers
 
     def spread_copy(move, slot, target):
-        buffer_out, buffer_in, sent, got = move
+        buffer_out, buffer_in, number = move
         return remote(
             buffer_out(slot),
             buffer_in(slot),
-            sent.at[slot],
-            got.at[slot],
+            s.sum_sent.at[number],
+            s.sum_got.at[2 * number + (slot + 1) // 2],
             (target * PLANE + place, core),
         )
 
+    def spread_prepare(move, product, own_ref):
+        for slot, index in enumerate((across, beside, beyond)):
+            move[0](slot)[...] = product(index).astype(BF16)
+        own_ref[...] = product(layer)
+
+    def spread_start(move):
+        for slot in range(2):
+            spread_copy(move, slot, beside).start()
+
     def spread(move, product, own_ref):
-        for slot, index in enumerate((beside, across, beyond)):
+        for slot, index in enumerate((across, beside, beyond)):
             move[0](slot)[...] = product(index).astype(BF16)
             if slot < 2:
                 spread_copy(move, slot, beside).start()
         own_ref[...] = product(layer)
 
     def spread_on(move):
-        spread_copy(move, 1, beside).wait_recv()
-        pair = move[0](2)[...].astype(F32) + move[1](1)[...].astype(F32)
+        settle(move[1](0), s.sum_got.at[2 * move[2]])
+        pair = move[0](2)[...].astype(F32) + move[1](0)[...].astype(F32)
         move[0](2)[...] = pair.astype(BF16)
         spread_copy(move, 2, beyond).start()
 
     def collect(move, own_ref):
-        for slot in (0, 2):
-            spread_copy(move, slot, beside).wait_recv()
-        own_ref[...] += move[1](0)[...].astype(F32) + move[1](2)[...].astype(F32)
+        settle(move[1](1, 2), s.sum_got.at[2 * move[2] + 1])
+        own_ref[...] += move[1](1)[...].astype(F32) + move[1](2)[...].astype(F32)
 
     def spread_drain(move):
-        for slot in range(3):
-            spread_copy(move, slot, beside).wait_send()
+        settle(move[0](0, 3), s.sum_sent.at[move[2]])
 
     proj_rows = ff // members // layers
     out_rows = share // layers
     fc_rows = width // layers
 
-    def rows_of(ref, start, count, columns=slice(None)):
-        return lambda i: ref.at[pl.ds(pl.multiple_of(start + i * count, count), count), columns]
-
-    sum_proj = (
-        rows_of(s.w_proj, 0, proj_rows),
-        rows_of(s.w_proj, 512, proj_rows),
-        s.rp_sent,
-        s.rp_got,
-    )
-    sum_out = (
-        rows_of(s.w_proj, 1024, out_rows),
-        rows_of(s.w_proj, 1152, out_rows),
-        s.ro_sent,
-        s.ro_got,
-    )
+    def rows_of(ref, start, size, columns=slice(None)):
+        return lambda slot, count=1: ref.at[pl.ds(start + slot * size, count * size), columns]
+
+    sum_proj = (rows_of(s.w_proj, 0, proj_rows), rows_of(s.w_proj, 512, proj_rows), 0)
+    sum_out = (rows_of(s.w_proj, 1024, out_rows), rows_of(s.w_proj, 1152, out_rows), 1)
     sum_fc = (
         rows_of(s.w_fc, 0, fc_rows, pl.ds(0, chunk)),
         rows_of(s.w_fc, 0, fc_rows, pl.ds(chunk, chunk)),
-        s.rf_sent,
-        s.rf_got,
+        2,
     )
     sum_qkv = (
         rows_of(s.w_fc, 0, fc_rows, pl.ds(2 * chunk, 3 * share)),
         rows_of(s.w_fc, 0, fc_rows, pl.ds(3 * chunk, 3 * share)),
-        s.rq_sent,
-        s.rq_got,
-    )
-    def grad_of_proj():
+        3,
+    )
+
+    def feed_again(index, _):
+        at = part(index, 2 * rows)
+        hidden = dot(s.fc_t[...], s.n2_t[:, at]) + jnp.concatenate([s.bias_t[...]] * 2, 1)
+        cotangents = s.cot_all[pl.ds(2 * index, 2)].reshape(2 * rows, width)
+        upstream = right_transposed(s.proj_own[...], cotangents)
+        active, slope = gelu_parts(hidden)
+        s.act_all[:, at] = active.astype(BF16)
+        s.hg_all[:, at] = (upstream * slope).astype(BF16)
+        return 0
+
+    def grads_of_feed():
         gather_finish(cot_at, s.cot_sent, s.cot_got)
-        deal_wait(*act_move)
-        spread(
+        gather_finish(n2_at, s.n2_sent, s.n2_got)
+        lax.fori_loop(0, PLANE, feed_again, 0)
+        spread_prepare(
             sum_proj,
-            lambda i: dot(s.act_all[i], s.cot_all[...].reshape(tokens, width)),
+            lambda i: dot(s.act_all[part(i, proj_rows), :], s.cot_all[...].reshape(tokens, width)),
             gproj_ref,
         )
-
-    def grad_of_fc():
-        gather_forward(n2_at, s.n2_sent, s.n2_got)
-        gather_finish(n2_at, s.n2_sent, s.n2_got)
-        deal_wait(*hg_move)
-        spread(
+        spread_prepare(
             sum_fc,
-            lambda i: dot(s.n2_t[part(i, fc_rows), :], s.hg_all[...].reshape(tokens, chunk)),
+            lambda i: right_transposed(s.n2_t[part(i, fc_rows), :], s.hg_all[...]),
             s.fc_own,
         )
 
@@ -939,75 +936,69 @@
             gout_ref,
         )
 
+    grads_of_feed()
     swap_wait(*g_move)
     upstream = s.g_in[...].astype(F32)
     s.g_low[0] = jnp.where(low_all, upstream, 0.0).astype(BF16)
     s.g_low[1] = jnp.where(low_all, swap(upstream), 0.0).astype(BF16)
     s.g_t[...] = upstream.T.astype(BF16)
     inner = upstream * s.mixed[...]
-    s.stat[0, :, 1:2] = jnp.sum(jnp.where(low_all, inner, 0.0), 1, keepdims=True)
-    s.stat[1, :, 1:2] = jnp.sum(jnp.where(low_all, 0.0, inner), 1, keepdims=True)
-    s.dk_t[...] = jnp.zeros_like(s.dk_t)
-    s.dv_t[...] = jnp.zeros_like(s.dv_t)
-
-    def back_tile(side, region, at_q, at_k, masked, total):
+    for side in range(2):
+        kept = jnp.where(low_all == (side == 0), inner, 0.0)
+        s.stat[1, side] = jnp.broadcast_to(jnp.sum(kept, 1, keepdims=True), (keys, 128))
+    s.dq[...] = jnp.zeros_like(s.dq)
+
+    def wide(block):
+        return jnp.concatenate([block] * (tile // 128), 1)
+
+    def back_tile(side, region, at_q, at_k, masked):
         scores = right_transposed(s.q_low[side, at_q, :], key_block(region, at_k))
-        probs = jnp.exp2(scores * factor - s.stat[side, at_q, 0:1])
+        probs = jnp.exp2(scores * factor - wide(s.stat[0, side, at_q, :]))
         if masked:
             probs = jnp.where(masks[region], probs, 0.0)
         prob_grad = right_transposed(s.g_low[side, at_q, :], value_block(region, at_k))
-        score_grad = (probs * (prob_grad - s.stat[side, at_q, 1:2])).astype(BF16)
+        score_grad = (probs * (prob_grad - wide(s.stat[1, side, at_q, :]))).astype(BF16)
         head = slice(side * 64, side * 64 + 64)
-        into = slice(region * 64, region * 64 + 64)
-        s.dk_t[into, at_k] += dot(s.q_t[head, at_q], score_grad)
-        s.dv_t[into, at_k] += dot(s.g_t[head, at_q], probs.astype(BF16))
-        more = dot(score_grad, key_block(region, at_k))
-        return more if total is None else total + more
-
-    def attend_back(index, _):
-        at = part(index, tile)
-        one = lax.fori_loop(
-            0,
-            index,
-            lambda k, total: back_tile(0, 0, at, part(k, tile), False, total),
-            back_tile(0, 0, at, at, True, None),
-        )
-        two = lax.fori_loop(
-            index + 1,
-            n_tiles,
-            lambda k, total: back_tile(1, 1, at, part(k, tile), False, total),
-            back_tile(1, 1, at, at, True, None),
-        )
-        two = lax.fori_loop(
-            0,
-            n_tiles // 2,
-            lambda k, total: back_tile(1, 0, at, part(k, 2 * tile), False, total),
-            two,
-        )
-        out = (jnp.where(low_tile, one, swap(two)) * scaling).astype(BF16)
-        s.stage[part(index, per_tile), 0] = out.reshape(per_tile, half, 128)
-        return 0
-
-    attend_back(0, 0)
-    grad_of_proj()
-    attend_back(1, 0)
-    attend_back(2, 0)
-    spread_on(sum_proj)
-    gather_start(bg_at, s.bg_sent, s.bg_got)
-    deal_start(*att_move)
-    attend_back(3, 0)
-    s.stage[:, 1] = (s.dk_t[...].T * scaling).astype(BF16).reshape(groups, half, 128)
-    s.stage[:, 2] = s.dv_t[...].T.astype(BF16).reshape(groups, half, 128)
+        s.dq[side, at_q, :] += dot(score_grad, key_block(region, at_k))
+        return dot(s.q_t[head, at_q], score_grad), dot(s.g_t[head, at_q], probs.astype(BF16))
+
+    def attend_back(index):
+        at = span(index)
+        early = [(0, 0, k, k == index) for k in range(index, n_tiles)]
+        early += [(1, 0, k, False) for k in range(n_tiles)]
+        late_pairs = [(1, 1, k, k == index) for k in range(index + 1)]
+        grads = []
+        for pairs in (early, late_pairs):
+            both = [
+                back_tile(side, region, span(k), at, masked) for side, region, k, masked in pairs
+            ]
+            grads.append([sum(parts) for parts in zip(*both)])
+        for third, scale in ((1, scaling), (2, 1.0)):
+            rows_t = jnp.concatenate([grads[0][third - 1], grads[1][third - 1]], 0)
+            s.stage[pl.ds(index * per_tile, per_tile), third] = (
+                (rows_t.T * scale).astype(BF16).reshape(per_tile, half, 128)
+            )
+        for step in range(per_tile):
+            swap_one(*kv_back, index * per_tile + order_in(step))
+
+    spread_start(sum_proj)
+    attend_back(0)
+    attend_back(1)
+    attend_back(2)
+    attend_back(3)
+    out = jnp.where(low_all, s.dq[0], swap(s.dq[1])) * scaling
+    s.stage[:, 0] = out.astype(BF16).reshape(groups, half, 128)
     for step in range(4):
         for head in range(4):
-            swap_one(*back_move, order(step) * 4 + head)
-    grad_of_fc()
+            swap_one(*q_back, order(step) * 4 + order_in(head))
+    spread_start(sum_fc)
+    gather_start(n1_at, s.n1_sent, s.n1_got)
     gather_forward(bg_at, s.bg_sent, s.bg_got)
     grad_of_out()
-    spread_on(sum_fc)
-
-    swap_wait(*back_move)
-    spread_on(sum_out)
+    spread_on(sum_proj)
+
+    swap_wait(*kv_back)
+    swap_wait(*q_back)
     for pair in range(HEADS // 2):
         for third in range(3):
             block = unpack_pair(
@@ -1016,7 +1007,6 @@
             s.qg_out[pair, :, third * 128 : third * 128 + 128] = block
             columns = slice(third * width + pair * 128, third * width + pair * 128 + 128)
             s.qg[:, columns] = block
-    qg_move = (lambda g: s.qg_out.at[g], lambda g: s.qg_all.at[g], s.qg_sent, s.qg_got)
     deal_start(*qg_move)
     s.sums[4:5, :] = jnp.sum(s.qg[:, :width].astype(F32), 0, keepdims=True)
     s.sums[5:6, :] = jnp.sum(s.qg[:, 2 * width :].astype(F32), 0, keepdims=True)
@@ -1032,11 +1022,33 @@
     s.sums[1:2, :] = shift_grad[None]
     gx_ref[...] = s.res_grad[...] + step_grad
 
-    def sum_copy(index, slot, device):
-        return remote(s.sums, s.sums_in.at[slot], s.s_sent.at[index], s.s_got.at[slot], device)
-
-    sum_copy(0, 0, twin).start()
-
+    lanes_of_layer = width // layers
+    for index in range(layers):
+        columns = slice(index * lanes_of_layer, (index + 1) * lanes_of_layer)
+        s.sums_out[index, 0:8, :] = s.sums[0:8, columns]
+        for quarter in range(layers):
+            columns = slice(quarter * lanes_of_layer, (quarter + 1) * lanes_of_layer)
+            s.sums_out[index, 8 + quarter : 9 + quarter, :] = s.sums[8 + index : 9 + index, columns]
+    for step in range(1, layers):
+        target = (layer + step) % layers
+        remote(
+            s.sums_out.at[target],
+            s.sums_in.at[step - 1],
+            s.low_sent.at[0],
+            s.low_got.at[0],
+            (target * PLANE + place, core),
+        ).start()
+
+    def low_copy(step):
+        return remote(
+            s.sums_all.at[member],
+            s.sums_all.at[member],
+            s.low_sent.at[1],
+            s.low_got.at[1],
+            at_member((member + step) % members),
+        )
+
+    gather_forward(n1_at, s.n1_sent, s.n1_got)
     gather_finish(n1_at, s.n1_sent, s.n1_got)
     deal_wait(*qg_move)
     spread(
@@ -1044,37 +1056,31 @@
         lambda i: dot(s.n1_t[part(i, fc_rows), :], s.qg_all[...].reshape(tokens, 3 * share)),
         s.qkv_own,
     )
-    sum_copy(0, 0, twin).wait()
-    s.sums[...] += s.sums_in[0]
-    for step in range(1, PLANE):
-        sum_copy(step, step, (layer * PLANE + (place + step) % PLANE, core)).start()
-
-    fx_move = (lambda g: s.fc_x.at[g], lambda g: s.fc_y.at[g], s.fx_sent, s.fx_got)
-    qx_move = (lambda g: s.qkv_x.at[g], lambda g: s.qkv_y.at[g], s.qx_sent, s.qx_got)
+    spread_on(sum_fc)
+    spread_on(sum_out)
+    settle(s.sums_in, s.low_got.at[0])
+    s.sums_all[member] = s.sums_out[layer] + s.sums_in[0] + s.sums_in[1] + s.sums_in[2]
+    for step in range(1, members):
+        low_copy(step).start()
+    spread_on(sum_qkv)
+    collect(sum_proj, gproj_ref)
     collect(sum_fc, s.fc_own)
     s.fc_x[...] = s.fc_own[...].astype(BF16).reshape(s.fc_x.shape)
     deal_start(*fx_move)
-    for step in range(1, PLANE):
-        sum_copy(step, step, twin).wait()
-    s.sums[...] += s.sums_in[1] + s.sums_in[2] + s.sums_in[3]
-    for step in range(1, layers):
-        peer = ((layer + step) % layers) * PLANE + place
-        sum_copy(3 + step, 3 + step, (peer, core)).start()
-    collect(sum_proj, gproj_ref)
     collect(sum_out, gout_ref)
-    spread_on(sum_qkv)
+    settle(s.sums_all.at[pl.ds(0, members - 1)], s.low_got.at[1])
+    total = s.sums_all[0]
+    for slot in range(1, members):
+        total = total + s.sums_all[slot]
+    s.sums[:, :lanes_of_layer] = total
     collect(sum_qkv, s.qkv_own)
     s.qkv_x[...] = s.qkv_own[...].astype(BF16).reshape(s.qkv_x.shape)
     deal_start(*qx_move)
-    for step in range(1, layers):
-        sum_copy(3 + step, 3 + step, twin).wait()
-    s.sums[...] += s.sums_in[4] + s.sums_in[5] + s.sums_in[6]
-    owner = me * 2 + core
     gvec_ref[...] = jnp.zeros_like(gvec_ref)
-    block = s.sums[0:8, part(owner // 4, 128)]
-    gvec_ref[0:8, :] = pltpu.roll(block, (128 - (owner % 4) * 32) % 128, 1)
-    block = s.sums[8:16, part(owner % 8, 128)]
-    chosen = lax.broadcasted_iota(jnp.int32, block.shape, 0) == owner // 8
+    block = s.sums[0:8, part(member // 4, 128)]
+    gvec_ref[0:8, :] = pltpu.roll(block, (128 - (member % 4) * 32) % 128, 1)
+    block = s.sums[8:16, part(member % 2, 128)]
+    chosen = lax.broadcasted_iota(jnp.int32, block.shape, 0) == member // 2
     gvec_ref[8:9, :] = jnp.sum(jnp.where(chosen, block, 0.0), 0, keepdims=True)
     deal_wait(*fx_move)
     for slot in range(members):
@@ -1091,15 +1097,15 @@
                 slot, :, third * 128 : third * 128 + 128
             ].astype(F32)
 
-    for step in range(4):
-        for third in range(3):
-            qkv_piece(step, third).wait_send()
+    settle(s.sums_in, s.low_sent.at[0])
+    settle(s.sums_all.at[pl.ds(0, members - 1)], s.low_sent.at[1])
+    settle(peer_rows(s.w_qkv, wq_hbm), s.w_sent.at[0])
     for index in range(3):
         big_piece(index).wait_send()
     vec_copy.wait_send()
-    for move in (o_move, g_move, back_move):
+    for move in (o_move, g_move, kv_back, q_back):
         swap_drain(*move)
-    for move in (att_move, hg_move, act_move, qg_move, fx_move, qx_move):
+    for move in (att_move, qg_move, fx_move, qx_move):
         deal_drain(*move)
     for where, sent, got in (
         (cot_at, s.cot_sent, s.cot_got),

time: 177 us -> 146 us (0.82)
  Pallas kernels: 173 us -> 143 us
    pallas_call x1, Pallas kernels: 170 us -> 140 us  [fused_layer(): pl.pallas_call(partial(layer_kernel, names), out_shape=(jax.ShapeDtypeStr...]
where the time goes in v4:
time: 146 us
  Pallas kernels  143 us (98%)
  other arithmetic  1.53 us (1%)
    pallas_call x1, Pallas kernels, fused_layer(): pl.pallas_call(partial(layer_kernel, names), out_shape=(jax.ShapeDtypeStr...  140 us
    pallas_call x1, Pallas kernels, fused_layer(): pl.pallas_call(hand_over, out_shape=tuple((jax.ShapeDtypeStruct(out.shape...  3.07 us

profile of v4, /device:TPU:0, one launch (start us, length us, event | category | flops | bytes accessed | tf_op | source)
XLA Modules:
  0.0 145.9 jit_solution(14176068784624351037)
XLA Ops:
  0.7 0.8 fusion
  1.5 1.5 %select_select_fusion.refs_2_ = bf16[16,512]{1,0:T(8,128)(2,1)} fusion(pred[16]{0:T(512)(128)(4,1)S(1)} %get-tuple-element.63, pred[16]{0:T(512)(128)(4,1)S(1)} %get-tuple-element.64, pred[16]{0:T(512)(128)(4,1)S(1)} %get-tuple-element.65, pred[16]{0:T(512)(128)(4,1)S(1)} %get-tuple-element.66, pred[16]{0:T(512)(128)(4,1)S(1)} %get-tuple-element.67, ...), kind=kLoop, calls=%fused_computation | loop fusion | flops 98304 | bytes 28864 | tf_op jit(solution)/shard_map/jit(_where)/select_n | solution.py:1156
  3.0 139.6 %shard_map.262 = (bf16[128,1024]{1,0:T(8,128)(2,1)}, f32[128,1024]{1,0:T(8,128)}, f32[32,3072]{1,0:T(8,128)}, f32[32,1024]{1,0:T(8,128)}, f32[32,4096]{1,0:T(8,1...) custom-call(bf16[128,1024]{1,0:T(8,128)(2,1)} %bitcast.14, bf16[128,1024]{1,0:T(8,128)(2,1)} %bitcast.15, ...), custom_call_target="tpu_custom_call" | custom-call | flops 14000000000 | bytes 30000000 | tf_op jit(solution)/shard_map/pallas_call | solution.py:1164
  142.6 3.1 %shard_map.263 = (bf16[128,1024]{1,0:T(8,128)(2,1)}, f32[128,1024]{1,0:T(8,128)}, f32[32,3072]{1,0:T(8,128)}, f32[32,1024]{1,0:T(8,128)}, f32[32,4096]{1,0:T(8,1...) custom-call(bf16[128,1024]{1,0:T(8,128)(2,1)} %get-tuple-element.37., ...), custom_call_target="tpu_custom_call" | custom-call | tf_op jit(solution)/shard_map/pallas_call | solution.py:1195
  (6 shorter events, 0.0 us)

commit v5 on v4

--- a/solution.py
+++ b/solution.py
@@ -367,8 +367,10 @@
         fc_t=((ff // members, width), BF16),
         bias_t=((ff // members, 128), F32),
         proj_own=((ff // members, width), BF16),
+        proj_in=((3 * (ff // members // layers), width), BF16),
         act_all=((ff // members, tokens), BF16),
         hg_all=((ff // members, tokens), BF16),
+        upstream=((members, rows, ff // members), F32),
         acc_o=((rows, width), F32),
         acc_d=((rows, width), F32),
         res_grad=((rows, width), F32),
@@ -381,10 +383,11 @@
         qg_all=((members, rows, 3 * share), BF16),
         fc_own=((width // layers, ff // members), F32),
         qkv_own=((width // layers, 3 * share), F32),
+        qkv_next=((width // layers, 3 * share), F32),
         fc_x=((members, width // layers // members, ff // members), BF16),
         fc_y=((members, width // layers // members, ff // members), BF16),
-        qkv_x=((members, width // layers // members, 3 * share), BF16),
-        qkv_y=((members, width // layers // members, 3 * share), BF16),
+        qkv_x=((2 * members, width // layers // members, 3 * share), BF16),
+        qkv_y=((2 * members, width // layers // members, 3 * share), BF16),
         sums=((16, width), F32),
         sums_out=((layers, 16, width // layers), F32),
         sums_in=((3, 16, width // layers), F32),
@@ -493,7 +496,7 @@
     for step in range(4):
         for third in range(3):
             qkv_piece(step, third).start()
-    big = ((wo_hbm, s.w_out), (wf_hbm, s.w_fc), (wp_hbm, s.w_proj))
+    big = ((wp_hbm, s.w_proj), (wo_hbm, s.w_out), (wf_hbm, s.w_fc))
 
     def big_piece(index):
         source, target = big[index]
@@ -508,17 +511,30 @@
     def gather_copy(where, sent, got, slot, index, device):
         return remote(where(slot), where(slot), sent.at[0], got.at[index], device)
 
+    near_x = place + 1 - 2 * (place % 2)
+    near_y = (place + 2) % PLANE
+    diagonal = (near_x + 2) % PLANE
+
     def gather_start(where, sent, got):
-        for step in range(1, PLANE):
-            peer = layer * PLANE + (place + step) % PLANE
-            gather_copy(where, sent, got, member, place, (peer, core)).start()
+        for peer in (near_x, near_y):
+            gather_copy(where, sent, got, member, place, (layer * PLANE + peer, core)).start()
         gather_copy(where, sent, got, member, PLANE, twin).start()
 
+    def gather_relay(where, sent, got):
+        for peer, onward, lower in ((near_x, near_y, 0), (near_y, near_x, 1)):
+            slot = peer * 2 + core
+            settle(where(slot), got.at[peer])
+            size = where(slot).shape[0] // 2
+            half_block = where(slot).at[pl.ds(lower * size, size)]
+            remote(
+                half_block, half_block, sent.at[0], got.at[peer], (layer * PLANE + onward, core)
+            ).start()
+            gather_copy(where, sent, got, slot, PLANE, twin).start()
+
     def gather_forward(where, sent, got):
-        for step in range(1, PLANE):
-            peer = (place + step) % PLANE
-            settle(where(peer * 2 + core), got.at[peer])
-            gather_copy(where, sent, got, peer * 2 + core, PLANE, twin).start()
+        slot = diagonal * 2 + core
+        settle(where(slot), got.at[diagonal])
+        gather_copy(where, sent, got, slot, PLANE, twin).start()
 
     def gather_finish(where, sent, got):
         settle(where(0, PLANE), got.at[PLANE])
@@ -612,7 +628,7 @@
     att_move = (lambda g: s.att_t.at[:, seven(g)], lambda g: s.att_all.at[:, :, lanes(g)], 0)
     qg_move = (lambda g: s.qg_out.at[seven(g)], lambda g: s.qg_all.at[whole(g)], 1)
     fx_move = (lambda g: s.fc_x.at[seven(g)], lambda g: s.fc_y.at[whole(g)], 2)
-    qx_move = (lambda g: s.qkv_x.at[seven(g)], lambda g: s.qkv_y.at[whole(g)], 3)
+    qx_move = (lambda g: s.qkv_x.at[g], lambda g: s.qkv_y.at[whole(g)], 3)
 
     def vec_row(index):
         return jnp.concatenate([s.vec[0, index : index + 1, :], s.vec[1, index : index + 1, :]], 1)
@@ -656,7 +672,17 @@
         big_piece(index).start()
         big_local(index).start()
 
+    settle(peer_rows(s.w_proj, wp_hbm), s.w_got.at[4])
+    big_local(0).wait()
+
+    def send_back(index, _):
+        s.upstream[index] = right_transposed(cot_ref[...], s.w_proj[part(index, chunk), :])
+        return 0
+
+    lax.fori_loop(0, members, send_back, 0)
+
     swap_wait(*qkv_move)
+    gather_relay(cot_at, s.cot_sent, s.cot_got)
     low_all = low_lanes(keys)
     query = s.qkv[0].astype(F32)
     s.q_low[0] = jnp.where(low_all, query, 0.0).astype(BF16)
@@ -738,7 +764,7 @@
     for index in range(n_tiles):
         attend(index)
 
-    for index in range(3):
+    for index in range(1, 3):
         settle(peer_rows(big[index][1], big[index][0]), s.w_got.at[4 + index])
         big_local(index).wait()
     quarters = ff // width
@@ -757,6 +783,7 @@
         bias = s.row[4 + quarter : 5 + quarter, part(member, piece)]
         s.bias_t[into, :] = jnp.broadcast_to(bias, (128, piece)).T
     swap_wait(*o_move)
+    gather_forward(cot_at, s.cot_sent, s.cot_got)
     for pair in range(HEADS // 2):
         columns = slice(pair * 128, pair * 128 + 128)
         s.att[:, columns] = unpack_pair(
@@ -791,27 +818,21 @@
         return hidden * rise, slope
 
     def feed(index, _):
-        places = features(index)
-        bias = jnp.concatenate(
-            [s.row[4 + quarter : 5 + quarter, part(index, piece)] for quarter in range(quarters)], 1
-        )
-        into = jnp.concatenate([s.w_fc[:, at] for at in places], 1)
-        back = jnp.concatenate([s.w_proj[at, :] for at in places], 0)
-        hidden = dot(s.n2[...], into) + bias
-        upstream = right_transposed(cot_ref[...], back)
-        active, slope = gelu_parts(hidden)
+        at = part(index, chunk)
+        bias = s.vec.at[index // 4][pl.ds(8 + index % 4, 1), :]
+        active, slope = gelu_parts(dot(s.n2[...], s.w_fc[:, at]) + bias)
         active = active.astype(BF16)
-        grad = (upstream * slope).astype(BF16)
-        s.acc_o[...] += dot(active, back)
-        s.acc_d[...] += right_transposed(grad, into)
-        total = jnp.sum(grad.astype(F32), 0, keepdims=True)
-        for quarter in range(quarters):
-            s.sums[8 + quarter : 9 + quarter, part(index, piece)] = total[
-                :, quarter * piece : quarter * piece + piece
-            ]
+        grad = (s.upstream[index] * slope).astype(BF16)
+        s.acc_o[...] += dot(active, s.w_proj[at, :])
+        s.acc_d[...] += right_transposed(grad, s.w_fc[:, at])
+        s.sums[pl.ds(8 + index // 2, 1), part(index % 2, chunk)] = jnp.sum(
+            grad.astype(F32), 0, keepdims=True
+        )
         return 0
 
-    lax.fori_loop(0, members, feed, 0)
+    lax.fori_loop(0, members - 3, feed, 0)
+    gather_relay(n2_at, s.n2_sent, s.n2_got)
+    lax.fori_loop(members - 3, members, feed, 0)
     upstream = cot_ref[...].astype(F32)
     normal, inverse = norm_parts(s.res[...])
     step_grad, gain_grad, shift_grad = norm_grads(s.acc_d[...], normal, inverse, vec_row(2))
@@ -835,7 +856,6 @@
     y_ref[...] = (s.res[...] + s.acc_o[...] + vec_row(7)).astype(BF16)
     gather_start(bg_at, s.bg_sent, s.bg_got)
     deal_start(*att_move)
-    gather_forward(cot_at, s.cot_sent, s.cot_got)
     gather_forward(n2_at, s.n2_sent, s.n2_got)
     swap_drain(*qkv_move)
 
@@ -889,7 +909,7 @@
     def rows_of(ref, start, size, columns=slice(None)):
         return lambda slot, count=1: ref.at[pl.ds(start + slot * size, count * size), columns]
 
-    sum_proj = (rows_of(s.w_proj, 0, proj_rows), rows_of(s.w_proj, 512, proj_rows), 0)
+    sum_proj = (rows_of(s.w_proj, 0, proj_rows), rows_of(s.proj_in, 0, proj_rows), 0)
     sum_out = (rows_of(s.w_proj, 1024, out_rows), rows_of(s.w_proj, 1152, out_rows), 1)
     sum_fc = (
         rows_of(s.w_fc, 0, fc_rows, pl.ds(0, chunk)),
@@ -902,25 +922,55 @@
         3,
     )
 
-    def feed_again(index, _):
-        at = part(index, 2 * rows)
-        hidden = dot(s.fc_t[...], s.n2_t[:, at]) + jnp.concatenate([s.bias_t[...]] * 2, 1)
-        cotangents = s.cot_all[pl.ds(2 * index, 2)].reshape(2 * rows, width)
+    part_rows = chunk // 2
+
+    def tokens_of(first, second):
+        return [part(first, rows), part(second, rows)]
+
+    def feed_again(first, second):
+        here = tokens_of(first, second)
+        normed = jnp.concatenate([s.n2_t[:, at] for at in here], 1)
+        hidden = dot(s.fc_t[...], normed) + jnp.concatenate([s.bias_t[...]] * 2, 1)
+        active, slope = gelu_parts(hidden)
+        active = active.astype(BF16)
+        for index, at in enumerate(here):
+            columns = slice(index * rows, (index + 1) * rows)
+            s.act_all[:, at] = active[:, columns]
+            s.scores[:, at] = slope[:part_rows, columns]
+            s.scores[:, part((first, second)[index] + members, rows)] = slope[part_rows:, columns]
+
+    def back_again(first, second):
+        cotangents = jnp.concatenate([s.cot_all[first], s.cot_all[second]], 0)
         upstream = right_transposed(s.proj_own[...], cotangents)
-        active, slope = gelu_parts(hidden)
-        s.act_all[:, at] = active.astype(BF16)
-        s.hg_all[:, at] = (upstream * slope).astype(BF16)
-        return 0
+        for index, slot in enumerate((first, second)):
+            at = part(slot, rows)
+            columns = slice(index * rows, (index + 1) * rows)
+            grad = upstream[:part_rows, columns] * s.scores[:, at]
+            s.hg_all[:part_rows, at] = grad.astype(BF16)
+            grad = upstream[part_rows:, columns] * s.scores[:, part(slot + members, rows)]
+            s.hg_all[part_rows:, at] = grad.astype(BF16)
 
     def grads_of_feed():
+        pairs = (
+            (member, near_x * 2 + core),
+            (near_y * 2 + core, diagonal * 2 + core),
+            (place * 2 + other, near_x * 2 + other),
+            (near_y * 2 + other, diagonal * 2 + other),
+        )
         gather_finish(cot_at, s.cot_sent, s.cot_got)
-        gather_finish(n2_at, s.n2_sent, s.n2_got)
-        lax.fori_loop(0, PLANE, feed_again, 0)
-        spread_prepare(
+        for index, pair in enumerate(pairs):
+            if index == 2:
+                gather_finish(n2_at, s.n2_sent, s.n2_got)
+            feed_again(*pair)
+        spread(
             sum_proj,
             lambda i: dot(s.act_all[part(i, proj_rows), :], s.cot_all[...].reshape(tokens, width)),
             gproj_ref,
         )
+        for pair in pairs:
+            back_again(*pair)
+
+    def grad_of_fc():
         spread_prepare(
             sum_fc,
             lambda i: right_transposed(s.n2_t[part(i, fc_rows), :], s.hg_all[...]),
@@ -981,10 +1031,12 @@
         for step in range(per_tile):
             swap_one(*kv_back, index * per_tile + order_in(step))
 
-    spread_start(sum_proj)
+    gather_relay(bg_at, s.bg_sent, s.bg_got)
     attend_back(0)
     attend_back(1)
+    grad_of_fc()
     attend_back(2)
+    gather_forward(bg_at, s.bg_sent, s.bg_got)
     attend_back(3)
     out = jnp.where(low_all, s.dq[0], swap(s.dq[1])) * scaling
     s.stage[:, 0] = out.astype(BF16).reshape(groups, half, 128)
@@ -993,11 +1045,11 @@
             swap_one(*q_back, order(step) * 4 + order_in(head))
     spread_start(sum_fc)
     gather_start(n1_at, s.n1_sent, s.n1_got)
-    gather_forward(bg_at, s.bg_sent, s.bg_got)
     grad_of_out()
     spread_on(sum_proj)
 
     swap_wait(*kv_back)
+    gather_relay(n1_at, s.n1_sent, s.n1_got)
     swap_wait(*q_back)
     for pair in range(HEADS // 2):
         for third in range(3):
@@ -1008,6 +1060,7 @@
             columns = slice(third * width + pair * 128, third * width + pair * 128 + 128)
             s.qg[:, columns] = block
     deal_start(*qg_move)
+    gather_forward(n1_at, s.n1_sent, s.n1_got)
     s.sums[4:5, :] = jnp.sum(s.qg[:, :width].astype(F32), 0, keepdims=True)
     s.sums[5:6, :] = jnp.sum(s.qg[:, 2 * width :].astype(F32), 0, keepdims=True)
 
@@ -1048,21 +1101,39 @@
             at_member((member + step) % members),
         )
 
-    gather_forward(n1_at, s.n1_sent, s.n1_got)
+    spread_on(sum_fc)
     gather_finish(n1_at, s.n1_sent, s.n1_got)
     deal_wait(*qg_move)
-    spread(
-        sum_qkv,
-        lambda i: dot(s.n1_t[part(i, fc_rows), :], s.qg_all[...].reshape(tokens, 3 * share)),
-        s.qkv_own,
-    )
-    spread_on(sum_fc)
+    def qkv_product(index):
+        return dot(
+            s.n1_t[part(index, fc_rows), :], s.qg_all[...].reshape(tokens, 3 * share)
+        )
+
+    for slot, index in enumerate((across, beside)):
+        sum_qkv[0](slot)[...] = qkv_product(index).astype(BF16)
+        spread_copy(sum_qkv, slot, beside).start()
+    s.qkv_next[...] = qkv_product(beyond)
+    s.qkv_own[...] = qkv_product(layer)
+
+    def pair_sum(move, slot, own, into):
+        settle(move[1](slot), s.sum_got.at[2 * move[2] + slot])
+        both = own[...] + move[1](slot)[...].astype(F32)
+        s.qkv_x[pl.ds(into, members)] = both.astype(BF16).reshape(members, -1, 3 * share)
+
     spread_on(sum_out)
+    pair_sum(sum_qkv, 0, s.qkv_next, members)
+    for index in range(members):
+        remote(
+            s.qkv_x.at[members + index],
+            s.qkv_y.at[members + member],
+            s.deal_sent.at[3],
+            s.deal_got.at[3],
+            (beyond * PLANE + index // 2, index % 2),
+        ).start()
     settle(s.sums_in, s.low_got.at[0])
     s.sums_all[member] = s.sums_out[layer] + s.sums_in[0] + s.sums_in[1] + s.sums_in[2]
     for step in range(1, members):
         low_copy(step).start()
-    spread_on(sum_qkv)
     collect(sum_proj, gproj_ref)
     collect(sum_fc, s.fc_own)
     s.fc_x[...] = s.fc_own[...].astype(BF16).reshape(s.fc_x.shape)
@@ -1073,8 +1144,7 @@
     for slot in range(1, members):
         total = total + s.sums_all[slot]
     s.sums[:, :lanes_of_layer] = total
-    collect(sum_qkv, s.qkv_own)
-    s.qkv_x[...] = s.qkv_own[...].astype(BF16).reshape(s.qkv_x.shape)
+    pair_sum(sum_qkv, 1, s.qkv_own, 0)
     deal_start(*qx_move)
     gvec_ref[...] = jnp.zeros_like(gvec_ref)
     block = s.sums[0:8, part(member // 4, 128)]
@@ -1093,9 +1163,10 @@
     for slot in range(members):
         for third in range(3):
             start = third * width + slot * 128
-            gqkv_ref[:, start : start + 128] = s.qkv_y[
-                slot, :, third * 128 : third * 128 + 128
-            ].astype(F32)
+            columns = slice(third * 128, third * 128 + 128)
+            gqkv_ref[:, start : start + 128] = s.qkv_y[slot, :, columns].astype(
+                F32
+            ) + s.qkv_y[members + slot, :, columns].astype(F32)
 
     settle(s.sums_in, s.low_sent.at[0])
     settle(s.sums_all.at[pl.ds(0, members - 1)], s.low_sent.at[1])
@@ -1105,8 +1176,9 @@
     vec_copy.wait_send()
     for move in (o_move, g_move, kv_back, q_back):
         swap_drain(*move)
-    for move in (att_move, qg_move, fx_move, qx_move):
+    for move in (att_move, qg_move, fx_move):
         deal_drain(*move)
+    settle(s.qkv_x.at[pl.ds(0, 2 * members - 1)], s.deal_sent.at[3])
     for where, sent, got in (
         (cot_at, s.cot_sent, s.cot_got),
         (n1_at, s.n1_sent, s.n1_got),
@@ -1114,8 +1186,9 @@
         (bg_at, s.bg_sent, s.bg_got),
     ):
         gather_drain(where, sent, got)
-    for move in (sum_proj, sum_fc, sum_out, sum_qkv):
+    for move in (sum_proj, sum_fc, sum_out):
         spread_drain(move)
+    settle(sum_qkv[0](0, 2), s.sum_sent.at[3])
 
 
 def hand_over(*refs):

time: 146 us -> 139 us (0.952)
  the two profiles are of different devices: /device:TPU:0 before, /device:TPU:25 now
where the time goes in v5:
time: 139 us
  Pallas kernels  136 us (98%)
  other arithmetic  1.53 us (1%)
    pallas_call x1, Pallas kernels, fused_layer(): pl.pallas_call(partial(layer_kernel, names), out_shape=(jax.ShapeDtypeStr...  133 us
    pallas_call x1, Pallas kernels, fused_layer(): pl.pallas_call(hand_over, out_shape=tuple((jax.ShapeDtypeStruct(out.shape...  3.07 us

profile of v5, /device:TPU:25, one launch (start us, length us, event | category | flops | bytes accessed | tf_op | source)
XLA Modules:
  0.0 138.9 jit_solution(14570877888533763158)
XLA Ops:
  0.7 0.8 fusion
  1.5 1.5 %select_select_fusion.refs_2_ = bf16[16,512]{1,0:T(8,128)(2,1)} fusion(pred[16]{0:T(512)(128)(4,1)S(1)} %get-tuple-element.63, pred[16]{0:T(512)(128)(4,1)S(1)} %get-tuple-element.64, pred[16]{0:T(512)(128)(4,1)S(1)} %get-tuple-element.65, pred[16]{0:T(512)(128)(4,1)S(1)} %get-tuple-element.66, pred[16]{0:T(512)(128)(4,1)S(1)} %get-tuple-element.67, ...), kind=kLoop, calls=%fused_computation | loop fusion | flops 98304 | bytes 28864 | tf_op jit(solution)/shard_map/jit(_where)/select_n | solution.py:1229
  3.0 132.7 %shard_map.262 = (bf16[128,1024]{1,0:T(8,128)(2,1)}, f32[128,1024]{1,0:T(8,128)}, f32[32,3072]{1,0:T(8,128)}, f32[32,1024]{1,0:T(8,128)}, f32[32,4096]{1,0:T(8,1...) custom-call(bf16[128,1024]{1,0:T(8,128)(2,1)} %bitcast.14, bf16[128,1024]{1,0:T(8,128)(2,1)} %bitcast.15, ...), custom_call_target="tpu_custom_call" | custom-call | flops 14000000000 | bytes 30000000 | tf_op jit(solution)/shard_map/pallas_call | solution.py:1237
  135.7 3.1 %shard_map.263 = (bf16[128,1024]{1,0:T(8,128)(2,1)}, f32[128,1024]{1,0:T(8,128)}, f32[32,3072]{1,0:T(8,128)}, f32[32,1024]{1,0:T(8,128)}, f32[32,4096]{1,0:T(8,1...) custom-call(bf16[128,1024]{1,0:T(8,128)(2,1)} %get-tuple-element.37., ...), custom_call_target="tpu_custom_call" | custom-call | tf_op jit(solution)/shard_map/pallas_call | solution.py:1268
  (6 shorter events, 0.0 us)

commit v6 on v5

--- a/solution.py
+++ b/solution.py
@@ -281,6 +281,7 @@
 
 
 MESH = pl.DeviceIdType.MESH
+HAND_STEPS = 2
 BF16, F32 = jnp.bfloat16, jnp.float32
 PLANE = 4
 NEG = -1e30
@@ -339,7 +340,6 @@
         w_out=((width, width), BF16),
         w_fc=((width, ff), BF16),
         w_proj=((ff, width), BF16),
-        vec_low=((2, 16, width // 2), BF16),
         vec=((2, 16, width // 2), F32),
         row=((8, width), F32),
         cot_all=((members, rows, width), BF16),
@@ -381,13 +381,16 @@
         qg=((rows, 3 * width), BF16),
         qg_out=((members, rows, 3 * share), BF16),
         qg_all=((members, rows, 3 * share), BF16),
-        fc_own=((width // layers, ff // members), F32),
-        qkv_own=((width // layers, 3 * share), F32),
-        qkv_next=((width // layers, 3 * share), F32),
         fc_x=((members, width // layers // members, ff // members), BF16),
         fc_y=((members, width // layers // members, ff // members), BF16),
         qkv_x=((2 * members, width // layers // members, 3 * share), BF16),
         qkv_y=((2 * members, width // layers // members, 3 * share), BF16),
+        out_y=((rows, width), BF16),
+        out_gx=((rows, width), F32),
+        out_gqkv=((width // members // layers, 3 * width), F32),
+        out_gout=((width // members // layers, width), F32),
+        out_gfc=((width // members // layers, ff), F32),
+        out_gproj=((ff // members // layers, width), F32),
         sums=((16, width), F32),
         sums_out=((layers, 16, width // layers), F32),
         sums_in=((3, 16, width // layers), F32),
@@ -397,6 +400,7 @@
 
 SEMAPHORES = dict(
     local=4,
+    out_sem=6,
     w_sent=4,
     w_got=7,
     vec_sent=1,
@@ -425,9 +429,16 @@
 
 
 def layer_kernel(names, *refs):
-    x_ref, cot_ref, vec_ref, wq_hbm, wo_hbm, wf_hbm, wp_hbm = refs[:7]
-    y_ref, gx_ref, gqkv_ref, gout_ref, gfc_ref, gproj_ref, gvec_ref = refs[7:14]
-    s = SimpleNamespace(**dict(zip(names, refs[14:])))
+    x_ref, cot_ref, wq_hbm, wo_hbm, wf_hbm, wp_hbm = refs[:6]
+    small = refs[6:15]
+    finals, gvec_ref = refs[15:21], refs[21]
+    s = SimpleNamespace(**dict(zip(names, refs[22:])))
+    held = (s.out_y, s.out_gx, s.out_gqkv, s.out_gout, s.out_gfc, s.out_gproj)
+    y_ref, gx_ref, gqkv_ref, gout_ref, gfc_ref, gproj_ref = held
+
+    def hand_out(index):
+        return pltpu.make_async_copy(held[index], finals[index], s.out_sem.at[index])
+
     rows, width = x_ref.shape
     ff = s.w_fc.shape[1]
     half = rows // 2
@@ -491,7 +502,14 @@
             twin,
         )
 
-    vec_copy = remote(vec_ref, s.vec_low.at[core], s.vec_sent.at[0], s.vec_got.at[0], twin)
+    at = 0
+    for vector in small:
+        for start in range(0, vector.shape[0], width // 2):
+            line = vector[start : start + width // 2].astype(F32)
+            s.vec[core, at : at + 1, :] = line.reshape(1, width // 2)
+            at += 1
+    s.vec[core, at:, :] = jnp.zeros((16 - at, width // 2), F32)
+    vec_copy = remote(s.vec.at[core], s.vec.at[core], s.vec_sent.at[0], s.vec_got.at[0], twin)
     vec_copy.start()
     for step in range(4):
         for third in range(3):
@@ -634,9 +652,9 @@
         return jnp.concatenate([s.vec[0, index : index + 1, :], s.vec[1, index : index + 1, :]], 1)
 
     s.cot_all[member] = cot_ref[...]
-    settle(vec_ref, s.vec_got.at[0])
-    s.vec[core] = vec_ref[...].astype(F32)
-    s.vec[other] = s.vec_low[other].astype(F32)
+    inputs = x_ref[...].astype(F32)
+    normal, _ = norm_parts(inputs)
+    settle(s.vec.at[other], s.vec_got.at[0])
     s.row[0:1, :] = vec_row(4)
     s.row[1:2, :] = vec_row(5)
     for quarter in range(4):
@@ -644,8 +662,6 @@
         s.row[4 + quarter : 5 + quarter, :] = jnp.concatenate(
             [s.vec[quarter // 2, at : at + 1, :], s.vec[quarter // 2, at + 1 : at + 2, :]], 1
         )
-    inputs = x_ref[...].astype(F32)
-    normal, _ = norm_parts(inputs)
     normed = (normal * vec_row(0) + vec_row(1)).astype(BF16)
     s.n1[...] = normed
     s.n1_t[:, part(member, rows)] = normed.astype(F32).T.astype(BF16)
@@ -818,21 +834,24 @@
         return hidden * rise, slope
 
     def feed(index, _):
-        at = part(index, chunk)
-        bias = s.vec.at[index // 4][pl.ds(8 + index % 4, 1), :]
+        at = part(index, 2 * chunk)
+        lines = s.vec.at[index // 2]
+        first = 8 + index % 2 * 2
+        bias = jnp.concatenate(
+            [lines[pl.ds(first, 1), :], lines[pl.ds(first + 1, 1), :]], 1
+        )
         active, slope = gelu_parts(dot(s.n2[...], s.w_fc[:, at]) + bias)
         active = active.astype(BF16)
-        grad = (s.upstream[index] * slope).astype(BF16)
+        upstream = jnp.concatenate([s.upstream[2 * index], s.upstream[2 * index + 1]], 1)
+        grad = (upstream * slope).astype(BF16)
         s.acc_o[...] += dot(active, s.w_proj[at, :])
         s.acc_d[...] += right_transposed(grad, s.w_fc[:, at])
-        s.sums[pl.ds(8 + index // 2, 1), part(index % 2, chunk)] = jnp.sum(
-            grad.astype(F32), 0, keepdims=True
-        )
+        s.sums[pl.ds(8 + index, 1), :] = jnp.sum(grad.astype(F32), 0, keepdims=True)
         return 0
 
-    lax.fori_loop(0, members - 3, feed, 0)
+    lax.fori_loop(0, PLANE - 1, feed, 0)
     gather_relay(n2_at, s.n2_sent, s.n2_got)
-    lax.fori_loop(members - 3, members, feed, 0)
+    lax.fori_loop(PLANE - 1, PLANE, feed, 0)
     upstream = cot_ref[...].astype(F32)
     normal, inverse = norm_parts(s.res[...])
     step_grad, gain_grad, shift_grad = norm_grads(s.acc_d[...], normal, inverse, vec_row(2))
@@ -854,6 +873,7 @@
         for head in range(4):
             swap_one(*g_move, four * 4 + order_in(head))
     y_ref[...] = (s.res[...] + s.acc_o[...] + vec_row(7)).astype(BF16)
+    hand_out(0).start()
     gather_start(bg_at, s.bg_sent, s.bg_got)
     deal_start(*att_move)
     gather_forward(n2_at, s.n2_sent, s.n2_got)
@@ -909,6 +929,10 @@
     def rows_of(ref, start, size, columns=slice(None)):
         return lambda slot, count=1: ref.at[pl.ds(start + slot * size, count * size), columns]
 
+    spare = s.upstream.reshape(tokens, chunk)
+    fc_own = spare.at[pl.ds(0, fc_rows), :]
+    qkv_own = spare.at[pl.ds(fc_rows, fc_rows), pl.ds(0, 3 * share)]
+    qkv_next = spare.at[pl.ds(2 * fc_rows, fc_rows), pl.ds(0, 3 * share)]
     sum_proj = (rows_of(s.w_proj, 0, proj_rows), rows_of(s.proj_in, 0, proj_rows), 0)
     sum_out = (rows_of(s.w_proj, 1024, out_rows), rows_of(s.w_proj, 1152, out_rows), 1)
     sum_fc = (
@@ -974,7 +998,7 @@
         spread_prepare(
             sum_fc,
             lambda i: right_transposed(s.n2_t[part(i, fc_rows), :], s.hg_all[...]),
-            s.fc_own,
+            fc_own,
         )
 
     def grad_of_out():
@@ -1074,6 +1098,7 @@
     s.sums[0:1, :] = gain_grad[None]
     s.sums[1:2, :] = shift_grad[None]
     gx_ref[...] = s.res_grad[...] + step_grad
+    hand_out(1).start()
 
     lanes_of_layer = width // layers
     for index in range(layers):
@@ -1112,8 +1137,8 @@
     for slot, index in enumerate((across, beside)):
         sum_qkv[0](slot)[...] = qkv_product(index).astype(BF16)
         spread_copy(sum_qkv, slot, beside).start()
-    s.qkv_next[...] = qkv_product(beyond)
-    s.qkv_own[...] = qkv_product(layer)
+    qkv_next[...] = qkv_product(beyond)
+    qkv_own[...] = qkv_product(layer)
 
     def pair_sum(move, slot, own, into):
         settle(move[1](slot), s.sum_got.at[2 * move[2] + slot])
@@ -1121,7 +1146,7 @@
         s.qkv_x[pl.ds(into, members)] = both.astype(BF16).reshape(members, -1, 3 * share)
 
     spread_on(sum_out)
-    pair_sum(sum_qkv, 0, s.qkv_next, members)
+    pair_sum(sum_qkv, 0, qkv_next, members)
     for index in range(members):
         remote(
             s.qkv_x.at[members + index],
@@ -1135,16 +1160,18 @@
     for step in range(1, members):
         low_copy(step).start()
     collect(sum_proj, gproj_ref)
-    collect(sum_fc, s.fc_own)
-    s.fc_x[...] = s.fc_own[...].astype(BF16).reshape(s.fc_x.shape)
+    hand_out(5).start()
+    collect(sum_fc, fc_own)
+    s.fc_x[...] = fc_own[...].astype(BF16).reshape(s.fc_x.shape)
     deal_start(*fx_move)
     collect(sum_out, gout_ref)
+    hand_out(3).start()
     settle(s.sums_all.at[pl.ds(0, members - 1)], s.low_got.at[1])
     total = s.sums_all[0]
     for slot in range(1, members):
         total = total + s.sums_all[slot]
     s.sums[:, :lanes_of_layer] = total
-    pair_sum(sum_qkv, 1, s.qkv_own, 0)
+    pair_sum(sum_qkv, 1, qkv_own, 0)
     deal_start(*qx_move)
     gvec_ref[...] = jnp.zeros_like(gvec_ref)
     block = s.sums[0:8, part(member // 4, 128)]
@@ -1159,6 +1186,7 @@
             gfc_ref[:, start : start + piece] = s.fc_y[
                 slot, :, quarter * piece : quarter * piece + piece
             ].astype(F32)
+    hand_out(4).start()
     deal_wait(*qx_move)
     for slot in range(members):
         for third in range(3):
@@ -1168,6 +1196,7 @@
                 F32
             ) + s.qkv_y[members + slot, :, columns].astype(F32)
 
+    hand_out(2).start()
     settle(s.sums_in, s.low_sent.at[0])
     settle(s.sums_all.at[pl.ds(0, members - 1)], s.low_sent.at[1])
     settle(peer_rows(s.w_qkv, wq_hbm), s.w_sent.at[0])
@@ -1189,6 +1218,8 @@
     for move in (sum_proj, sum_fc, sum_out):
         spread_drain(move)
     settle(sum_qkv[0](0, 2), s.sum_sent.at[3])
+    for index in range(6):
+        hand_out(index).wait()
 
 
 def hand_over(*refs):
@@ -1221,13 +1252,6 @@
     groups = lax.axis_size("ctx")
     shards = 2 * groups
     small = (ln1_gain, ln1_bias, ln2_gain, ln2_bias, bias_q, bias_v, bias_out, bias_proj, bias_fc)
-    line = lax.broadcasted_iota(jnp.int32, (16, width // 2), 0)
-    vectors, at = jnp.zeros(line.shape, BF16), 0
-    for vector in small:
-        for start in range(0, vector.shape[0], width // 2):
-            piece = lax.broadcast_in_dim(vector[start : start + width // 2], line.shape, (1,))
-            vectors = jnp.where(line == at, piece, vectors)
-            at += 1
     shapes = layer_shapes(rows, width, ff, groups)
     names = tuple(shapes) + tuple(SEMAPHORES)
     scratch = [pltpu.VMEM(shape, kind) for shape, kind in shapes.values()]
@@ -1245,8 +1269,8 @@
             jax.ShapeDtypeStruct((ff // shards, width), F32),
             jax.ShapeDtypeStruct((16, 128), F32),
         ),
-        in_specs=[in_vmem] * 3 + [in_hbm] * 4,
-        out_specs=(in_vmem,) * 7,
+        in_specs=[in_vmem] * 2 + [in_hbm] * 4 + [in_vmem] * 9,
+        out_specs=(in_hbm,) * 6 + (in_vmem,),
         scratch_shapes=scratch,
         compiler_params=pltpu.CompilerParams(
             collective_id=0, has_side_effects=True, vmem_limit_bytes=VMEM_BYTES
@@ -1257,21 +1281,26 @@
     )(
         block_input.reshape(rows, width),
         cotangent.reshape(rows, width),
-        vectors,
         w_qkv,
         w_out,
         w_fc,
         w_proj,
+        *small,
     )
     piece = width // shards
     wide = ff // shards
+
+    def block_of(array):
+        return pl.BlockSpec((array.shape[0] // HAND_STEPS, array.shape[1]), lambda i: (i, 0))
+
     results = pl.pallas_call(
         hand_over,
         out_shape=tuple(jax.ShapeDtypeStruct(out.shape, out.dtype) for out in outs[:6])
         + (jax.ShapeDtypeStruct((1, piece), F32),) * 8
         + (jax.ShapeDtypeStruct((1, wide), F32),),
-        in_specs=[in_vmem] * 7,
-        out_specs=(in_vmem,) * 15,
+        grid=(HAND_STEPS,),
+        in_specs=[block_of(out) for out in outs[:6]] + [in_vmem],
+        out_specs=tuple(block_of(out) for out in outs[:6]) + (in_vmem,) * 9,
     )(*outs)
     block_output, input_grad, grad_qkv, grad_out, grad_fc, grad_proj = results[:6]
     lows = [result.reshape(-1) for result in results[6:]]

time: 139 us -> 135 us (0.971)
  Pallas kernels: 136 us -> 134 us
  other arithmetic: 1.53 us -> 0 us
    pallas_call x1, Pallas kernels: 133 us -> 131 us  [fused_layer(): pl.pallas_call(partial(layer_kernel, names), out_shape=(jax.ShapeDtypeStr...]
    select_n x1 -> x0, other arithmetic: 1.5 us -> none  [fused_layer(): vectors = jnp.where(line == at, piece, vectors)]
where the time goes in v6:
time: 135 us
  Pallas kernels  134 us (99%)
    pallas_call x1, Pallas kernels, fused_layer(): pl.pallas_call(partial(layer_kernel, names), out_shape=(jax.ShapeDtypeStr...  131 us
    pallas_call x1, Pallas kernels, fused_layer(): pl.pallas_call(hand_over, out_shape=tuple((jax.ShapeDtypeStruct(out.shape...  2.84 us

profile of v6, /device:TPU:25, one launch (start us, length us, event | category | flops | bytes accessed | tf_op | source)
XLA Modules:
  0.0 134.8 jit_solution(15845342303419537751)
XLA Ops:
  0.7 131.1 %shard_map.262 = (bf16[128,1024]{1,0:T(8,128)(2,1)}, f32[128,1024]{1,0:T(8,128)}, f32[32,3072]{1,0:T(8,128)}, f32[32,1024]{1,0:T(8,128)}, f32[32,4096]{1,0:T(8,1...) custom-call(bf16[128,1024]{1,0:T(8,128)(2,1)} %bitcast.14, bf16[128,1024]{1,0:T(8,128)(2,1)} %bitcast.15, ...), custom_call_target="tpu_custom_call" | custom-call | flops 14000000000 | bytes 30000000 | tf_op jit(solution)/shard_map/pallas_call | solution.py:1261
  131.8 2.8 %shard_map.263 = (bf16[128,1024]{1,0:T(8,128)(2,1)}, f32[128,1024]{1,0:T(8,128)}, f32[32,3072]{1,0:T(8,128)}, f32[32,1024]{1,0:T(8,128)}, f32[32,4096]{1,0:T(8,1...) custom-call(bf16[128,1024]{1,0:T(8,128)(2,1)} %get-tuple-element.37., ...), custom_call_target="tpu_custom_call" | custom-call | tf_op jit(solution)/shard_map/pallas_call | solution.py:1296

commit v7 on v6

--- a/solution.py
+++ b/solution.py
@@ -664,7 +664,6 @@
         )
     normed = (normal * vec_row(0) + vec_row(1)).astype(BF16)
     s.n1[...] = normed
-    s.n1_t[:, part(member, rows)] = normed.astype(F32).T.astype(BF16)
     pltpu.make_async_copy(wq_hbm, top_rows(s.w_qkv, wq_hbm), s.local.at[0]).wait()
 
     for step in range(4):
@@ -688,6 +687,7 @@
         big_piece(index).start()
         big_local(index).start()
 
+    s.n1_t[:, part(member, rows)] = s.n1[...].astype(F32).T.astype(BF16)
     settle(peer_rows(s.w_proj, wp_hbm), s.w_got.at[4])
     big_local(0).wait()
 
@@ -703,7 +703,6 @@
     query = s.qkv[0].astype(F32)
     s.q_low[0] = jnp.where(low_all, query, 0.0).astype(BF16)
     s.q_low[1] = jnp.where(low_all, swap(query), 0.0).astype(BF16)
-    s.q_t[...] = query.T.astype(BF16)
     s.kv_roll[0] = swap(s.qkv[1].astype(F32)).astype(BF16)
     s.kv_roll[1] = swap(s.qkv[2].astype(F32)).astype(BF16)
 
@@ -777,8 +776,9 @@
         for step in range(per_tile):
             swap_one(*o_move, index * per_tile + order_in(step))
 
-    for index in range(n_tiles):
+    for index in (0, 3, 1, 2):
         attend(index)
+    s.q_t[...] = s.qkv[0].astype(F32).T.astype(BF16)
 
     for index in range(1, 3):
         settle(peer_rows(big[index][1], big[index][0]), s.w_got.at[4 + index])
@@ -805,8 +805,6 @@
         s.att[:, columns] = unpack_pair(
             s.o_in[2 * pair].astype(F32), s.o_in[2 * pair + 1].astype(F32)
         ).astype(BF16)
-    turned = s.att[...].astype(F32).T.astype(BF16)
-    s.att_t[...] = turned.reshape(s.att_t.shape)
     def project(index, _):
         at = part(index, 256)
         s.acc_d[:, at] = dot(s.att[...], s.w_out[:, at])
@@ -875,6 +873,7 @@
     y_ref[...] = (s.res[...] + s.acc_o[...] + vec_row(7)).astype(BF16)
     hand_out(0).start()
     gather_start(bg_at, s.bg_sent, s.bg_got)
+    s.att_t[...] = s.att[...].astype(F32).T.astype(BF16).reshape(s.att_t.shape)
     deal_start(*att_move)
     gather_forward(n2_at, s.n2_sent, s.n2_got)
     swap_drain(*qkv_move)
@@ -1057,11 +1056,11 @@
 
     gather_relay(bg_at, s.bg_sent, s.bg_got)
     attend_back(0)
-    attend_back(1)
+    attend_back(3)
     grad_of_fc()
     attend_back(2)
     gather_forward(bg_at, s.bg_sent, s.bg_got)
-    attend_back(3)
+    attend_back(1)
     out = jnp.where(low_all, s.dq[0], swap(s.dq[1])) * scaling
     s.stage[:, 0] = out.astype(BF16).reshape(groups, half, 128)
     for step in range(4):

time: 135 us -> 131 us (0.970)
  the two profiles are of different devices: /device:TPU:25 before, /device:TPU:0 now
where the time goes in v7:
time: 131 us; the launch traced here: 130 us
  Pallas kernels  130 us (99%)
    pallas_call x1, Pallas kernels, fused_layer(): pl.pallas_call(partial(layer_kernel, names), out_shape=(jax.ShapeDtypeStr...  127 us
    pallas_call x1, Pallas kernels, fused_layer(): pl.pallas_call(hand_over, out_shape=tuple((jax.ShapeDtypeStruct(out.shape...  2.84 us

profile of v7, /device:TPU:0, one launch (start us, length us, event | category | flops | bytes accessed | tf_op | source)
XLA Modules:
  0.0 130.4 jit_solution(17198272402967187992)
XLA Ops:
  0.7 126.8 %shard_map.262 = (bf16[128,1024]{1,0:T(8,128)(2,1)}, f32[128,1024]{1,0:T(8,128)}, f32[32,3072]{1,0:T(8,128)}, f32[32,1024]{1,0:T(8,128)}, f32[32,4096]{1,0:T(8,1...) custom-call(bf16[128,1024]{1,0:T(8,128)(2,1)} %bitcast.14, bf16[128,1024]{1,0:T(8,128)(2,1)} %bitcast.15, ...), custom_call_target="tpu_custom_call" | custom-call | flops 14000000000 | bytes 30000000 | tf_op jit(solution)/shard_map/pallas_call | solution.py:1260
  127.4 2.8 %shard_map.263 = (bf16[128,1024]{1,0:T(8,128)(2,1)}, f32[128,1024]{1,0:T(8,128)}, f32[32,3072]{1,0:T(8,128)}, f32[32,1024]{1,0:T(8,128)}, f32[32,4096]{1,0:T(8,1...) custom-call(bf16[128,1024]{1,0:T(8,128)(2,1)} %get-tuple-element.37., ...), custom_call_target="tpu_custom_call" | custom-call | tf_op jit(solution)/shard_map/pallas_call | solution.py:1295

commit v8 on v7

--- a/solution.py
+++ b/solution.py
@@ -776,7 +776,7 @@
         for step in range(per_tile):
             swap_one(*o_move, index * per_tile + order_in(step))
 
-    for index in (0, 3, 1, 2):
+    for index in (0, 3, 2, 1):
         attend(index)
     s.q_t[...] = s.qkv[0].astype(F32).T.astype(BF16)
 

time: 131 us -> 132 us (level)
  no operation moved by 1% of the time
where the time goes in v8:
time: 132 us
  Pallas kernels  131 us (99%)
    pallas_call x1, Pallas kernels, fused_layer(): pl.pallas_call(partial(layer_kernel, names), out_shape=(jax.ShapeDtypeStr...  128 us
    pallas_call x1, Pallas kernels, fused_layer(): pl.pallas_call(hand_over, out_shape=tuple((jax.ShapeDtypeStruct(out.shape...  2.84 us

profile of v8, /device:TPU:0, one launch (start us, length us, event | category | flops | bytes accessed | tf_op | source)
XLA Modules:
  0.0 131.6 jit_solution(15505685866382118097)
XLA Ops:
  0.7 128.0 %shard_map.262 = (bf16[128,1024]{1,0:T(8,128)(2,1)}, f32[128,1024]{1,0:T(8,128)}, f32[32,3072]{1,0:T(8,128)}, f32[32,1024]{1,0:T(8,128)}, f32[32,4096]{1,0:T(8,1...) custom-call(bf16[128,1024]{1,0:T(8,128)(2,1)} %bitcast.14, bf16[128,1024]{1,0:T(8,128)(2,1)} %bitcast.15, ...), custom_call_target="tpu_custom_call" | custom-call | flops 14000000000 | bytes 30000000 | tf_op jit(solution)/shard_map/pallas_call | solution.py:1260
  128.6 2.8 %shard_map.263 = (bf16[128,1024]{1,0:T(8,128)(2,1)}, f32[128,1024]{1,0:T(8,128)}, f32[32,3072]{1,0:T(8,128)}, f32[32,1024]{1,0:T(8,128)}, f32[32,4096]{1,0:T(8,1...) custom-call(bf16[128,1024]{1,0:T(8,128)(2,1)} %get-tuple-element.37., ...), custom_call_target="tpu_custom_call" | custom-call | tf_op jit(solution)/shard_map/pallas_call | solution.py:1295
